TPU v7x, 32 devices: a whole 2x2x4 slice. The times are simulated.
32 devices in a mesh: dp: 2 (over x), expert: 4 (over y, core), tensor: 4 (over z).
Axes of the slice: x: 2, y: 2, z: 4, core: 2. Of those that a mesh axis runs over, the one named last changes fastest.
Arguments:
- layer_input: bfloat16 [2, 2048, 2048], P('dp', 'expert'), may hold values from -6 to 6
- attention_gain: bfloat16 [2048], replicated, may hold values from 0.25 to 1.75
- query_weight: bfloat16 [2048, 2048], P(('dp', 'expert'), 'tensor'), may hold values from -0.125 to 0.125
- key_weight: bfloat16 [2048, 2048], P(('dp', 'expert'), 'tensor'), may hold values from -0.125 to 0.125
- value_weight: bfloat16 [2048, 2048], P(('dp', 'expert'), 'tensor'), may hold values from -0.125 to 0.125
- query_bias: bfloat16 [2048], P('tensor'), may hold values from -0.59765625 to 0.59765625
- key_bias: bfloat16 [2048], P('tensor'), may hold values from -0.59765625 to 0.59765625
- value_bias: bfloat16 [2048], P('tensor'), may hold values from -0.59765625 to 0.59765625
- output_weight: bfloat16 [2048, 2048], P(('dp', 'expert'), 'tensor'), may hold values from -1 to 1
- mixture_gain: bfloat16 [2048], replicated, may hold values from 0.25 to 1.75
- router_weight: bfloat16 [2048, 8], replicated, may hold values from -0.0625 to 0.0625
- expert_gate: bfloat16 [8, 2048, 1408], P('expert', None, 'tensor'), may hold values from -0.125 to 0.125
- expert_up: bfloat16 [8, 2048, 1408], P('expert', None, 'tensor'), may hold values from -0.125 to 0.125
- expert_down: bfloat16 [8, 2048, 1408], P('expert', None, 'tensor'), may hold values from -1 to 1
- shared_gate: bfloat16 [2048, 5632], P(('dp', 'expert'), 'tensor'), may hold values from -0.125 to 0.125
- shared_up: bfloat16 [2048, 5632], P(('dp', 'expert'), 'tensor'), may hold values from -0.125 to 0.125
- shared_down: bfloat16 [2048, 5632], P(('dp', 'expert'), 'tensor'), may hold values from -0.21875 to 0.21875
- shared_switch: bfloat16 [2048], replicated, may hold values from -0.125 to 0.125
- slot_lengths: int32 [2], P('dp'), may hold values from 512 to 2048, as said below
- routes: int32 [2, 2048, 4], P('dp', 'expert'), may hold values from 0 to 7, all different within a row
- cotangent: bfloat16 [2, 2048, 2048], P('dp', 'expert'), may hold values from -6 to 6
Outputs:
- layer_output: bfloat16 [2, 2048, 2048], P('dp', 'expert')
- input_grad: float32 [2, 2048, 2048], P('dp', 'expert')
- attention_gain_grad: float32 [2048], replicated
- query_weight_grad: float32 [2048, 2048], P(('dp', 'expert'), 'tensor')
- key_weight_grad: float32 [2048, 2048], P(('dp', 'expert'), 'tensor')
- value_weight_grad: float32 [2048, 2048], P(('dp', 'expert'), 'tensor')
- query_bias_grad: float32 [2048], P('tensor')
- key_bias_grad: float32 [2048], P('tensor')
- value_bias_grad: float32 [2048], P('tensor')
- output_weight_grad: float32 [2048, 2048], P(('dp', 'expert'), 'tensor')
- mixture_gain_grad: float32 [2048], replicated
- router_weight_grad: float32 [2048, 8], replicated
- expert_gate_grad: float32 [8, 2048, 1408], P('expert', None, 'tensor')
- expert_up_grad: float32 [8, 2048, 1408], P('expert', None, 'tensor')
- expert_down_grad: float32 [8, 2048, 1408], P('expert', None, 'tensor')
- shared_gate_grad: float32 [2048, 5632], P(('dp', 'expert'), 'tensor')
- shared_up_grad: float32 [2048, 5632], P(('dp', 'expert'), 'tensor')
- shared_down_grad: float32 [2048, 5632], P(('dp', 'expert'), 'tensor')
- shared_switch_grad: float32 [2048], replicated
Inputs may be any that keep to these rules, and one draw needn't show every extreme that they name: `slot_lengths`: one slot has exactly 2048 valid tokens.
All inputs are finite; a program needn't handle non-finite values.
Results may differ from a plain program's by a relative error of at most 0.02.
Values may be sent and summed in bfloat16 or wider, within the bound.
No kernel may reach another device: no remote copies, remote signals or barrier semaphores. Data moves between devices by JAX's collectives and lax.ppermute only.
A program may use at most 320 MiB of HBM per device.

v0:
```python
import jax
import jax.numpy as jnp
from jax import lax
from jax.sharding import PartitionSpec as P

HD = 128
TOP = 4


EPS = 1e-06
ROPE_BASE = 1000000.0
NEGATIVE = -1e30


def rotary_tables(positions, head_size):
    half_size = head_size // 2
    exponent = 2.0 * jnp.arange(half_size, dtype=jnp.float32) / head_size
    inverse = ROPE_BASE ** (-exponent)
    angles = positions.astype(jnp.float32)[:, None] * inverse[None, :]
    cosine_half = jnp.cos(angles)
    sine_half = jnp.sin(angles)
    return (
        jnp.concatenate([cosine_half, cosine_half], axis=1),
        jnp.concatenate([sine_half, sine_half], axis=1),
    )


def rotate(values, cosine_table, sine_table):
    half_size = values.shape[-1] // 2
    first_half = values[..., :half_size]
    second_half = values[..., half_size:]
    turned = jnp.concatenate([-second_half, first_half], axis=-1)
    return values * cosine_table + turned * sine_table


def capacity_tables(route_block, live_block, experts, capacity):
    rows_here = route_block.shape[0]
    picks = route_block.shape[1]
    chosen = (
        route_block[:, :, None] == jnp.arange(experts, dtype=jnp.int32)[None, None, :]
    ) & live_block[:, None, None]
    counts = chosen.astype(jnp.int32).reshape(rows_here * picks, experts)
    before = jnp.cumsum(counts, axis=0, dtype=jnp.int32) - counts
    place = jnp.sum(before * counts, axis=1, dtype=jnp.int32).reshape(rows_here, picks)
    kept = live_block[:, None] & (place < capacity)
    flat = jnp.where(kept, route_block * capacity + place, experts * capacity)
    row_ids = jnp.broadcast_to(jnp.arange(rows_here, dtype=jnp.int32)[:, None], (rows_here, picks))
    table = (
        jnp.full((experts * capacity,), rows_here, jnp.int32)
        .at[flat.reshape(-1)]
        .set(row_ids.reshape(-1), mode="drop")
    )
    return (kept, flat, table)


def silu_slope(linear, logistic):
    return logistic * (1.0 + linear * (1.0 - logistic))


def expert_trip(payload, compute):
    arrived = lax.all_to_all(payload, "expert", split_axis=0, concat_axis=0, tiled=True)
    result, kept_parts = compute(arrived)
    returned = lax.all_to_all(result, "expert", split_axis=0, concat_axis=0, tiled=True)
    return (returned, kept_parts)


def shards(
    layer_input,
    attention_gain,
    query_weight,
    key_weight,
    value_weight,
    query_bias,
    key_bias,
    value_bias,
    output_weight,
    mixture_gain,
    router_weight,
    expert_gate,
    expert_up,
    expert_down,
    shared_gate,
    shared_up,
    shared_down,
    shared_switch,
    slot_lengths,
    routes,
    cotangent,
):
    inputs = layer_input[0].astype(jnp.float32)
    row_count = inputs.shape[0]
    groups = lax.axis_size("expert")
    total_rows = row_count * groups
    experts = router_weight.shape[1]
    local_experts = expert_gate.shape[0]
    capacity = row_count * TOP // experts
    score_scale = HD ** (-0.5)
    positions = lax.axis_index("expert") * row_count + jnp.arange(row_count, dtype=jnp.int32)
    length = slot_lengths[0]
    live_rows = positions < length
    key_positions = jnp.arange(total_rows, dtype=jnp.int32)
    allowed = (key_positions[None, :] <= positions[:, None]) & (key_positions[None, :] < length)
    cosine_table, sine_table = rotary_tables(positions, HD)
    cosine_table = cosine_table[:, None, :]
    sine_table = sine_table[:, None, :]
    query_full, key_full, value_full, output_full, gate_full, up_full, down_full = (
        lax.all_gather(query_weight, ("dp", "expert"), axis=0, tiled=True),
        lax.all_gather(key_weight, ("dp", "expert"), axis=0, tiled=True),
        lax.all_gather(value_weight, ("dp", "expert"), axis=0, tiled=True),
        lax.all_gather(output_weight, ("dp", "expert"), axis=0, tiled=True),
        lax.all_gather(shared_gate, ("dp", "expert"), axis=0, tiled=True),
        lax.all_gather(shared_up, ("dp", "expert"), axis=0, tiled=True),
        lax.all_gather(shared_down, ("dp", "expert"), axis=0, tiled=True),
    )
    heads_here = query_full.shape[1] // HD
    gain_one = attention_gain.astype(jnp.float32)
    inverse_one = lax.rsqrt(jnp.mean(inputs * inputs, axis=1, keepdims=True) + EPS)
    normed = (inputs * inverse_one * gain_one).astype(jnp.bfloat16)
    query_pre = jnp.dot(normed, query_full, preferred_element_type=jnp.float32) + query_bias.astype(
        jnp.float32
    )
    key_pre = jnp.dot(normed, key_full, preferred_element_type=jnp.float32) + key_bias.astype(
        jnp.float32
    )
    value_pre = jnp.dot(normed, value_full, preferred_element_type=jnp.float32) + value_bias.astype(
        jnp.float32
    )
    query_heads = (
        rotate(query_pre.reshape(row_count, heads_here, HD), cosine_table, sine_table)
        .astype(jnp.bfloat16)
        .transpose(1, 0, 2)
    )
    key_heads = (
        rotate(key_pre.reshape(row_count, heads_here, HD), cosine_table, sine_table)
        .astype(jnp.bfloat16)
        .transpose(1, 0, 2)
    )
    value_heads = (
        value_pre.astype(jnp.bfloat16).reshape(row_count, heads_here, HD).transpose(1, 0, 2)
    )
    key_all, value_all = (
        lax.all_gather(key_heads, "expert", axis=1, tiled=True),
        lax.all_gather(value_heads, "expert", axis=1, tiled=True),
    )

    def attend(operands):
        query_head, key_head, value_head = operands
        raw_scores = (
            jnp.einsum("qd,kd->qk", query_head, key_head, preferred_element_type=jnp.float32)
            * score_scale
        )
        masked = jnp.where(allowed, raw_scores, NEGATIVE)
        row_peak = jnp.max(masked, axis=1, keepdims=True)
        lifted = jnp.exp(masked - row_peak)
        denominator = jnp.sum(lifted, axis=1, keepdims=True)
        weights = (lifted / denominator).astype(jnp.bfloat16)
        head_mix = jnp.einsum("qk,kd->qd", weights, value_head, preferred_element_type=jnp.float32)
        return (head_mix, row_peak[:, 0] + jnp.log(denominator[:, 0]))

    head_out, log_sums = lax.map(attend, (query_heads, key_all, value_all))
    heads_low = head_out.astype(jnp.bfloat16).transpose(1, 0, 2).reshape(row_count, heads_here * HD)
    attended = lax.psum(
        jnp.einsum("rh,dh->rd", heads_low, output_full, preferred_element_type=jnp.float32),
        "tensor",
    )
    residual = inputs + attended
    gain_two = mixture_gain.astype(jnp.float32)
    inverse_two = lax.rsqrt(jnp.mean(residual * residual, axis=1, keepdims=True) + EPS)
    mix_in = (residual * inverse_two * gain_two).astype(jnp.bfloat16)
    logits = jnp.dot(mix_in, router_weight, preferred_element_type=jnp.float32)
    logit_lift = jnp.exp(logits - jnp.max(logits, axis=1, keepdims=True))
    router_probs = logit_lift / jnp.sum(logit_lift, axis=1, keepdims=True)
    route_block = routes[0]
    gates = jnp.take_along_axis(router_probs, route_block, axis=1)
    gate_lin = jnp.dot(mix_in, gate_full, preferred_element_type=jnp.float32)
    up_lin = jnp.dot(mix_in, up_full, preferred_element_type=jnp.float32)
    shared_hidden = (jax.nn.silu(gate_lin) * up_lin).astype(jnp.bfloat16)
    shared_part = jnp.einsum(
        "rf,df->rd", shared_hidden, down_full, preferred_element_type=jnp.float32
    )
    switch = jax.nn.sigmoid(jnp.dot(mix_in, shared_switch, preferred_element_type=jnp.float32))
    kept, flat, table = capacity_tables(route_block, live_rows, experts, capacity)
    flat_index = flat.reshape(-1)
    payload = jnp.take(mix_in, table, axis=0, mode="fill", fill_value=0).reshape(
        groups, local_experts, capacity, -1
    )

    def expert_forward(arrived):
        expert_gate_lin = jnp.einsum(
            "sjcd,jdf->sjcf", arrived, expert_gate, preferred_element_type=jnp.float32
        )
        expert_up_lin = jnp.einsum(
            "sjcd,jdf->sjcf", arrived, expert_up, preferred_element_type=jnp.float32
        )
        expert_hidden = (jax.nn.silu(expert_gate_lin) * expert_up_lin).astype(jnp.bfloat16)
        result = jnp.einsum(
            "sjcf,jdf->sjcd", expert_hidden, expert_down, preferred_element_type=jnp.float32
        )
        return (result, (arrived, expert_gate_lin, expert_up_lin, expert_hidden))

    returned, expert_kept = expert_trip(payload, expert_forward)
    pairs = jnp.take(
        returned.reshape(experts * capacity, -1), flat_index, axis=0, mode="fill", fill_value=0.0
    ).reshape(row_count, TOP, -1)
    mixture_part = switch[:, None] * shared_part + jnp.sum(gates[:, :, None] * pairs, axis=1)
    mixture = lax.psum(mixture_part, "tensor")
    layer_output = jnp.where(live_rows[:, None], residual + mixture, 0.0).astype(jnp.bfloat16)
    upstream = jnp.where(live_rows[:, None], cotangent[0].astype(jnp.float32), 0.0)
    switch_part = jnp.sum(upstream * shared_part, axis=1)
    gate_part = jnp.sum(upstream[:, None, :] * pairs, axis=2)
    shared_grad = (switch[:, None] * upstream).astype(jnp.bfloat16)
    hidden_grad = jnp.einsum(
        "rd,df->rf", shared_grad, down_full, preferred_element_type=jnp.float32
    )
    logistic = jax.nn.sigmoid(gate_lin)
    up_lin_grad = (hidden_grad * gate_lin * logistic).astype(jnp.bfloat16)
    gate_lin_grad = (hidden_grad * up_lin * silu_slope(gate_lin, logistic)).astype(jnp.bfloat16)
    down_full_grad = jnp.einsum(
        "rd,rf->df", shared_grad, shared_hidden, preferred_element_type=jnp.float32
    )
    gate_full_grad = jnp.einsum(
        "rd,rf->df", mix_in, gate_lin_grad, preferred_element_type=jnp.float32
    )
    up_full_grad = jnp.einsum("rd,rf->df", mix_in, up_lin_grad, preferred_element_type=jnp.float32)
    input_part = jnp.einsum(
        "rf,df->rd", gate_lin_grad, gate_full, preferred_element_type=jnp.float32
    ) + jnp.einsum("rf,df->rd", up_lin_grad, up_full, preferred_element_type=jnp.float32)
    gate_table = (
        jnp.zeros((experts * capacity,), jnp.float32)
        .at[flat_index]
        .set(gates.reshape(-1), mode="drop")
    )
    gathered_up = jnp.take(upstream, table, axis=0, mode="fill", fill_value=0.0)
    back_payload = (
        (gate_table[:, None] * gathered_up)
        .astype(jnp.bfloat16)
        .reshape(groups, local_experts, capacity, -1)
    )

    def expert_backward(arrived_grad):
        arrived, expert_gate_lin, expert_up_lin, expert_hidden = expert_kept
        expert_hidden_grad = jnp.einsum(
            "sjcd,jdf->sjcf", arrived_grad, expert_down, preferred_element_type=jnp.float32
        )
        expert_logistic = jax.nn.sigmoid(expert_gate_lin)
        expert_up_grad = (expert_hidden_grad * expert_gate_lin * expert_logistic).astype(
            jnp.bfloat16
        )
        expert_gate_grad = (
            expert_hidden_grad * expert_up_lin * silu_slope(expert_gate_lin, expert_logistic)
        ).astype(jnp.bfloat16)
        down_sum = jnp.einsum(
            "sjcd,sjcf->jdf", arrived_grad, expert_hidden, preferred_element_type=jnp.float32
        )
        gate_sum = jnp.einsum(
            "sjcd,sjcf->jdf", arrived, expert_gate_grad, preferred_element_type=jnp.float32
        )
        up_sum = jnp.einsum(
            "sjcd,sjcf->jdf", arrived, expert_up_grad, preferred_element_type=jnp.float32
        )
        result = jnp.einsum(
            "sjcf,jdf->sjcd", expert_gate_grad, expert_gate, preferred_element_type=jnp.float32
        ) + jnp.einsum(
            "sjcf,jdf->sjcd", expert_up_grad, expert_up, preferred_element_type=jnp.float32
        )
        return (result, (gate_sum, up_sum, down_sum))

    returned_grad, expert_sums = expert_trip(back_payload, expert_backward)
    pair_grads = jnp.take(
        returned_grad.reshape(experts * capacity, -1),
        flat_index,
        axis=0,
        mode="fill",
        fill_value=0.0,
    ).reshape(row_count, TOP, -1)
    expert_input = jnp.sum(pair_grads, axis=1)
    summed_input, summed_gates, summed_switch = lax.psum(
        (input_part + expert_input, gate_part, switch_part), "tensor"
    )
    one_hot = (
        route_block[:, :, None] == jnp.arange(experts, dtype=jnp.int32)[None, None, :]
    ).astype(jnp.float32)
    probs_grad = jnp.sum(summed_gates[:, :, None] * one_hot, axis=1)
    logits_grad = (
        router_probs * (probs_grad - jnp.sum(router_probs * probs_grad, axis=1, keepdims=True))
    ).astype(jnp.bfloat16)
    switch_grad = (summed_switch * switch * (1.0 - switch)).astype(jnp.bfloat16)
    router_grad = jnp.einsum("rd,re->de", mix_in, logits_grad, preferred_element_type=jnp.float32)
    switch_vector_grad = jnp.einsum(
        "rd,r->d", mix_in, switch_grad, preferred_element_type=jnp.float32
    )
    mix_grad = (
        summed_input
        + jnp.einsum("re,de->rd", logits_grad, router_weight, preferred_element_type=jnp.float32)
        + switch_grad.astype(jnp.float32)[:, None] * shared_switch.astype(jnp.float32)[None, :]
    )
    scaled_two = mix_grad * gain_two
    mixture_gain_grad = jnp.sum(mix_grad * residual * inverse_two, axis=0)
    residual_grad = (
        upstream
        + inverse_two * scaled_two
        - residual * inverse_two**3 * jnp.mean(scaled_two * residual, axis=1, keepdims=True)
    )
    attended_grad = residual_grad.astype(jnp.bfloat16)
    output_full_grad = jnp.einsum(
        "rd,rh->dh", attended_grad, heads_low, preferred_element_type=jnp.float32
    )
    heads_grad = jnp.einsum(
        "rd,dh->rh", attended_grad, output_full, preferred_element_type=jnp.float32
    )
    heads_grad = (
        heads_grad.astype(jnp.bfloat16).reshape(row_count, heads_here, HD).transpose(1, 0, 2)
    )

    def attend_back(operands):
        query_head, key_head, value_head, grad_head, log_sum = operands
        raw_scores = (
            jnp.einsum("qd,kd->qk", query_head, key_head, preferred_element_type=jnp.float32)
            * score_scale
        )
        masked = jnp.where(allowed, raw_scores, NEGATIVE)
        weights = jnp.exp(masked - log_sum[:, None])
        weight_grad = jnp.einsum(
            "qd,kd->qk", grad_head, value_head, preferred_element_type=jnp.float32
        )
        centre = jnp.sum(weights * weight_grad, axis=1, keepdims=True)
        score_grad = (weights * (weight_grad - centre)).astype(jnp.bfloat16)
        query_grad = (
            jnp.einsum("qk,kd->qd", score_grad, key_head, preferred_element_type=jnp.float32)
            * score_scale
        )
        key_grad = (
            jnp.einsum("qk,qd->kd", score_grad, query_head, preferred_element_type=jnp.float32)
            * score_scale
        )
        value_grad = jnp.einsum(
            "qk,qd->kd", weights.astype(jnp.bfloat16), grad_head, preferred_element_type=jnp.float32
        )
        return (query_grad, key_grad, value_grad)

    query_grads, key_grads, value_grads = lax.map(
        attend_back, (query_heads, key_all, value_all, heads_grad, log_sums)
    )
    key_sums, value_sums = (
        lax.psum_scatter(key_grads, "expert", scatter_dimension=1, tiled=True),
        lax.psum_scatter(value_grads, "expert", scatter_dimension=1, tiled=True),
    )
    query_pre_grad = (
        rotate(query_grads.transpose(1, 0, 2), cosine_table, -sine_table)
        .astype(jnp.bfloat16)
        .reshape(row_count, -1)
    )
    key_pre_grad = (
        rotate(key_sums.transpose(1, 0, 2), cosine_table, -sine_table)
        .astype(jnp.bfloat16)
        .reshape(row_count, -1)
    )
    value_pre_grad = value_sums.transpose(1, 0, 2).astype(jnp.bfloat16).reshape(row_count, -1)
    query_full_grad = jnp.einsum(
        "rd,rh->dh", normed, query_pre_grad, preferred_element_type=jnp.float32
    )
    key_full_grad = jnp.einsum(
        "rd,rh->dh", normed, key_pre_grad, preferred_element_type=jnp.float32
    )
    value_full_grad = jnp.einsum(
        "rd,rh->dh", normed, value_pre_grad, preferred_element_type=jnp.float32
    )
    query_bias_grad = jnp.sum(query_pre_grad.astype(jnp.float32), axis=0)
    key_bias_grad = jnp.sum(key_pre_grad.astype(jnp.float32), axis=0)
    value_bias_grad = jnp.sum(value_pre_grad.astype(jnp.float32), axis=0)
    normed_part = (
        jnp.einsum("rh,dh->rd", query_pre_grad, query_full, preferred_element_type=jnp.float32)
        + jnp.einsum("rh,dh->rd", key_pre_grad, key_full, preferred_element_type=jnp.float32)
        + jnp.einsum("rh,dh->rd", value_pre_grad, value_full, preferred_element_type=jnp.float32)
    )
    normed_grad = lax.psum(normed_part, "tensor")
    scaled_one = normed_grad * gain_one
    attention_gain_grad = jnp.sum(normed_grad * inputs * inverse_one, axis=0)
    input_grad = (
        residual_grad
        + inverse_one * scaled_one
        - inputs * inverse_one**3 * jnp.mean(scaled_one * inputs, axis=1, keepdims=True)
    )
    dense_sums = (
        lax.psum_scatter(query_full_grad, ("dp", "expert"), scatter_dimension=0, tiled=True),
        lax.psum_scatter(key_full_grad, ("dp", "expert"), scatter_dimension=0, tiled=True),
        lax.psum_scatter(value_full_grad, ("dp", "expert"), scatter_dimension=0, tiled=True),
        lax.psum_scatter(output_full_grad, ("dp", "expert"), scatter_dimension=0, tiled=True),
        lax.psum_scatter(gate_full_grad, ("dp", "expert"), scatter_dimension=0, tiled=True),
        lax.psum_scatter(up_full_grad, ("dp", "expert"), scatter_dimension=0, tiled=True),
        lax.psum_scatter(down_full_grad, ("dp", "expert"), scatter_dimension=0, tiled=True),
    )
    gate_sums, up_sums, down_sums = expert_sums
    expert_totals = lax.psum((gate_sums, up_sums, down_sums), "dp")
    small_totals = lax.psum(
        (
            attention_gain_grad,
            query_bias_grad,
            key_bias_grad,
            value_bias_grad,
            mixture_gain_grad,
            router_grad,
            switch_vector_grad,
        ),
        ("dp", "expert"),
    )
    return (
        layer_output[None],
        input_grad[None],
        small_totals[0],
        dense_sums[0],
        dense_sums[1],
        dense_sums[2],
        small_totals[1],
        small_totals[2],
        small_totals[3],
        dense_sums[3],
        small_totals[4],
        small_totals[5],
        expert_totals[0],
        expert_totals[1],
        expert_totals[2],
        dense_sums[4],
        dense_sums[5],
        dense_sums[6],
        small_totals[6],
    )


def solution(mesh):
    in_specs = (
        P("dp", "expert", None),
        P(),
        P(("dp", "expert"), "tensor"),
        P(("dp", "expert"), "tensor"),
        P(("dp", "expert"), "tensor"),
        P("tensor"),
        P("tensor"),
        P("tensor"),
        P(("dp", "expert"), "tensor"),
        P(),
        P(),
        P("expert", None, "tensor"),
        P("expert", None, "tensor"),
        P("expert", None, "tensor"),
        P(("dp", "expert"), "tensor"),
        P(("dp", "expert"), "tensor"),
        P(("dp", "expert"), "tensor"),
        P(),
        P("dp"),
        P("dp", "expert", None),
        P("dp", "expert", None),
    )
    out_specs = (
        P("dp", "expert", None),
        P("dp", "expert", None),
        P(),
        P(("dp", "expert"), "tensor"),
        P(("dp", "expert"), "tensor"),
        P(("dp", "expert"), "tensor"),
        P("tensor"),
        P("tensor"),
        P("tensor"),
        P(("dp", "expert"), "tensor"),
        P(),
        P(),
        P("expert", None, "tensor"),
        P("expert", None, "tensor"),
        P("expert", None, "tensor"),
        P(("dp", "expert"), "tensor"),
        P(("dp", "expert"), "tensor"),
        P(("dp", "expert"), "tensor"),
        P(),
    )
    return jax.shard_map(shards, mesh=mesh, in_specs=in_specs, out_specs=out_specs, check_vma=False)
```

profile of v0, /device:TPU:0, one launch (start us, length us, event | category | flops | bytes accessed | tf_op | source)
XLA Modules:
  0.0 2849.2 jit_solution(13813683340053790222)
XLA Ops:
  15.6 25.0 all-gather.12.cloned.1.call-done
  46.2 24.2 all-gather.10.cloned.1.call-done
  76.0 24.2 all-gather.16.cloned.1.call-done
  128.7 20.7 all-gather.18.cloned.1.call-done
  149.4 39.8 %while.30 = (s32[]{:T(128)}, bf16[4,512,128]{1,2,0:T(8,128)(2,1)S(1)}, f32[4,512]{1,0:T(4,128)}, bf16[4,512,128]{2,1,0:T(8,128)(2,1)}, bf16[4,2048,128]{2,1,0:T(...) while((s32[]{:T(128)}, ...), condition=%wide.region_4.5_spmd.clone.clone, body=%wide.region_1.4_spmd.clone.sunk.clone | while | flops 547356160 | bytes 30828660 | solution.py:160
  208.0 141.7 %all-reduce.10.cloned.1.call-done = f32[512,2048]{1,0:T(8,128)} async-done(((f32[512,2048]{1,0:T(8,128)}), f32[512,2048]{1,0:T(8,128)}) %all-reduce.10.cloned.1.call-update) | async-done | bytes 4194320 | tf_op jit(solution)/shard_map/psum | solution.py:162
  357.0 18.4 gather_fusion
  389.2 116.2 %all-to-all-done = bf16[4,2,256,2048]{3,2,1,0:T(8,128)(2,1)} async-done(((bf16[4,2,256,2048]{3,2,1,0:T(8,128)(2,1)}), bf16[4,2,256,2048]{3,2,1,0:T(8,128)(2,1)}, u32[]{:S(2)}, u32[]{:S(2)}) %all-to-all-start) | async-done | bytes 8388640 | tf_op jit(solution)/shard_map/all_to_all | solution.py:61
  559.4 51.0 %all-gather.26.cloned.1.call-done = bf16[2048,1408]{1,0:T(8,128)(2,1)} async-done(((bf16[256,1408]{1,0:T(8,128)(2,1)}), bf16[2048,1408]{1,0:T(8,128)(2,1)}) %all-gather.26.cloned.1.call-update) | async-done | bytes 5767184 | tf_op jit(solution)/shard_map/all_gather | solution.py:113
  621.0 18.8 gather_fusion.1
  650.2 19.4 mul.424
  671.8 74.1 %all-to-all-done.1 = f32[4,2,256,2048]{3,2,1,0:T(8,128)} async-done(((f32[4,2,256,2048]{3,2,1,0:T(8,128)}), f32[4,2,256,2048]{3,2,1,0:T(8,128)}, u32[]{:S(2)}, u32[]{:S(2)}) %all-to-all-start.1) | async-done | bytes 16777248 | tf_op jit(solution)/shard_map/all_to_all | solution.py:63
  745.9 22.3 gather_fusion.3
  786.4 24.5 all-reduce.1
  839.3 96.9 %all_to_all.20 = bf16[4,2,256,2048]{3,2,1,0:T(8,128)(2,1)} all-to-all(bf16[4,2,256,2048]{3,2,1,0:T(8,128)(2,1)S(1)} %multiply_convert_fusion.1), channel_id=1, replica_groups=mesh['dp'=2,'expert'=4,'tensor'=4] {'expert'}, dimensions={0} | all-to-all | bytes 16777216 | tf_op jit(solution)/shard_map/all_to_all | solution.py:61
  1006.4 163.6 %all-to-all-done.3 = f32[4,2,256,2048]{3,2,1,0:T(8,128)} async-done(((f32[4,2,256,2048]{3,2,1,0:T(8,128)}), f32[4,2,256,2048]{3,2,1,0:T(8,128)}, u32[]{:S(2)}, u32[]{:S(2)}) %all-to-all-start.3) | async-done | bytes 16777248 | tf_op jit(solution)/shard_map/all_to_all | solution.py:63
  1170.0 22.4 gather_fusion.4
  1204.0 19.0 reshape.433
  1247.9 151.7 %all-reduce.12.cloned.1.call-done = f32[512,2048]{1,0:T(8,128)} async-done(((f32[512,2048]{1,0:T(8,128)}), f32[512,2048]{1,0:T(8,128)}) %all-reduce.12.cloned.1.call-update) | async-done | bytes 4194320 | tf_op jit(solution)/shard_map/psum | solution.py:277
  1410.1 81.5 %while.31 = (s32[]{:T(128)}, f32[4,512,128]{1,2,0:T(8,128)}, f32[4,2048,128]{1,2,0:T(8,128)}, f32[4,2048,128]{1,2,0:T(8,128)}, bf16[4,512,128]{2,1,0:T(8,128)(2,...) while((s32[]{:T(128)}, f32[4,512,128]{1,2,0:T(8,128)}, ...), condition=%wide.region_27.29_spmd.clone.clone, body=%wide.region_25.28_spmd.clone.sunk.clone | while | flops 1354038784 | bytes 57952912 | solution.py:341
  1492.9 18.0 reshape.431
  1545.2 37.3 %reduce-scatter.12.cloned.1.call-done = f32[4,512,128]{1,2,0:T(8,128)} async-done(((f32[4,2048,128]{1,2,0:T(8,128)}), f32[4,512,128]{1,2,0:T(8,128)}) %reduce-scatter.12.cloned.1.call-update) | async-done | bytes 1048592 | tf_op jit(solution)/shard_map/reduce_scatter | solution.py:346
  1670.5 212.6 %all-reduce.16.cloned.1.call-done = (f32[512,2048]{1,0:T(8,128)}, f32[512,2048]{1,0:T(8,128)}) async-done(((f32[512,2048]{1,0:T(8,128)}, f32[512,2048]{1,0:T(8,128)}), (f32[512,2048]{1,0:T(8,128)}, f32[512,2048]{1,0:T(8,128)})) %all-reduce.16.cloned.1.call-update) | async-done | bytes 8388624 | tf_op jit(solution)/shard_map/psum | solution.py:206
  1887.3 24.6 all-reduce
  1938.1 90.6 %reduce-scatter.22.cloned.1.call-done = f32[256,1408]{1,0:T(8,128)} async-done(((f32[2048,1408]{1,0:T(8,128)}), f32[256,1408]{1,0:T(8,128)}) %reduce-scatter.22.cloned.1.call-update) | async-done | bytes 1441808 | tf_op jit(solution)/shard_map/reduce_scatter | solution.py:389
  2028.7 91.1 %reduce-scatter.24.cloned.1.call-done = f32[256,1408]{1,0:T(8,128)} async-done(((f32[2048,1408]{1,0:T(8,128)}), f32[256,1408]{1,0:T(8,128)}) %reduce-scatter.24.cloned.1.call-update) | async-done | bytes 1441808 | tf_op jit(solution)/shard_map/reduce_scatter | solution.py:390
  2119.8 91.1 %reduce-scatter.26.cloned.1.call-done = f32[256,1408]{1,0:T(8,128)} async-done(((f32[2048,1408]{1,0:T(8,128)}), f32[256,1408]{1,0:T(8,128)}) %reduce-scatter.26.cloned.1.call-update) | async-done | bytes 1441808 | tf_op jit(solution)/shard_map/reduce_scatter | solution.py:391
  2210.9 394.5 %all-reduce.18.cloned.1.call-done = (f32[2,2048,352]{1,2,0:T(8,128)}, f32[2,2048,352]{1,2,0:T(8,128)}, f32[2,2048,352]{1,2,0:T(8,128)}) async-done(((f32[2,2048,352]{1,2,0:T(8,128)}, f32[2,2048,352]{1,2,0:T(8,128)}, f32[2,2048,352]{1,2,0:T(8,128)}), (f32[2,2048,352]{1,2,0:T(8,128)}, f32[2,2048,352]{1,2,0:T(8,128)}, f32[2,2048,352]{1,2,0:T(8,128)})) %all-reduce.18.cloned.1.call-update) | async-done | bytes 17301520 | tf_op jit(solution)/shard_map/psum | solution.py:394
  2605.4 56.9 %reduce-scatter.20.cloned.1.call-done = f32[256,512]{1,0:T(8,128)} async-done(((f32[2048,512]{1,0:T(8,128)}), f32[256,512]{1,0:T(8,128)}) %reduce-scatter.20.cloned.1.call-update) | async-done | bytes 524304 | tf_op jit(solution)/shard_map/reduce_scatter | solution.py:388
  2662.4 55.3 %reduce-scatter.14.cloned.1.call-done = f32[256,512]{1,0:T(8,128)} async-done(((f32[2048,512]{1,0:T(8,128)}), f32[256,512]{1,0:T(8,128)}) %reduce-scatter.14.cloned.1.call-update) | async-done | bytes 524304 | tf_op jit(solution)/shard_map/reduce_scatter | solution.py:385
  2717.7 55.7 %reduce-scatter.16.cloned.1.call-done = f32[256,512]{1,0:T(8,128)} async-done(((f32[2048,512]{1,0:T(8,128)}), f32[256,512]{1,0:T(8,128)}) %reduce-scatter.16.cloned.1.call-update) | async-done | bytes 524304 | tf_op jit(solution)/shard_map/reduce_scatter | solution.py:386
  2773.3 55.3 %reduce-scatter.18.cloned.1.call-done = f32[256,512]{1,0:T(8,128)} async-done(((f32[2048,512]{1,0:T(8,128)}), f32[256,512]{1,0:T(8,128)}) %reduce-scatter.18.cloned.1.call-update) | async-done | bytes 524304 | tf_op jit(solution)/shard_map/reduce_scatter | solution.py:387
  (433 shorter events, 615.9 us)
Async XLA Ops:
  7.2 514.4 %copy-start = (bf16[2,2048,352]{1,2,0:T(8,128)(2,1)S(1)}, bf16[2,2048,352]{1,2,0:T(8,128)(2,1)}, u32[]{:S(2)}) copy-start(bf16[2,2048,352]{1,2,0:T(8,128)(2,1)} %param.40) | copy-start | bytes 8650756
  7.2 33.4 %all-gather.12.cloned.1.call-start = ((), (), s32[]{:S(2)}) async-start(), calls=%async_computation.14 | async-start | bytes 2359296 | tf_op jit(solution)/shard_map/all_gather | solution.py:108
  7.9 62.4 %all-gather.10.cloned.1.call-start = ((), (), s32[]{:S(2)}) async-start(), calls=%async_computation.13 | async-start | bytes 2359296 | tf_op jit(solution)/shard_map/all_gather | solution.py:107
  8.7 91.5 %all-gather.16.cloned.1.call-start = ((), (), s32[]{:S(2)}) async-start(), calls=%async_computation.16 | async-start | bytes 2359296 | tf_op jit(solution)/shard_map/all_gather | solution.py:109
  9.4 115.4 %all-gather.14.cloned.1.call-start = ((), (), s32[]{:S(2)}) async-start(), calls=%async_computation.15 | async-start | bytes 2621440 | tf_op jit(solution)/shard_map/all_gather | solution.py:142
  75.9 73.5 %all-gather.18.cloned.1.call-start = ((), (), s32[]{:S(2)}) async-start(), calls=%async_computation.17 | async-start | bytes 2621440 | tf_op jit(solution)/shard_map/all_gather | solution.py:143
  106.7 82.6 %all-gather.20.cloned.1.call-start = ((), (), s32[]{:S(2)}) async-start(), calls=%async_computation.18 | async-start | bytes 2359296 | tf_op jit(solution)/shard_map/all_gather | solution.py:110
  107.2 242.5 %all-reduce.10.cloned.1.call-start = ((), (), s32[]{:S(2)}) async-start(), calls=%async_computation.19 | async-start | bytes 8388608 | tf_op jit(solution)/shard_map/psum | solution.py:162
  194.4 346.4 %all-gather.22.cloned.1.call-start = ((), (), s32[]{:S(2)}) async-start(), calls=%async_computation.20 | async-start | bytes 6488064 | tf_op jit(solution)/shard_map/all_gather | solution.py:111
  195.3 345.0 %copy-start.14 = (s32[1,512,4]{2,1,0:T(8,128)}, s32[1,512,4]{2,1,0:T(8,128)S(1)}, u32[]{:S(2)}) copy-start(s32[1,512,4]{2,1,0:T(8,128)S(1)} %copy.100) | copy-start | bytes 24580
  195.7 345.1 %copy-start.42 = (s32[2048]{0:T(1024)}, s32[2048]{0:T(1024)S(1)}, u32[]{:S(2)}) copy-start(s32[2048]{0:T(1024)S(1)} %eq.39) | copy-start | bytes 24580
  195.7 414.8 %copy-start.69 = (pred[512]{0:T(512)(128)(4,1)}, pred[512]{0:T(512)(128)(4,1)S(1)}, u32[]{:S(2)}) copy-start(pred[512]{0:T(512)(128)(4,1)S(1)} %fusion.119) | copy-start | bytes 1540
  382.7 122.7 %all-to-all-start = ((bf16[4,2,256,2048]{3,2,1,0:T(8,128)(2,1)}), bf16[4,2,256,2048]{3,2,1,0:T(8,128)(2,1)}, u32[]{:S(2)}, u32[]{:S(2)}) async-start(bf16[4,2,256,2048]{3,2,1,0:T(8,128)(2,1)} %broadcast_select_fusion.2), calls=%async_computation | async-start | bytes 16777216 | tf_op jit(solution)/shard_map/all_to_all | solution.py:61
  388.5 160.6 %all-gather.24.cloned.1.call-start = ((), (), s32[]{:S(2)}) async-start(), calls=%async_computation.21 | async-start | bytes 6488064 | tf_op jit(solution)/shard_map/all_gather | solution.py:112
  532.7 213.3 %all-to-all-start.1 = ((f32[4,2,256,2048]{3,2,1,0:T(8,128)}), f32[4,2,256,2048]{3,2,1,0:T(8,128)}, u32[]{:S(2)}, u32[]{:S(2)}) async-start(f32[4,2,256,2048]{3,2,1,0:T(8,128)} %copy.108), calls=%async_computation.1 | async-start | bytes 33554432 | tf_op jit(solution)/shard_map/all_to_all | solution.py:63
  539.7 70.7 %all-gather.26.cloned.1.call-start = ((), (), s32[]{:S(2)}) async-start(), calls=%async_computation.22 | async-start | bytes 6488064 | tf_op jit(solution)/shard_map/all_gather | solution.py:113
  979.7 190.2 %all-to-all-start.3 = ((f32[4,2,256,2048]{3,2,1,0:T(8,128)}), f32[4,2,256,2048]{3,2,1,0:T(8,128)}, u32[]{:S(2)}, u32[]{:S(2)}) async-start(f32[4,2,256,2048]{3,2,1,0:T(8,128)} %copy.110), calls=%async_computation.3 | async-start | bytes 33554432 | tf_op jit(solution)/shard_map/all_to_all | solution.py:63
  986.9 412.7 %all-reduce.12.cloned.1.call-start = ((), (), s32[]{:S(2)}) async-start(), calls=%async_computation.23 | async-start | bytes 8388608 | tf_op jit(solution)/shard_map/psum | solution.py:277
  1247.2 288.1 %reduce-scatter.10.cloned.1.call-start = ((), (), s32[]{:S(2)}) async-start(), calls=%async_computation.24 | async-start | bytes 5242880 | tf_op jit(solution)/shard_map/reduce_scatter | solution.py:345
  1491.6 90.9 %reduce-scatter.12.cloned.1.call-start = ((), (), s32[]{:S(2)}) async-start(), calls=%async_computation.25 | async-start | bytes 5242880 | tf_op jit(solution)/shard_map/reduce_scatter | solution.py:346
  1492.3 390.8 %all-reduce.16.cloned.1.call-start = ((), (), s32[]{:S(2)}) async-start(), calls=%async_computation.34 | async-start | bytes 16777216 | tf_op jit(solution)/shard_map/psum | solution.py:206
  1591.4 346.7 %all-reduce.14.cloned.1.call-start = ((), (), s32[]{:S(2)}) async-start(), calls=%async_computation.30 | async-start | bytes 131072 | tf_op jit(solution)/shard_map/psum | solution.py:395
  1594.0 434.6 %reduce-scatter.22.cloned.1.call-start = ((), (), s32[]{:S(2)}) async-start(), calls=%async_computation.31 | async-start | bytes 12976128 | tf_op jit(solution)/shard_map/reduce_scatter | solution.py:389
  1601.6 518.2 %reduce-scatter.24.cloned.1.call-start = ((), (), s32[]{:S(2)}) async-start(), calls=%async_computation.32 | async-start | bytes 12976128 | tf_op jit(solution)/shard_map/reduce_scatter | solution.py:390
  1609.3 601.6 %reduce-scatter.26.cloned.1.call-start = ((), (), s32[]{:S(2)}) async-start(), calls=%async_computation.33 | async-start | bytes 12976128 | tf_op jit(solution)/shard_map/reduce_scatter | solution.py:391
  1619.6 985.8 %all-reduce.18.cloned.1.call-start = ((), (), s32[]{:S(2)}) async-start(), calls=%async_computation.35 | async-start | bytes 34603008 | tf_op jit(solution)/shard_map/psum | solution.py:394
  1646.3 1016.1 %reduce-scatter.20.cloned.1.call-start = ((), (), s32[]{:S(2)}) async-start(), calls=%async_computation.29 | async-start | bytes 4718592 | tf_op jit(solution)/shard_map/reduce_scatter | solution.py:388
  1652.0 1065.6 %reduce-scatter.14.cloned.1.call-start = ((), (), s32[]{:S(2)}) async-start(), calls=%async_computation.26 | async-start | bytes 4718592 | tf_op jit(solution)/shard_map/reduce_scatter | solution.py:385
  1657.9 1115.5 %reduce-scatter.16.cloned.1.call-start = ((), (), s32[]{:S(2)}) async-start(), calls=%async_computation.27 | async-start | bytes 4718592 | tf_op jit(solution)/shard_map/reduce_scatter | solution.py:386
  1663.3 1165.3 %reduce-scatter.18.cloned.1.call-start = ((), (), s32[]{:S(2)}) async-start(), calls=%async_computation.28 | async-start | bytes 4718592 | tf_op jit(solution)/shard_map/reduce_scatter | solution.py:387
  1670.1 241.8 %copy-start.63 = (f32[512]{0:T(512)S(1)}, f32[512]{0:T(512)}, u32[]{:S(2)}) copy-start(f32[512]{0:T(512)} %get-tuple-element.316) | copy-start | bytes 6148
  1670.5 241.4 %copy-start.7 = (bf16[1,512,2048]{2,1,0:T(8,128)(2,1)S(1)}, bf16[1,512,2048]{2,1,0:T(8,128)(2,1)}, u32[]{:S(2)}) copy-start(bf16[1,512,2048]{2,1,0:T(8,128)(2,1)} %param.27) | copy-start | bytes 6291460
  (83 other events, 2502.9 us)
Sparse Core Ops, SparseCore 0:
  9.9 30.5 all-gather.11
  42.4 27.8 all-gather.9
  72.3 27.8 all-gather.15
  102.2 22.5 all-gather.13
  126.8 22.5 all-gather.17
  151.2 27.8 all-gather.19
  194.5 155.1 all-reduce.9
  351.8 43.0 all-gather.21
  396.9 68.3 all-gather.23
  542.3 68.1 all-gather.25
  1247.3 152.2 all-reduce.11
  1491.7 43.5 reduce-scatter.9
  1537.9 44.5 reduce-scatter.11
  1591.6 291.5 all-reduce.15
  1886.6 51.4 all-reduce.13
  1942.5 86.1 reduce-scatter.21
  2033.0 86.7 reduce-scatter.23
  2124.1 86.7 reduce-scatter.25
  2214.4 390.9 all-reduce.17
  2609.6 52.7 reduce-scatter.19
  2666.3 51.2 reduce-scatter.13
  2722.0 51.3 reduce-scatter.15
  2777.3 51.2 reduce-scatter.17
where the time goes:
time: 2860 us; the launch traced here: 2850 us
  waiting for transfers between devices  1980 us (69%)
  matrix products  293 us (10%)
  local copies, waits for them, and re-layouts  276 us (10%)
  blocking collectives  146 us (5%)
  other arithmetic  119 us (4%)
    psum x1, waiting for transfers between devices, shards(): expert_totals = lax.psum((gate_sums, up_sums, down_sums), 'dp')  395 us
    all_to_all x2, waiting for transfers between devices, expert_trip(): lax.all_to_all(result, 'expert', split_axis=0, concat_axis=0, tiled=True)  238 us
    psum x1, waiting for transfers between devices, shards(): mixture = lax.psum(mixture_part, 'tensor')  213 us
    psum x1, waiting for transfers between devices, shards(): lax.psum((input_part + expert_input, gate_part, switch_part), 'tensor')  152 us
    psum x1, waiting for transfers between devices, shards(): lax.psum(jnp.einsum('rh,dh->rd', heads_low, output_full, preferred_elemen...  142 us
    all_to_all x1, waiting for transfers between devices, expert_trip(): lax.all_to_all(payload, 'expert', split_axis=0, concat_axis=0, tiled=True)  116 us
    all_to_all x1, blocking collectives, expert_trip(): lax.all_to_all(payload, 'expert', split_axis=0, concat_axis=0, tiled=True)  96.9 us
    reduce_scatter x1, waiting for transfers between devices, shards(): lax.psum_scatter(down_full_grad, ('dp', 'expert'), scatter_dimension=0, t...  91.1 us
  transfers between devices with their start and end apart: 26, of which 23 were waited for; matrix products, arithmetic and copies ran while one was open for 13% of the time, Pallas kernels for 0%

commit v1 on v0

v1 whole, which is shorter than its diff:
```python
import functools

import jax
import jax.numpy as jnp
from jax import lax
from jax.experimental import pallas as pl
from jax.experimental.pallas import tpu as pltpu
from jax.sharding import PartitionSpec as P

HD = 128
TOP = 4
LANES = 128

EPS = 1e-06
ROPE_BASE = 1000000.0
NEGATIVE = -1e30
F32 = jnp.float32
BF16 = jnp.bfloat16


def up_to(value, multiple):
    return -(-value // multiple) * multiple


def rotary_tables(positions, head_size):
    half_size = head_size // 2
    exponent = 2.0 * jnp.arange(half_size, dtype=F32) / head_size
    inverse = ROPE_BASE ** (-exponent)
    angles = positions.astype(F32)[:, None] * inverse[None, :]
    cosine_half = jnp.cos(angles)
    sine_half = jnp.sin(angles)
    return (
        jnp.concatenate([cosine_half, cosine_half], axis=1),
        jnp.concatenate([sine_half, sine_half], axis=1),
    )


def rotate(values, cosine_table, sine_table):
    half_size = values.shape[-1] // 2
    first_half = values[..., :half_size]
    second_half = values[..., half_size:]
    turned = jnp.concatenate([-second_half, first_half], axis=-1)
    return values * cosine_table + turned * sine_table


def swap(value, axis, bit):
    size = lax.axis_size(axis)
    return lax.ppermute(value, axis, [(i, i ^ bit) for i in range(size)])


def shift(value, axis, by):
    size = lax.axis_size(axis)
    return lax.ppermute(value, axis, [(i, (i + by) % size) for i in range(size)])


def spread(value, axis):
    size = lax.axis_size(axis)
    held = {0: value}
    bit = size // 2
    while bit:
        held.update({s ^ bit: swap(v, axis, bit) for s, v in list(held.items())})
        bit //= 2
    return [held[s] for s in range(size)]


def collect(parts, axis):
    held = dict(enumerate(parts))
    bit = 1
    while bit < len(parts):
        sent = {s: swap(v, axis, bit) for s, v in held.items() if s & bit}
        held = {
            s: (v.astype(F32) + sent[s ^ bit].astype(F32)).astype(v.dtype)
            for s, v in held.items()
            if not s & bit
        }
        bit *= 2
    return held[0]


def rows_at(value, start, size):
    return lax.dynamic_slice_in_dim(value, start, size, axis=0)


def in_order(pieces, index, axis):
    size = pieces[0].shape[axis]
    shape = list(pieces[0].shape)
    shape[axis] = size * len(pieces)
    whole = jnp.zeros(shape, pieces[0].dtype)
    for piece, place in zip(pieces, index):
        whole = lax.dynamic_update_slice_in_dim(whole, piece, place * size, axis)
    return whole


def gather_over_tensor(piece):
    size = lax.axis_size("tensor")
    me = lax.axis_index("tensor")
    pieces = [piece] + [shift(piece, "tensor", k) for k in range(1, size)]
    return in_order(pieces, [(me - k) % size for k in range(size)], 0)


def dot_tt(a, b):
    return lax.dot_general(a, b, (((1,), (1,)), ((), ())), preferred_element_type=F32)


def dot_nt(a, b):
    return lax.dot_general(a, b, (((0,), (0,)), ((), ())), preferred_element_type=F32)


def dot(a, b):
    return jnp.dot(a, b, preferred_element_type=F32)


def attend_kernel(place_ref, q_ref, *refs, groups, score_scale):
    kv_refs = refs[:groups]
    out_ref, log_ref, peak, total, mix = refs[groups:]
    me, length = place_ref[0], place_ref[1]
    rows = q_ref.shape[0]
    query = q_ref[...]

    def block(s):
        key, value = kv_refs[s][:, :HD], kv_refs[s][:, HD:]
        scores = dot_tt(query, key) * score_scale
        column = lax.broadcasted_iota(jnp.int32, (rows, rows), 1)
        good = column < length - (me ^ s) * rows
        if s == 0:
            good &= column <= lax.broadcasted_iota(jnp.int32, (rows, rows), 0)
        scores = jnp.where(good, scores, NEGATIVE)
        here = jnp.max(scores, axis=1, keepdims=True)
        if s == 0:
            lifted = jnp.exp(scores - here)
            peak[...] = here
            total[...] = jnp.sum(lifted, axis=1, keepdims=True)
            mix[...] = dot(lifted.astype(BF16), value)
        else:
            new_peak = jnp.maximum(peak[...], here)
            keep = jnp.exp(peak[...] - new_peak)
            lifted = jnp.exp(scores - new_peak)
            peak[...] = new_peak
            total[...] = total[...] * keep + jnp.sum(lifted, axis=1, keepdims=True)
            mix[...] = mix[...] * keep + dot(lifted.astype(BF16), value)

    block(0)
    for s in range(1, groups):
        pl.when(((me ^ s) < me) & ((me ^ s) * rows < length))(functools.partial(block, s))
    out_ref[...] = (mix[...] / total[...]).astype(BF16)
    log_ref[0] = peak[...] + jnp.log(total[...])


def attend(place, query, kv, heads, score_scale):
    rows = query.shape[0]
    groups = len(kv)
    spec = pltpu.PrefetchScalarGridSpec(
        num_scalar_prefetch=1,
        grid=(heads,),
        in_specs=[pl.BlockSpec((rows, HD), lambda h, p: (0, h))]
        + [pl.BlockSpec((rows, 2 * HD), lambda h, p: (0, h))] * groups,
        out_specs=[
            pl.BlockSpec((rows, HD), lambda h, p: (0, h)),
            pl.BlockSpec((1, rows, 1), lambda h, p: (h, 0, 0)),
        ],
        scratch_shapes=[
            pltpu.VMEM((rows, 1), F32),
            pltpu.VMEM((rows, 1), F32),
            pltpu.VMEM((rows, HD), F32),
        ],
    )
    work = heads * rows * rows * groups
    return pl.pallas_call(
        functools.partial(attend_kernel, groups=groups, score_scale=score_scale),
        grid_spec=spec,
        out_shape=[
            jax.ShapeDtypeStruct((rows, heads * HD), BF16),
            jax.ShapeDtypeStruct((heads, rows, 1), F32),
        ],
        compiler_params=pltpu.CompilerParams(vmem_limit_bytes=40 << 20),
        cost_estimate=pl.CostEstimate(
            flops=4 * work * HD, bytes_accessed=6 << 20, transcendentals=work
        ),
    )(place, query, *kv)


def attend_back_kernel(place_ref, q_ref, g_ref, o_ref, log_ref, *refs, groups, score_scale):
    kv_refs = refs[:groups]
    dq_ref = refs[groups]
    dkv_refs = refs[groups + 1 : 2 * groups + 1]
    total = refs[2 * groups + 1]
    me, length = place_ref[0], place_ref[1]
    rows = q_ref.shape[0]
    query, grad = q_ref[...], g_ref[...]
    log_sum = log_ref[0]
    centre = jnp.sum(grad.astype(F32) * o_ref[...].astype(F32), axis=1, keepdims=True)

    def block(s):
        key, value = kv_refs[s][:, :HD], kv_refs[s][:, HD:]
        scores = dot_tt(query, key) * score_scale
        column = lax.broadcasted_iota(jnp.int32, (rows, rows), 1)
        good = column < length - (me ^ s) * rows
        if s == 0:
            good &= column <= lax.broadcasted_iota(jnp.int32, (rows, rows), 0)
        weights = jnp.exp(jnp.where(good, scores, NEGATIVE) - log_sum)
        weight_grad = dot_tt(grad, value)
        score_grad = (weights * (weight_grad - centre)).astype(BF16)
        query_grad = dot(score_grad, key)
        if s == 0:
            total[...] = query_grad
        else:
            total[...] += query_grad
        dkv_refs[s][:, :HD] = (dot_nt(score_grad, query) * score_scale).astype(BF16)
        dkv_refs[s][:, HD:] = dot_nt(weights.astype(BF16), grad).astype(BF16)

    def nothing(s):
        dkv_refs[s][...] = jnp.zeros_like(dkv_refs[s])

    block(0)
    for s in range(1, groups):
        seen = ((me ^ s) < me) & ((me ^ s) * rows < length)
        pl.when(seen)(functools.partial(block, s))
        pl.when(jnp.logical_not(seen))(functools.partial(nothing, s))
    dq_ref[...] = total[...] * score_scale


def attend_back(place, query, grad, out, log_sums, kv, heads, score_scale):
    rows = query.shape[0]
    groups = len(kv)
    head = pl.BlockSpec((rows, HD), lambda h, p: (0, h))
    pair = pl.BlockSpec((rows, 2 * HD), lambda h, p: (0, h))
    spec = pltpu.PrefetchScalarGridSpec(
        num_scalar_prefetch=1,
        grid=(heads,),
        in_specs=[head, head, head, pl.BlockSpec((1, rows, 1), lambda h, p: (h, 0, 0))]
        + [pair] * groups,
        out_specs=[head] + [pair] * groups,
        scratch_shapes=[pltpu.VMEM((rows, HD), F32)],
    )
    work = heads * rows * rows * groups
    return pl.pallas_call(
        functools.partial(attend_back_kernel, groups=groups, score_scale=score_scale),
        grid_spec=spec,
        out_shape=[jax.ShapeDtypeStruct((rows, heads * HD), F32)]
        + [jax.ShapeDtypeStruct((rows, 2 * heads * HD), BF16)] * groups,
        compiler_params=pltpu.CompilerParams(vmem_limit_bytes=48 << 20),
        cost_estimate=pl.CostEstimate(
            flops=10 * work * HD, bytes_accessed=12 << 20, transcendentals=work
        ),
    )(place, query, grad, out, log_sums, *kv)


def mixture_kernel(
    mix_ref, hidden_grad_ref, kept_ref, spot_ref, router_ref, weight_ref,
    lin_grad_ref, hidden_ref, small_ref, part_ref,
    total, probs_ref, logits_ref, gate_grad_ref, *, experts, local,
):
    step = pl.program_id(0)
    width = hidden_ref.shape[1]
    mix = mix_ref[...]
    lane = lax.broadcasted_iota(jnp.int32, kept_ref.shape, 1)

    @pl.when(step == 0)
    def _():
        logits = dot(mix, router_ref[...])
        logits_ref[...] = logits
        masked = jnp.where(lane < experts, logits, NEGATIVE)
        lifted = jnp.exp(masked - jnp.max(masked, axis=1, keepdims=True))
        probs_ref[...] = lifted / jnp.sum(lifted, axis=1, keepdims=True)
        gate_grad_ref[...] = jnp.zeros_like(gate_grad_ref)
        total[...] = jnp.zeros_like(total)

    spot = spot_ref[pl.ds(step, 1), :]
    kept = kept_ref[...].astype(F32)
    gate = jnp.sum(probs_ref[...] * kept * spot, axis=1, keepdims=True)
    switch = jax.nn.sigmoid(jnp.sum(logits_ref[...] * spot, axis=1, keepdims=True))
    routed = step < local
    scale = jnp.where(routed, gate, switch)
    weight = weight_ref[...]
    lin = dot(mix, weight)
    gate_lin, up_lin = lin[:, :width], lin[:, width:]
    logistic = jax.nn.sigmoid(gate_lin)
    silu = gate_lin * logistic
    hidden = silu * up_lin
    hidden_grad = hidden_grad_ref[...]
    row_sum = jnp.sum(hidden * hidden_grad, axis=1, keepdims=True)
    factor = jnp.where(routed, jnp.sum(kept * spot, axis=1, keepdims=True), switch * (1.0 - switch))
    gate_grad_ref[...] += row_sum * factor * spot
    hidden_ref[...] = (scale * hidden).astype(BF16)
    scaled = scale * hidden_grad
    lin_grad_ref[:, :width] = (
        scaled * up_lin * logistic * (1.0 + gate_lin * (1.0 - logistic))
    ).astype(BF16)
    lin_grad_ref[:, width:] = (scaled * silu).astype(BF16)
    total[...] += dot_tt(lin_grad_ref[...], weight)

    @pl.when(step == local)
    def _():
        grads = gate_grad_ref[...]
        probs = probs_ref[...]
        routed_grads = jnp.where(lane < experts, grads, 0.0)
        inner = jnp.sum(probs * routed_grads, axis=1, keepdims=True)
        small = jnp.where(lane < experts, probs * (grads - inner), grads).astype(BF16)
        small_ref[...] = small
        part_ref[...] = (total[...] + dot_tt(small, router_ref[...])).astype(BF16)


def mixture_chunk(mix, hidden_grad, kept, spot, router, weight, experts, local):
    rows, depth = mix.shape
    steps = local + 1
    pair = weight.shape[1] // steps
    width = pair // 2
    whole = lambda shape: pl.BlockSpec(shape, lambda j: (0, 0))
    return pl.pallas_call(
        functools.partial(mixture_kernel, experts=experts, local=local),
        grid=(steps,),
        in_specs=[
            whole((rows, depth)),
            pl.BlockSpec((rows, width), lambda j: (0, j)),
            whole((rows, LANES)),
            whole(spot.shape),
            whole((depth, LANES)),
            pl.BlockSpec((depth, pair), lambda j: (0, j)),
        ],
        out_specs=[
            pl.BlockSpec((rows, pair), lambda j: (0, j)),
            pl.BlockSpec((rows, width), lambda j: (0, j)),
            whole((rows, LANES)),
            whole((rows, depth)),
        ],
        out_shape=[
            jax.ShapeDtypeStruct((rows, steps * pair), BF16),
            jax.ShapeDtypeStruct((rows, steps * width), BF16),
            jax.ShapeDtypeStruct((rows, LANES), BF16),
            jax.ShapeDtypeStruct((rows, depth), BF16),
        ],
        scratch_shapes=[
            pltpu.VMEM((rows, depth), F32),
            pltpu.VMEM((rows, LANES), F32),
            pltpu.VMEM((rows, LANES), F32),
            pltpu.VMEM((rows, LANES), F32),
        ],
        compiler_params=pltpu.CompilerParams(vmem_limit_bytes=56 << 20),
        cost_estimate=pl.CostEstimate(
            flops=4 * rows * depth * steps * pair,
            bytes_accessed=20 << 20,
            transcendentals=rows * steps * width,
        ),
    )(mix, hidden_grad, kept, spot, router, weight)


def shards(
    layer_input,
    attention_gain,
    query_weight,
    key_weight,
    value_weight,
    query_bias,
    key_bias,
    value_bias,
    output_weight,
    mixture_gain,
    router_weight,
    expert_gate,
    expert_up,
    expert_down,
    shared_gate,
    shared_up,
    shared_down,
    shared_switch,
    slot_lengths,
    routes,
    cotangent,
):
    rows, depth = layer_input.shape[1:]
    groups = lax.axis_size("expert")
    tensors = lax.axis_size("tensor")
    slots = lax.axis_size("dp")
    slot_at = lax.axis_index("dp")
    block_at = lax.axis_index("expert")
    tensor_at = lax.axis_index("tensor")
    experts = router_weight.shape[1]
    local, _, expert_units = expert_gate.shape
    shared_units = shared_gate.shape[1] // groups
    capacity = rows * TOP // experts
    score_scale = HD ** (-0.5)
    heads_here = query_weight.shape[1] // HD
    wide = heads_here * HD
    piece = rows // tensors
    width = up_to(max(expert_units, shared_units), LANES)
    pair = 2 * width
    steps = local + 1
    length = slot_lengths[0]
    positions = block_at * rows + jnp.arange(rows, dtype=jnp.int32)
    live_rows = positions < length
    place = jnp.stack([block_at.astype(jnp.int32), length])

    qkv_full = lax.all_gather(
        jnp.concatenate([query_weight, key_weight, value_weight], axis=1),
        ("dp", "expert"), axis=0, tiled=True,
    )
    output_wide = [output_weight] + [shift(output_weight, "tensor", k) for k in range(1, tensors)]
    output_wide = in_order(output_wide, [(tensor_at - k) % tensors for k in range(tensors)], 1)
    output_full = lax.all_gather(output_wide, ("dp", "expert"), axis=0, tiled=True)

    route_block = routes[0]
    expert_ids = jnp.arange(experts, dtype=jnp.int32)
    chosen = jnp.any(route_block[:, :, None] == expert_ids[None, None, :], axis=1) & live_rows[:, None]
    row_ids = jnp.arange(rows, dtype=jnp.int32)
    earlier = (row_ids[None, :] < row_ids[:, None]).astype(BF16)
    before = dot(earlier, chosen.astype(BF16))
    kept = chosen & (before < capacity)
    kept = jnp.pad(kept.astype(BF16), ((0, 0), (0, LANES - experts)))
    kept_blocks = spread(kept, "expert")

    shared_own = jnp.stack([shared_gate, shared_up, shared_down])
    own_rows = shared_own.shape[1]

    def units_of(block):
        return lax.dynamic_slice_in_dim(shared_own, block * shared_units, shared_units, axis=2)

    shared_pieces = [units_of(block_at)] + [
        swap(units_of(block_at ^ s), "expert", s) for s in range(1, groups)
    ]
    shared_half = in_order(shared_pieces, [block_at ^ s for s in range(groups)], 1)
    halves = [shared_half] + [shift(shared_half, "dp", k) for k in range(1, slots)]
    shared_all = in_order(halves, [(slot_at - k) % slots for k in range(slots)], 1)

    def pad_units(weight):
        return jnp.pad(weight, ((0, 0), (0, width - weight.shape[1])))

    weight_parts = []
    for j in range(local):
        weight_parts += [pad_units(expert_gate[j]), pad_units(expert_up[j])]
    weight_parts += [pad_units(shared_all[0]), pad_units(shared_all[1])]
    lin_weight = jnp.concatenate(weight_parts, axis=1)
    down_weight = jnp.concatenate(
        [pad_units(expert_down[j]) for j in range(local)] + [pad_units(shared_all[2])], axis=1
    )
    small_weight = jnp.pad(
        jnp.concatenate([router_weight, shared_switch[:, None]], axis=1),
        ((0, 0), (0, LANES - experts - 1)),
    )
    spot_at = jnp.concatenate(
        [block_at * local + jnp.arange(local, dtype=jnp.int32), jnp.full((1,), experts, jnp.int32)]
    )
    spot = (spot_at[:, None] == jnp.arange(LANES, dtype=jnp.int32)[None, :]).astype(F32)
    spot = jnp.pad(spot, ((0, up_to(steps, 8) - steps), (0, 0)))

    inputs = layer_input[0].astype(F32)
    gain_one = attention_gain.astype(F32)
    inverse_one = lax.rsqrt(jnp.mean(inputs * inputs, axis=1, keepdims=True) + EPS)
    normed = (inputs * inverse_one * gain_one).astype(BF16)
    bias = jnp.concatenate([query_bias, key_bias, value_bias]).astype(F32)
    pre = dot(normed, qkv_full) + bias
    cosine_table, sine_table = rotary_tables(positions, HD)
    cosine_table = cosine_table[:, None, :]
    sine_table = sine_table[:, None, :]
    pre = pre.reshape(rows, 3, heads_here, HD)
    queries = rotate(pre[:, 0], cosine_table, sine_table).astype(BF16).reshape(rows, wide)
    keys = rotate(pre[:, 1], cosine_table, sine_table).astype(BF16)
    values = pre[:, 2].astype(BF16)
    kv = spread(jnp.stack([keys, values], axis=2).reshape(rows, 2 * wide), "expert")
    heads_low, log_sums = attend(place, queries, kv, heads_here, score_scale)

    def rows_of(value, index):
        return rows_at(value, index * piece, piece)

    mine = [rows_of(heads_low, tensor_at)] + [
        shift(rows_of(heads_low, (tensor_at + k) % tensors), "tensor", k) for k in range(1, tensors)
    ]
    heads_rows = in_order(mine, [(tensor_at - k) % tensors for k in range(tensors)], 1)
    attended = dot_tt(heads_rows, output_full)
    inputs_own = rows_of(inputs, tensor_at)
    live_own = rows_of(live_rows, tensor_at)[:, None]
    residual = inputs_own + attended
    gain_two = mixture_gain.astype(F32)
    inverse_two = lax.rsqrt(jnp.mean(residual * residual, axis=1, keepdims=True) + EPS)
    mix_own = (residual * inverse_two * gain_two).astype(BF16)

    upstream_low = jnp.where(live_rows[:, None], cotangent[0], jnp.zeros((), BF16))
    upstream_blocks = spread(upstream_low, "expert")

    lin_grads, hiddens, smalls, mixes, ups, sums = [], [], [], [], [], []
    for k in range(tensors):
        at = (tensor_at + k) % tensors
        arrived = mix_own if k == 0 else shift(mix_own, "tensor", tensors - k)
        mix = jnp.concatenate(spread(arrived, "expert"), axis=0)
        up = jnp.concatenate([rows_of(u, at) for u in upstream_blocks], axis=0)
        kept_here = jnp.concatenate([rows_of(m, at) for m in kept_blocks], axis=0)
        hidden_grad = dot(up, down_weight)
        lin_grad, hidden, small, part = mixture_chunk(
            mix, hidden_grad, kept_here, spot, small_weight, lin_weight, experts, local
        )
        parts = [part[s * piece : (s + 1) * piece] for s in range(groups)]
        total = collect(parts, "expert")
        sums.append(total if k == 0 else shift(total, "tensor", k))
        lin_grads.append(lin_grad)
        hiddens.append(hidden)
        smalls.append(small)
        mixes.append(mix)
        ups.append(up)

    mix_grad = sum(s.astype(F32) for s in sums)
    scaled_two = mix_grad * gain_two
    mixture_gain_grad = jnp.sum(mix_grad * residual * inverse_two, axis=0)
    upstream_own = rows_of(upstream_low, tensor_at).astype(F32)
    residual_grad = (
        upstream_own
        + inverse_two * scaled_two
        - residual * inverse_two**3 * jnp.mean(scaled_two * residual, axis=1, keepdims=True)
    )
    attended_grad = residual_grad.astype(BF16)
    heads_grad_rows = dot(attended_grad, output_full).astype(BF16)

    def heads_of(index):
        return lax.dynamic_slice_in_dim(heads_grad_rows, index * wide, wide, axis=1)

    grads_in = [heads_of(tensor_at)] + [
        shift(heads_of((tensor_at + k) % tensors), "tensor", k) for k in range(1, tensors)
    ]
    heads_grad = in_order(grads_in, [(tensor_at - k) % tensors for k in range(tensors)], 0)
    query_grads, *kv_grads = attend_back(
        place, queries, heads_grad, heads_low, log_sums, kv, heads_here, score_scale
    )
    kv_sum = collect(kv_grads, "expert").astype(F32).reshape(rows, heads_here, 2, HD)
    query_pre_grad = rotate(query_grads.reshape(rows, heads_here, HD), cosine_table, -sine_table)
    key_pre_grad = rotate(kv_sum[:, :, 0], cosine_table, -sine_table)
    pre_grad = jnp.concatenate(
        [
            query_pre_grad.astype(BF16).reshape(rows, wide),
            key_pre_grad.astype(BF16).reshape(rows, wide),
            kv_sum[:, :, 1].astype(BF16).reshape(rows, wide),
        ],
        axis=1,
    )
    normed_part = dot_tt(pre_grad, qkv_full).astype(BF16)
    normed_rows = [rows_of(normed_part, tensor_at)] + [
        shift(rows_of(normed_part, (tensor_at + k) % tensors), "tensor", k)
        for k in range(1, tensors)
    ]
    normed_grad = sum(n.astype(F32) for n in normed_rows)
    inverse_own = rows_of(inverse_one, tensor_at)
    scaled_one = normed_grad * gain_one
    attention_gain_grad = jnp.sum(normed_grad * inputs_own * inverse_own, axis=0)
    input_grad = (
        residual_grad
        + inverse_own * scaled_one
        - inputs_own * inverse_own**3 * jnp.mean(scaled_one * inputs_own, axis=1, keepdims=True)
    )
    input_grad = gather_over_tensor(input_grad.astype(BF16)).astype(F32)

    lin_all = jnp.concatenate(lin_grads, axis=0)
    hidden_all = jnp.concatenate(hiddens, axis=0)
    small_all = jnp.concatenate(smalls, axis=0)
    mix_all = jnp.concatenate(mixes, axis=0)
    up_all = jnp.concatenate(ups, axis=0)
    down_grad = dot_nt(hidden_all, up_all).astype(BF16)
    lin_weight_grad = dot_nt(lin_all, mix_all).astype(BF16)
    small_grad = dot_nt(mix_all, small_all)[:, : experts + 1]

    def total_over_slots(part):
        whole = part.astype(F32)
        for k in range(1, slots):
            whole += shift(part, "dp", k).astype(F32)
        return whole

    expert_grads = [[], [], []]
    for j in range(local):
        first = j * pair
        found = (
            lin_weight_grad[first : first + expert_units],
            lin_weight_grad[first + width : first + width + expert_units],
            down_grad[j * width : j * width + expert_units],
        )
        for store, part in zip(expert_grads, found):
            store.append(total_over_slots(part).T)
    expert_grads = [jnp.stack(store) for store in expert_grads]

    first = local * pair
    shared_part = jnp.stack(
        [
            lin_weight_grad[first : first + shared_units],
            lin_weight_grad[first + width : first + width + shared_units],
            down_grad[local * width : local * width + shared_units],
        ]
    )
    half = depth // slots

    def half_of(index):
        return lax.dynamic_slice_in_dim(shared_part, index * half, half, axis=2)

    shared_sum = half_of(slot_at).astype(F32)
    for k in range(1, slots):
        shared_sum += shift(half_of((slot_at + k) % slots), "dp", k).astype(F32)
    shared_sum = shared_sum.astype(BF16)

    def owned_by(block):
        return lax.dynamic_slice_in_dim(shared_sum, block * own_rows, own_rows, axis=2)

    shared_back = [owned_by(block_at)] + [
        swap(owned_by(block_at ^ s), "expert", s) for s in range(1, groups)
    ]
    shared_grads = in_order(shared_back, [block_at ^ s for s in range(groups)], 1)
    shared_grads = shared_grads.astype(F32).transpose(0, 2, 1)

    attended_all = lax.all_gather(attended_grad, "tensor", axis=0, tiled=True)
    output_grad = lax.psum_scatter(
        dot_nt(attended_all, heads_low).astype(BF16), ("dp", "expert"), scatter_dimension=0, tiled=True
    ).astype(F32)
    qkv_grad = lax.psum_scatter(
        dot_nt(normed, pre_grad).astype(BF16), ("dp", "expert"), scatter_dimension=0, tiled=True
    ).astype(F32)

    mixture_sums = []
    for k in range(tensors):
        part = dot_tt(hiddens[k], down_weight).astype(BF16)
        parts = [part[s * piece : (s + 1) * piece] for s in range(groups)]
        total = collect(parts, "expert")
        mixture_sums.append(total if k == 0 else shift(total, "tensor", k))
    mixture = sum(s.astype(F32) for s in mixture_sums)
    output_own = jnp.where(live_own, residual + mixture, 0.0).astype(BF16)
    layer_output = gather_over_tensor(output_own)

    bias_grad = jnp.sum(pre_grad.astype(F32), axis=0)
    bias_place = lax.dynamic_update_slice_in_dim(
        jnp.zeros((tensors * 3 * wide,), F32), bias_grad, tensor_at * 3 * wide, axis=0
    )
    packed = jnp.concatenate(
        [attention_gain_grad, mixture_gain_grad, small_grad.T.reshape(-1), bias_place]
    )
    packed = lax.psum(packed, ("dp", "expert", "tensor"))
    small_total = packed[2 * depth : (3 + experts) * depth].reshape(experts + 1, depth)
    bias_total = lax.dynamic_slice_in_dim(
        packed, (3 + experts) * depth + tensor_at * 3 * wide, 3 * wide, axis=0
    )
    return (
        layer_output[None],
        input_grad[None],
        packed[:depth],
        qkv_grad[:, :wide],
        qkv_grad[:, wide : 2 * wide],
        qkv_grad[:, 2 * wide :],
        bias_total[:wide],
        bias_total[wide : 2 * wide],
        bias_total[2 * wide :],
        output_grad,
        packed[depth : 2 * depth],
        small_total[:experts].T,
        expert_grads[0],
        expert_grads[1],
        expert_grads[2],
        shared_grads[0],
        shared_grads[1],
        shared_grads[2],
        small_total[experts],
    )


def solution(mesh):
    dense = P(("dp", "expert"), "tensor")
    routed = P("expert", None, "tensor")
    rows = P("dp", "expert", None)
    in_specs = (
        rows, P(), dense, dense, dense, P("tensor"), P("tensor"), P("tensor"), dense, P(), P(),
        routed, routed, routed, dense, dense, dense, P(), P("dp"), rows, rows,
    )
    out_specs = (
        rows, rows, P(), dense, dense, dense, P("tensor"), P("tensor"), P("tensor"), dense, P(), P(),
        routed, routed, routed, dense, dense, dense, P(),
    )
    return jax.shard_map(shards, mesh=mesh, in_specs=in_specs, out_specs=out_specs, check_vma=False)
```

time: 2860 us -> 1150 us (0.40)
  waiting for transfers between devices: 1980 us -> 439 us
  matrix products: 293 us -> 123 us
  blocking collectives: 146 us -> 0 us
  Pallas kernels: 0 us -> 96.5 us
  starting transfers between devices: 22.9 us -> 118 us
  local copies, waits for them, and re-layouts: 276 us -> 234 us
    psum x5 -> x1, waiting for transfers between devices: 917 us -> 0.01 us  [shards(): packed = lax.psum(packed, ('dp', 'expert', 'tensor'))]
    reduce_scatter x9 -> x2, waiting for transfers between devices: 540 us -> 0.01 us  [the longest x1 0.01 us: shards(): lax.psum_scatter(dot_nt(attended_all, heads_low).astype(BF16), ('dp', 'ex...]
    ppermute x0 -> x89, waiting for transfers between devices: none -> 439 us  [the longest x35 311 us: shift(): lax.ppermute(value, axis, [(i, (i + by) % size) for i in range(size)])]
    all_to_all x3 -> x0, waiting for transfers between devices: 354 us -> none  [the longest x2 238 us: expert_trip(): lax.all_to_all(result, 'expert', split_axis=0, concat_axis=0, tiled=True)]
    dot_general x63 -> x18, matrix products: 293 us -> 123 us  [the longest x5 54.7 us: dot_nt(): lax.dot_general(a, b, (((0,), (0,)), ((), ())), preferred_element_type=F32)]
    all_gather x9 -> x3, waiting for transfers between devices: 160 us -> 0.04 us  [the longest x1 0.02 us: shards(): lax.all_gather(output_wide, ('dp', 'expert'), axis=0, tiled=True)]
    ppermute x0 -> x89, starting transfers between devices: none -> 117 us  [the longest x35 72 us: shift(): lax.ppermute(value, axis, [(i, (i + by) % size) for i in range(size)])]
    all_to_all x1 -> x0, blocking collectives: 96.9 us -> none  [expert_trip(): lax.all_to_all(payload, 'expert', split_axis=0, concat_axis=0, tiled=True)]
  transfers between devices with their start and end apart: 26 -> 95, of which waited for: 23 -> 30; matrix products, arithmetic and copies ran while one was open for 13% -> 39% of each run, Pallas kernels for 0% -> 9%
where the time goes in v1:
time: 1150 us; the launch traced here: 1140 us
  waiting for transfers between devices  439 us (38%)
  local copies, waits for them, and re-layouts  234 us (20%)
  matrix products  123 us (11%)
  starting transfers between devices  118 us (10%)
  other arithmetic  109 us (9%)
  Pallas kernels  96.5 us (8%)
  between operations  17.4 us (2%)
    ppermute x35, waiting for transfers between devices, shift(): lax.ppermute(value, axis, [(i, (i + by) % size) for i in range(size)])  311 us
    ppermute x54, waiting for transfers between devices, swap(): return lax.ppermute(value, axis, [(i, i ^ bit) for i in range(size)])  128 us
    unnamed x305, local copies, waits for them, and re-layouts  91.9 us
    pallas_call x4, Pallas kernels, mixture_chunk(): pl.pallas_call(functools.partial(mixture_kernel, experts=experts, local=l...  83.3 us
    ppermute x35, starting transfers between devices, shift(): lax.ppermute(value, axis, [(i, (i + by) % size) for i in range(size)])  72 us
    dot_general x5, matrix products, dot_nt(): lax.dot_general(a, b, (((0,), (0,)), ((), ())), preferred_element_type=F32)  54.7 us
    dynamic_update_slice x26, local copies, waits for them, and re-layouts, in_order(): whole = lax.dynamic_update_slice_in_dim(whole, piece, place * size, axis)  46.6 us
    ppermute x54, starting transfers between devices, swap(): return lax.ppermute(value, axis, [(i, i ^ bit) for i in range(size)])  45 us
  transfers between devices with their start and end apart: 95, of which 30 were waited for; matrix products, arithmetic and copies ran while one was open for 39% of the time, Pallas kernels for 9%

profile of v1, /device:TPU:0, one launch (start us, length us, event | category | flops | bytes accessed | tf_op | source)
XLA Modules:
  0.0 1135.3 jit_solution(5771617465989497757)
XLA Ops:
  73.6 8.3 collective-permute-done.17
  113.0 45.2 %collective-permute-done.13 = bf16[512,2048]{1,0:T(8,128)(2,1)} collective-permute-done((bf16[512,2048]{1,0:T(8,128)(2,1)}, bf16[512,2048]{1,0:T(8,128)(2,1)}, u32[]{:S(2)}, u32[]{:S(2)}) %collective-permute-start.13) | collective-permute-done | bytes 2097184 | tf_op jit(solution)/shard_map/ppermute | solution.py:48
  192.8 7.9 convolution_add_fusion
  224.4 14.9 %collective-permute-done.1.refs_2_ = bf16[512,1024]{1,0:T(8,128)(2,1)S(1)} collective-permute-done((bf16[512,1024]{1,0:T(8,128)(2,1)S(1)}, bf16[512,1024]{1,0:T(8,128)(2,1)S(1)}, u32[]{:S(2)}, u32[]{:S(2)}) %collective-permute-start.1) | collective-permute-done | bytes 1048608 | tf_op jit(solution)/shard_map/ppermute | solution.py:48
  277.5 10.7 collective-permute-start.10
  311.0 18.8 %collective-permute-done.25 = bf16[128,2048]{1,0:T(8,128)(2,1)} collective-permute-done((bf16[128,2048]{1,0:T(8,128)(2,1)S(1)}, bf16[128,2048]{1,0:T(8,128)(2,1)}, u32[]{:S(2)}, u32[]{:S(2)}) %collective-permute-start.25) | collective-permute-done | bytes 524320 | tf_op jit(solution)/shard_map/ppermute | solution.py:53
  336.7 20.9 %shard_map.349 = (bf16[512,2304]{1,0:T(8,128)(2,1)}, bf16[512,1152]{1,0:T(8,128)(2,1)}, bf16[512,128]{1,0:T(8,128)(2,1)}, bf16[512,2048]{1,0:T(8,128)(2,1)}) custom-call(bf16[512,2048]{1,0:T(8,128)(2,1)} %pad_maximum_fusion.5.mix_ref, f32[512,1152]{1,0:T(8,128)} %fusion.23.hidden_grad_ref, bf16[512,128]{1,0:T(8,128)(2,1)} %pad_maximum_fusion.20.kept_ref, ...), custom_call_target="tpu_custom_call" | custom-call | flops 9663676416 | bytes 20971520 | tf_op jit(solution)/shard_map/pallas_call | solution.py:309
  375.5 21.1 %shard_map.350 = (bf16[512,2304]{1,0:T(8,128)(2,1)}, bf16[512,1152]{1,0:T(8,128)(2,1)}, bf16[512,128]{1,0:T(8,128)(2,1)}, bf16[512,2048]{1,0:T(8,128)(2,1)}) custom-call(bf16[512,2048]{1,0:T(8,128)(2,1)} %pad_maximum_fusion.6.mix_ref, f32[512,1152]{1,0:T(8,128)} %fusion.31.hidden_grad_ref, bf16[512,128]{1,0:T(8,128)(2,1)} %pad_maximum_fusion.21.kept_ref, ...), custom_call_target="tpu_custom_call" | custom-call | flops 9663676416 | bytes 20971520 | tf_op jit(solution)/shard_map/pallas_call | solution.py:309
  402.9 20.6 %shard_map.351 = (bf16[512,2304]{1,0:T(8,128)(2,1)}, bf16[512,1152]{1,0:T(8,128)(2,1)}, bf16[512,128]{1,0:T(8,128)(2,1)}, bf16[512,2048]{1,0:T(8,128)(2,1)}) custom-call(bf16[512,2048]{1,0:T(8,128)(2,1)} %pad_maximum_fusion.7.mix_ref, f32[512,1152]{1,0:T(8,128)} %fusion.39.hidden_grad_ref, bf16[512,128]{1,0:T(8,128)(2,1)} %pad_maximum_fusion.22.kept_ref, ...), custom_call_target="tpu_custom_call" | custom-call | flops 9663676416 | bytes 20971520 | tf_op jit(solution)/shard_map/pallas_call | solution.py:309
  433.8 20.6 %shard_map.352 = (bf16[512,2304]{1,0:T(8,128)(2,1)}, bf16[512,1152]{1,0:T(8,128)(2,1)}, bf16[512,128]{1,0:T(8,128)(2,1)}, bf16[512,2048]{1,0:T(8,128)(2,1)}) custom-call(bf16[512,2048]{1,0:T(8,128)(2,1)} %pad_maximum_fusion.8.mix_ref, f32[512,1152]{1,0:T(8,128)} %fusion.47.hidden_grad_ref, bf16[512,128]{1,0:T(8,128)(2,1)} %pad_maximum_fusion.23.kept_ref, ...), custom_call_target="tpu_custom_call" | custom-call | flops 9663676416 | bytes 20971520 | tf_op jit(solution)/shard_map/pallas_call | solution.py:309
  460.2 14.1 %convolution_convert_fusion.2 = bf16[1152,2048]{1,0:T(8,128)(2,1)} fusion(bf16[2048,2048]{1,0:T(8,128)(2,1)} %get-tuple-element.69, bf16[512,1152]{1,0:T(8,128)(2,1)S(1)} %copy-done.117, bf16[512,1152]{1,0:T(8,128)(2,1)S(1)} %copy-done.113, bf16[512,1152]{1,0:T(8,128)(2,1)S(1)} %copy-done.116, bf16[512,1152]{1,0:T(8,128)(2,1)S(1)} %copy-done.115), kind=kOutput, calls=%fused_computation.17 | convolution fusion | flops 9684910080 | bytes 17825792 | tf_op jit(solution)/shard_map/dot_general | solution.py:106
  490.5 26.1 %convolution_convert_fusion = bf16[2304,2048]{1,0:T(8,128)(2,1)} fusion(bf16[2048,2048]{1,0:T(8,128)(2,1)} %constant_dynamic-update-slice_fusion, bf16[512,2304]{1,0:T(8,128)(2,1)} %get-tuple-element.64, bf16[512,2304]{1,0:T(8,128)(2,1)} %get-tuple-element.63, bf16[512,2304]{1,0:T(8,128)(2,1)S(1)} %copy-done.119, bf16[512,2304]{1,0:T(8,128)(2,1)S(1)} %copy-done.118), kind=kOutput, calls=%fused_computation.2 | convolution fusion | flops 19369820160 | bytes 27262976 | tf_op jit(solution)/shard_map/dot_general | solution.py:106
  523.5 12.3 %collective-permute-done.57 = bf16[128,2048]{1,0:T(8,128)(2,1)S(1)} collective-permute-done((bf16[128,2048]{1,0:T(8,128)(2,1)S(1)}, bf16[128,2048]{1,0:T(8,128)(2,1)S(1)}, u32[]{:S(2)}, u32[]{:S(2)}) %collective-permute-start.57) | collective-permute-done | bytes 524320 | tf_op jit(solution)/shard_map/ppermute | solution.py:48
  547.0 14.2 %collective-permute-start.58 = (bf16[128,2048]{1,0:T(8,128)(2,1)S(1)}, bf16[128,2048]{1,0:T(8,128)(2,1)S(1)}, u32[]{:S(2)}, u32[]{:S(2)}) collective-permute-start(bf16[128,2048]{1,0:T(8,128)(2,1)S(1)} %add_convert_fusion.10), channel_id=1, source_target_pairs={{0,1},{1,2},{2,3},{3,0},{4,5},{5,6},{6,7},{7,4},{8,9},{9,10},{10,1... | collective-permute-start | bytes 1572872 | tf_op jit(solution)/shard_map/ppermute | solution.py:53
  574.5 16.1 %collective-permute-done.62 = bf16[128,2048]{1,0:T(8,128)(2,1)S(1)} collective-permute-done((bf16[128,2048]{1,0:T(8,128)(2,1)S(1)}, bf16[128,2048]{1,0:T(8,128)(2,1)S(1)}, u32[]{:S(2)}, u32[]{:S(2)}) %collective-permute-start.62) | collective-permute-done | bytes 524320 | tf_op jit(solution)/shard_map/ppermute | solution.py:53
  627.4 8.3 shard_map.353
  642.0 8.3 collective-permute-start.72
  659.9 14.3 %collective-permute-done.72 = bf16[512,1024]{1,0:T(8,128)(2,1)} collective-permute-done((bf16[512,1024]{1,0:T(8,128)(2,1)}, bf16[512,1024]{1,0:T(8,128)(2,1)}, u32[]{:S(2)}, u32[]{:S(2)}) %collective-permute-start.72) | collective-permute-done | bytes 1048608 | tf_op jit(solution)/shard_map/ppermute | solution.py:48
  713.0 9.1 collective-permute-done.75
  722.2 23.2 %collective-permute-done.74 = bf16[128,2048]{1,0:T(8,128)(2,1)} collective-permute-done((bf16[128,2048]{1,0:T(8,128)(2,1)}, bf16[128,2048]{1,0:T(8,128)(2,1)}, u32[]{:S(2)}, u32[]{:S(2)}) %collective-permute-start.74) | collective-permute-done | bytes 524320 | tf_op jit(solution)/shard_map/ppermute | solution.py:53
  764.3 9.2 collective-permute-done.31
  807.3 20.0 %collective-permute-done.81 = bf16[352,2048]{1,0:T(8,128)(2,1)S(1)} collective-permute-done((bf16[352,2048]{1,0:T(8,128)(2,1)}, bf16[352,2048]{1,0:T(8,128)(2,1)S(1)}, u32[]{:S(2)}, u32[]{:S(2)}) %collective-permute-start.81) | collective-permute-done | bytes 1441824 | tf_op jit(solution)/shard_map/ppermute | solution.py:53
  827.3 31.3 %collective-permute-done.80 = bf16[352,2048]{1,0:T(8,128)(2,1)} collective-permute-done((bf16[352,2048]{1,0:T(8,128)(2,1)}, bf16[352,2048]{1,0:T(8,128)(2,1)}, u32[]{:S(2)}, u32[]{:S(2)}) %collective-permute-start.80) | collective-permute-done | bytes 1441824 | tf_op jit(solution)/shard_map/ppermute | solution.py:53
  859.1 30.4 %collective-permute-done.79 = bf16[352,2048]{1,0:T(8,128)(2,1)} collective-permute-done((bf16[352,2048]{1,0:T(8,128)(2,1)S(1)}, bf16[352,2048]{1,0:T(8,128)(2,1)}, u32[]{:S(2)}, u32[]{:S(2)}) %collective-permute-start.79) | collective-permute-done | bytes 1441824 | tf_op jit(solution)/shard_map/ppermute | solution.py:53
  890.7 9.0 add_bitcast_fusion.3
  899.6 29.2 %collective-permute-done.84 = bf16[352,2048]{1,0:T(8,128)(2,1)} collective-permute-done((bf16[352,2048]{1,0:T(8,128)(2,1)}, bf16[352,2048]{1,0:T(8,128)(2,1)}, u32[]{:S(2)}, u32[]{:S(2)}) %collective-permute-start.84) | collective-permute-done | bytes 1441824 | tf_op jit(solution)/shard_map/ppermute | solution.py:53
  929.7 37.6 %collective-permute-done.83 = bf16[352,2048]{1,0:T(8,128)(2,1)} collective-permute-done((bf16[352,2048]{1,0:T(8,128)(2,1)}, bf16[352,2048]{1,0:T(8,128)(2,1)}, u32[]{:S(2)}, u32[]{:S(2)}) %collective-permute-start.83) | collective-permute-done | bytes 1441824 | tf_op jit(solution)/shard_map/ppermute | solution.py:53
  974.1 10.2 collective-permute-done.40
  1003.6 26.6 %collective-permute-done.85 = bf16[3,352,1024]{2,1,0:T(8,128)(2,1)} collective-permute-done((bf16[3,352,1024]{2,1,0:T(8,128)(2,1)}, bf16[3,352,1024]{2,1,0:T(8,128)(2,1)}, u32[]{:S(2)}, u32[]{:S(2)}) %collective-permute-start.85) | collective-permute-done | bytes 2162720 | tf_op jit(solution)/shard_map/ppermute | solution.py:53
  1046.8 9.6 dynamic_update_slice.129
  1060.3 9.6 dynamic_update_slice.130
  1099.2 21.0 %collective-permute-done.77 = bf16[128,2048]{1,0:T(8,128)(2,1)} collective-permute-done((bf16[128,2048]{1,0:T(8,128)(2,1)S(1)}, bf16[128,2048]{1,0:T(8,128)(2,1)}, u32[]{:S(2)}, u32[]{:S(2)}) %collective-permute-start.77) | collective-permute-done | bytes 524320 | tf_op jit(solution)/shard_map/ppermute | solution.py:53
  (673 shorter events, 539.1 us)
Async XLA Ops:
  7.2 185.6 %all-gather.4.cloned.1.call-start = ((), (), s32[]{:S(2)}) async-start(), calls=%async_computation.2 | async-start | bytes 7077888 | tf_op jit(solution)/shard_map/all_gather | solution.py:393
  9.3 260.3 %all-gather.6.cloned.1.call-start = ((), (), s32[]{:S(2)}) async-start(), calls=%async_computation.3 | async-start | bytes 9437184 | tf_op jit(solution)/shard_map/all_gather | solution.py:399
  12.1 93.1 %collective-permute-start.20 = (bf16[512,128]{1,0:T(8,128)(2,1)}, bf16[512,128]{1,0:T(8,128)(2,1)}, u32[]{:S(2)}, u32[]{:S(2)}) collective-permute-start(bf16[512,128]{1,0:T(8,128)(2,1)} %pad_convert_fusion), channel_id=1, source_target_pairs={{0,8},{4,12},{8,0},{12,4},{1,9},{5,13},{9,1},{13,5},{2,10},{6,14},... | collective-permute-start | bytes 393224 | tf_op jit(solution)/shard_map/ppermute | solution.py:48
  15.0 91.4 %collective-permute-start.19 = (bf16[512,128]{1,0:T(8,128)(2,1)}, bf16[512,128]{1,0:T(8,128)(2,1)}, u32[]{:S(2)}, u32[]{:S(2)}) collective-permute-start(bf16[512,128]{1,0:T(8,128)(2,1)} %pad_convert_fusion), channel_id=1, source_target_pairs={{0,4},{4,0},{8,12},{12,8},{1,5},{5,1},{9,13},{13,9},{2,6},{6,2},{1... | collective-permute-start | bytes 393224 | tf_op jit(solution)/shard_map/ppermute | solution.py:48
  54.6 694.4 %all-gather.8.cloned.1.call-start = ((), (), s32[]{:S(2)}) async-start(), calls=%async_computation.6 | async-start | bytes 2621440 | tf_op jit(solution)/shard_map/all_gather | solution.py:602
  70.4 87.9 %collective-permute-start.13 = (bf16[512,2048]{1,0:T(8,128)(2,1)}, bf16[512,2048]{1,0:T(8,128)(2,1)}, u32[]{:S(2)}, u32[]{:S(2)}) collective-permute-start(bf16[512,2048]{1,0:T(8,128)(2,1)} %bitcast_select_fusion), channel_id=1, source_target_pairs={{0,8},{4,12},{8,0},{12,4},{1,9},{5,13},{9,1},{13,5},{2,10},{6,14},... | collective-permute-start | bytes 6291464 | tf_op jit(solution)/shard_map/ppermute | solution.py:48
  72.1 86.1 %collective-permute-start.12 = (bf16[512,2048]{1,0:T(8,128)(2,1)}, bf16[512,2048]{1,0:T(8,128)(2,1)}, u32[]{:S(2)}, u32[]{:S(2)}) collective-permute-start(bf16[512,2048]{1,0:T(8,128)(2,1)} %bitcast_select_fusion), channel_id=1, source_target_pairs={{0,4},{4,0},{8,12},{12,8},{1,5},{5,1},{9,13},{13,9},{2,6},{6,2},{1... | collective-permute-start | bytes 6291464 | tf_op jit(solution)/shard_map/ppermute | solution.py:48
  87.9 74.7 %collective-permute-start.18 = (bf16[3,1024,352]{1,2,0:T(8,128)(2,1)}, bf16[3,1024,352]{1,2,0:T(8,128)(2,1)}, u32[]{:S(2)}, u32[]{:S(2)}) collective-permute-start(bf16[3,1024,352]{1,2,0:T(8,128)(2,1)} %copy.154), channel_id=1, source_target_pairs={{0,16},{16,0},{1,17},{17,1},{2,18},{18,2},{3,19},{19,3},{4,20},{20... | collective-permute-start | bytes 6488072 | tf_op jit(solution)/shard_map/ppermute | solution.py:53
  311.0 87.8 %collective-permute-start.43 = (bf16[128,2048]{1,0:T(8,128)(2,1)}, bf16[128,2048]{1,0:T(8,128)(2,1)}, u32[]{:S(2)}, u32[]{:S(2)}) collective-permute-start(bf16[128,2048]{1,0:T(8,128)(2,1)} %collective-permute-done.41), channel_id=1, source_target_pairs={{0,8},{4,12},{8,0},{12,4},{1,9},{5,13},{9,1},{13,5},{2,10},{6,14},... | collective-permute-start | bytes 1572872 | tf_op jit(solution)/shard_map/ppermute | solution.py:48
  329.8 100.3 %collective-permute-start.42 = (bf16[128,2048]{1,0:T(8,128)(2,1)}, bf16[128,2048]{1,0:T(8,128)(2,1)}, u32[]{:S(2)}, u32[]{:S(2)}) collective-permute-start(bf16[128,2048]{1,0:T(8,128)(2,1)} %collective-permute-done.41), channel_id=1, source_target_pairs={{0,4},{4,0},{8,12},{12,8},{1,5},{5,1},{9,13},{13,9},{2,6},{6,2},{1... | collective-permute-start | bytes 1572872 | tf_op jit(solution)/shard_map/ppermute | solution.py:48
  371.7 202.2 %collective-permute-start.52 = (bf16[128,2048]{1,0:T(8,128)(2,1)}, bf16[128,2048]{1,0:T(8,128)(2,1)}, u32[]{:S(2)}, u32[]{:S(2)}) collective-permute-start(bf16[128,2048]{1,0:T(8,128)(2,1)} %get-tuple-element.153), channel_id=1, source_target_pairs={{0,4},{4,0},{8,12},{12,8},{1,5},{5,1},{9,13},{13,9},{2,6},{6,2},{1... | collective-permute-start | bytes 1572872 | tf_op jit(solution)/shard_map/ppermute | solution.py:48
  398.8 119.0 %collective-permute-start.53 = (bf16[128,2048]{1,0:T(8,128)(2,1)}, bf16[128,2048]{1,0:T(8,128)(2,1)}, u32[]{:S(2)}, u32[]{:S(2)}) collective-permute-start(bf16[128,2048]{1,0:T(8,128)(2,1)} %get-tuple-element.154), channel_id=1, source_target_pairs={{0,4},{4,0},{8,12},{12,8},{1,5},{5,1},{9,13},{13,9},{2,6},{6,2},{1... | collective-permute-start | bytes 1572872 | tf_op jit(solution)/shard_map/ppermute | solution.py:48
  399.4 124.0 %collective-permute-start.55 = (bf16[128,2048]{1,0:T(8,128)(2,1)}, bf16[128,2048]{1,0:T(8,128)(2,1)}, u32[]{:S(2)}, u32[]{:S(2)}) collective-permute-start(bf16[128,2048]{1,0:T(8,128)(2,1)} %get-tuple-element.155), channel_id=1, source_target_pairs={{0,4},{4,0},{8,12},{12,8},{1,5},{5,1},{9,13},{13,9},{2,6},{6,2},{1... | collective-permute-start | bytes 1572872 | tf_op jit(solution)/shard_map/ppermute | solution.py:48
  430.2 89.2 %collective-permute-start.56 = (bf16[128,2048]{1,0:T(8,128)(2,1)}, bf16[128,2048]{1,0:T(8,128)(2,1)}, u32[]{:S(2)}, u32[]{:S(2)}) collective-permute-start(bf16[128,2048]{1,0:T(8,128)(2,1)} %get-tuple-element.156), channel_id=1, source_target_pairs={{0,4},{4,0},{8,12},{12,8},{1,5},{5,1},{9,13},{13,9},{2,6},{6,2},{1... | collective-permute-start | bytes 1572872 | tf_op jit(solution)/shard_map/ppermute | solution.py:48
  430.2 108.1 %collective-permute-start.59 = (bf16[128,2048]{1,0:T(8,128)(2,1)}, bf16[128,2048]{1,0:T(8,128)(2,1)}, u32[]{:S(2)}, u32[]{:S(2)}) collective-permute-start(bf16[128,2048]{1,0:T(8,128)(2,1)} %get-tuple-element.157), channel_id=1, source_target_pairs={{0,4},{4,0},{8,12},{12,8},{1,5},{5,1},{9,13},{13,9},{2,6},{6,2},{1... | collective-permute-start | bytes 1572872 | tf_op jit(solution)/shard_map/ppermute | solution.py:48
  573.8 126.1 %collective-permute-start.23 = (bf16[128,2048]{1,0:T(8,128)(2,1)}, bf16[128,2048]{1,0:T(8,128)(2,1)}, u32[]{:S(2)}, u32[]{:S(2)}) collective-permute-start(bf16[128,2048]{1,0:T(8,128)(2,1)} %get-tuple-element.162), channel_id=1, source_target_pairs={{0,4},{4,0},{8,12},{12,8},{1,5},{5,1},{9,13},{13,9},{2,6},{6,2},{1... | collective-permute-start | bytes 1572872 | tf_op jit(solution)/shard_map/ppermute | solution.py:48
  573.9 187.4 %collective-permute-start.29 = (bf16[128,2048]{1,0:T(8,128)(2,1)}, bf16[128,2048]{1,0:T(8,128)(2,1)}, u32[]{:S(2)}, u32[]{:S(2)}) collective-permute-start(bf16[128,2048]{1,0:T(8,128)(2,1)} %get-tuple-element.163), channel_id=1, source_target_pairs={{0,4},{4,0},{8,12},{12,8},{1,5},{5,1},{9,13},{13,9},{2,6},{6,2},{1... | collective-permute-start | bytes 1572872 | tf_op jit(solution)/shard_map/ppermute | solution.py:48
  574.4 182.5 %collective-permute-start.30 = (bf16[128,2048]{1,0:T(8,128)(2,1)}, bf16[128,2048]{1,0:T(8,128)(2,1)}, u32[]{:S(2)}, u32[]{:S(2)}) collective-permute-start(bf16[128,2048]{1,0:T(8,128)(2,1)} %get-tuple-element.164), channel_id=1, source_target_pairs={{0,4},{4,0},{8,12},{12,8},{1,5},{5,1},{9,13},{13,9},{2,6},{6,2},{1... | collective-permute-start | bytes 1572872 | tf_op jit(solution)/shard_map/ppermute | solution.py:48
  654.9 432.4 %all-reduce.14.cloned.1.call-start = ((), (), s32[]{:S(2)}) async-start(), calls=%async_computation.4 | async-start | bytes 229376 | tf_op jit(solution)/shard_map/psum | solution.py:627
  699.9 45.4 %collective-permute-start.74 = (bf16[128,2048]{1,0:T(8,128)(2,1)}, bf16[128,2048]{1,0:T(8,128)(2,1)}, u32[]{:S(2)}, u32[]{:S(2)}) collective-permute-start(bf16[128,2048]{1,0:T(8,128)(2,1)} %get-tuple-element.152), channel_id=1, source_target_pairs={{0,2},{1,3},{2,0},{3,1},{4,6},{5,7},{6,4},{7,5},{8,10},{9,11},{10,... | collective-permute-start | bytes 1572872 | tf_op jit(solution)/shard_map/ppermute | solution.py:53
  713.0 64.0 %collective-permute-start.45 = (bf16[128,2048]{1,0:T(8,128)(2,1)}, bf16[128,2048]{1,0:T(8,128)(2,1)}, u32[]{:S(2)}, u32[]{:S(2)}) collective-permute-start(bf16[128,2048]{1,0:T(8,128)(2,1)} %get-tuple-element.167), channel_id=1, source_target_pairs={{0,4},{4,0},{8,12},{12,8},{1,5},{5,1},{9,13},{13,9},{2,6},{6,2},{1... | collective-permute-start | bytes 1572872 | tf_op jit(solution)/shard_map/ppermute | solution.py:48
  748.9 375.0 %reduce-scatter.5.cloned.1.call-start = ((), (), s32[]{:S(2)}) async-start(), calls=%async_computation.7 | async-start | bytes 2359296 | tf_op jit(solution)/shard_map/reduce_scatter | solution.py:603
  753.2 372.5 %reduce-scatter.3.cloned.1.call-start = ((), (), s32[]{:S(2)}) async-start(), calls=%async_computation.5 | async-start | bytes 7077888 | tf_op jit(solution)/shard_map/reduce_scatter | solution.py:606
  777.0 50.2 %collective-permute-start.81 = (bf16[352,2048]{1,0:T(8,128)(2,1)}, bf16[352,2048]{1,0:T(8,128)(2,1)S(1)}, u32[]{:S(2)}, u32[]{:S(2)}) collective-permute-start(bf16[352,2048]{1,0:T(8,128)(2,1)} %get-tuple-element.115), channel_id=1, source_target_pairs={{0,16},{16,0},{1,17},{17,1},{2,18},{18,2},{3,19},{19,3},{4,20},{20... | collective-permute-start | bytes 4325384 | tf_op jit(solution)/shard_map/ppermute | solution.py:53
  778.2 80.4 %collective-permute-start.80 = (bf16[352,2048]{1,0:T(8,128)(2,1)}, bf16[352,2048]{1,0:T(8,128)(2,1)}, u32[]{:S(2)}, u32[]{:S(2)}) collective-permute-start(bf16[352,2048]{1,0:T(8,128)(2,1)} %get-tuple-element.116), channel_id=1, source_target_pairs={{0,16},{16,0},{1,17},{17,1},{2,18},{18,2},{3,19},{19,3},{4,20},{20... | collective-permute-start | bytes 4325384 | tf_op jit(solution)/shard_map/ppermute | solution.py:53
  784.9 104.6 %collective-permute-start.79 = (bf16[352,2048]{1,0:T(8,128)(2,1)S(1)}, bf16[352,2048]{1,0:T(8,128)(2,1)}, u32[]{:S(2)}, u32[]{:S(2)}) collective-permute-start(bf16[352,2048]{1,0:T(8,128)(2,1)S(1)} %copy-done.63), channel_id=1, source_target_pairs={{0,16},{16,0},{1,17},{17,1},{2,18},{18,2},{3,19},{19,3},{4,20},{20... | collective-permute-start | bytes 4325384 | tf_op jit(solution)/shard_map/ppermute | solution.py:53
  795.2 133.6 %collective-permute-start.84 = (bf16[352,2048]{1,0:T(8,128)(2,1)}, bf16[352,2048]{1,0:T(8,128)(2,1)}, u32[]{:S(2)}, u32[]{:S(2)}) collective-permute-start(bf16[352,2048]{1,0:T(8,128)(2,1)} %get-tuple-element.123), channel_id=1, source_target_pairs={{0,16},{16,0},{1,17},{17,1},{2,18},{18,2},{3,19},{19,3},{4,20},{20... | collective-permute-start | bytes 4325384 | tf_op jit(solution)/shard_map/ppermute | solution.py:53
  797.5 169.8 %collective-permute-start.83 = (bf16[352,2048]{1,0:T(8,128)(2,1)}, bf16[352,2048]{1,0:T(8,128)(2,1)}, u32[]{:S(2)}, u32[]{:S(2)}) collective-permute-start(bf16[352,2048]{1,0:T(8,128)(2,1)} %get-tuple-element.124), channel_id=1, source_target_pairs={{0,16},{16,0},{1,17},{17,1},{2,18},{18,2},{3,19},{19,3},{4,20},{20... | collective-permute-start | bytes 4325384 | tf_op jit(solution)/shard_map/ppermute | solution.py:53
  827.3 72.3 %collective-permute-start.22 = (bf16[128,2048]{1,0:T(8,128)(2,1)}, bf16[128,2048]{1,0:T(8,128)(2,1)}, u32[]{:S(2)}, u32[]{:S(2)}) collective-permute-start(bf16[128,2048]{1,0:T(8,128)(2,1)} %get-tuple-element.161), channel_id=1, source_target_pairs={{0,4},{4,0},{8,12},{12,8},{1,5},{5,1},{9,13},{13,9},{2,6},{6,2},{1... | collective-permute-start | bytes 1572872 | tf_op jit(solution)/shard_map/ppermute | solution.py:48
  858.6 115.5 %collective-permute-start.24 = (bf16[128,2048]{1,0:T(8,128)(2,1)}, bf16[128,2048]{1,0:T(8,128)(2,1)}, u32[]{:S(2)}, u32[]{:S(2)}) collective-permute-start(bf16[128,2048]{1,0:T(8,128)(2,1)} %add_convert_fusion.26), channel_id=1, source_target_pairs={{0,8},{4,12},{8,0},{12,4},{1,9},{5,13},{9,1},{13,5},{2,10},{6,14},... | collective-permute-start | bytes 1572872 | tf_op jit(solution)/shard_map/ppermute | solution.py:48
  889.5 140.6 %collective-permute-start.85 = (bf16[3,352,1024]{2,1,0:T(8,128)(2,1)}, bf16[3,352,1024]{2,1,0:T(8,128)(2,1)}, u32[]{:S(2)}, u32[]{:S(2)}) collective-permute-start(bf16[3,352,1024]{2,1,0:T(8,128)(2,1)} %constant_dynamic-slice_fusion.4), channel_id=1, source_target_pairs={{0,16},{16,0},{1,17},{17,1},{2,18},{18,2},{3,19},{19,3},{4,20},{20... | collective-permute-start | bytes 6488072 | tf_op jit(solution)/shard_map/ppermute | solution.py:53
  899.6 74.5 %collective-permute-start.32 = (bf16[128,2048]{1,0:T(8,128)(2,1)}, bf16[128,2048]{1,0:T(8,128)(2,1)S(1)}, u32[]{:S(2)}, u32[]{:S(2)}) collective-permute-start(bf16[128,2048]{1,0:T(8,128)(2,1)} %add_convert_fusion.22), channel_id=1, source_target_pairs={{0,1},{1,2},{2,3},{3,0},{4,5},{5,6},{6,7},{7,4},{8,9},{9,10},{10,1... | collective-permute-start | bytes 1572872 | tf_op jit(solution)/shard_map/ppermute | solution.py:53
  (194 other events, 3698.2 us)
Sparse Core Ops, SparseCore 0:
  9.9 51.5 all-gather.3
  63.4 90.4 all-gather.5
  655.0 45.4 all-gather.7
  749.0 119.6 all-reduce.13
  871.8 50.5 reduce-scatter.4
  926.0 87.0 reduce-scatter.2

commit v2 on v1

v2 whole, which is shorter than its diff:
```python
import functools

import jax
import jax.numpy as jnp
from jax import lax
from jax.experimental import pallas as pl
from jax.experimental.pallas import tpu as pltpu
from jax.sharding import PartitionSpec as P

HD = 128
TOP = 4
LANES = 128

EPS = 1e-06
ROPE_BASE = 1000000.0
NEGATIVE = -1e30
F32 = jnp.float32
QUICK = pl.CostEstimate(flops=0, bytes_accessed=1 << 20, transcendentals=0)
BF16 = jnp.bfloat16


def up_to(value, multiple):
    return -(-value // multiple) * multiple


def rotary_tables(positions, head_size):
    half_size = head_size // 2
    exponent = 2.0 * jnp.arange(half_size, dtype=F32) / head_size
    inverse = ROPE_BASE ** (-exponent)
    angles = positions.astype(F32)[:, None] * inverse[None, :]
    cosine_half = jnp.cos(angles)
    sine_half = jnp.sin(angles)
    return (
        jnp.concatenate([cosine_half, cosine_half], axis=1),
        jnp.concatenate([-sine_half, sine_half], axis=1),
    )


class Links:
    def __init__(self):
        self.last = {}

    def send(self, link, values, axis, perms):
        before = None if link == "core" else self.last.get(link)
        if before is not None:
            tied = lax.optimization_barrier((tuple(values), before))
            values = tied[0]
        with jax.named_scope("over_" + link):
            arrived = tuple(lax.ppermute(v, axis, p) for v, p in zip(values, perms))
        self.last[link] = arrived
        return list(arrived)

    def swap(self, value, axis, bit):
        link = "x" if axis == "dp" else "core" if bit == 1 else "y"
        size = lax.axis_size(axis)
        return self.send(link, [value], axis, [[(i, i ^ bit) for i in range(size)]])[0]

    def swaps(self, values, axis):
        size = lax.axis_size(axis)
        perms = [[(i, i ^ s) for i in range(size)] for s in range(1, size)]
        return self.send("y", values, axis, perms)

    def shift(self, value, axis, by):
        size = lax.axis_size(axis)
        perm = [(i, (i + by) % size) for i in range(size)]
        return self.send("x" if axis == "dp" else "z", [value], axis, [perm])[0]

    def shifts(self, values, axis, direction=1):
        link = "x" if axis == "dp" else "z"
        size = lax.axis_size(axis)
        perms = [[(i, (i + direction * k) % size) for i in range(size)] for k in range(1, size)]
        return self.send(link, values, axis, perms[: len(values)])

    def spread(self, value, axis, low=1):
        bit = lax.axis_size(axis) // 2
        while bit >= low:
            value = jnp.concatenate([value, self.swap(value, axis, bit)], axis=0)
            bit //= 2
        return value

    def meet(self, near, far, axis, bit):
        arrived = self.swap(far, axis, bit)
        return (near.astype(F32) + arrived.astype(F32)).astype(near.dtype)

    def scatter(self, value, axis, wait):
        at = lax.axis_index(axis)
        bit = 1
        while value.shape[0] > 1:
            value = value.reshape(value.shape[0] // 2, 2, *value.shape[1:])
            own = lax.rem(at // bit, 2)
            near, far = (
                lax.dynamic_index_in_dim(value, i, axis=1, keepdims=False) for i in (own, 1 - own)
            )
            value = self.meet(near, far, axis, bit)
            if bit == 1:
                value = after(value, wait)
            bit *= 2
        return value[0]

    def collect(self, near, far, axis, low=1):
        bit = low
        while True:
            arrived = self.swap(far, axis, bit)
            near = (near.astype(F32) + arrived.astype(F32)).astype(near.dtype)
            bit *= 2
            if bit >= lax.axis_size(axis):
                return near
            half = near.shape[0] // 2
            near, far = near[:half], near[half:]


def sum_over_all(value, axes):
    for axis in axes:
        size = lax.axis_size(axis)
        bit = 1
        while bit < size:
            value = value + lax.ppermute(value, axis, [(i, i ^ bit) for i in range(size)])
            bit *= 2
    return value


def reversed_order(size):
    order, bit = [0], size // 2
    while bit:
        order = order + [i ^ bit for i in order]
        bit //= 2
    return order


def after(value, *others):
    return lax.optimization_barrier((value, others))[0]


def together(*values):
    return lax.optimization_barrier(values)


def rows_at(value, start, size):
    return lax.dynamic_slice_in_dim(value, start, size, axis=0)


def in_order(pieces, index, axis):
    size = pieces[0].shape[axis]
    shape = list(pieces[0].shape)
    shape[axis] = size * len(pieces)
    whole = jnp.zeros(shape, pieces[0].dtype)
    for piece, place in zip(pieces, index):
        whole = lax.dynamic_update_slice_in_dim(whole, piece, place * size, axis)
    return whole


def dot_tt(a, b):
    return lax.dot_general(a, b, (((1,), (1,)), ((), ())), preferred_element_type=F32)


def dot_nt(a, b):
    return lax.dot_general(a, b, (((0,), (0,)), ((), ())), preferred_element_type=F32)


def dot(a, b):
    return jnp.dot(a, b, preferred_element_type=F32)


def project_kernel(
    rows_ref, wq_ref, wk_ref, wv_ref, bq_ref, bk_ref, bv_ref, cosine_ref, sine_ref, q_ref, kv_ref
):
    source = rows_ref[...]
    cosine, sine = cosine_ref[...], sine_ref[...]

    def turned(value):
        return value * cosine + pltpu.roll(value, HD // 2, 1) * sine

    query = dot(source, wq_ref[...]) + bq_ref[...].astype(F32)
    key = dot(source, wk_ref[...]) + bk_ref[...].astype(F32)
    value = dot(source, wv_ref[...]) + bv_ref[...].astype(F32)
    for i in range(q_ref.shape[1] // HD):
        here = slice(i * HD, (i + 1) * HD)
        q_ref[:, here] = turned(query[:, here]).astype(BF16)
        kv_ref[:, 2 * i * HD : (2 * i + 1) * HD] = turned(key[:, here]).astype(BF16)
        kv_ref[:, (2 * i + 1) * HD : (2 * i + 2) * HD] = value[:, here].astype(BF16)


def project(source, weight, bias, cosine, sine):
    rows, depth = source.shape
    wide = weight.shape[1] // 3
    block = 2 * HD
    steps = wide // block
    whole = lambda shape: pl.BlockSpec(shape, lambda h: (0, 0))
    third = lambda size, i: pl.BlockSpec((size, block), lambda h: (0, i * steps + h))
    return pl.pallas_call(
        project_kernel,
        grid=(steps,),
        in_specs=[whole((rows, depth))]
        + [third(depth, i) for i in range(3)]
        + [third(1, i) for i in range(3)]
        + [whole((rows, HD))] * 2,
        out_specs=[
            pl.BlockSpec((rows, block), lambda h: (0, h)),
            pl.BlockSpec((rows, 2 * block), lambda h: (0, h)),
        ],
        out_shape=[
            jax.ShapeDtypeStruct((rows, wide), BF16),
            jax.ShapeDtypeStruct((rows, 2 * wide), BF16),
        ],
        compiler_params=pltpu.CompilerParams(vmem_limit_bytes=40 << 20),
        cost_estimate=QUICK,
    )(source, weight, weight, weight, bias, bias, bias, cosine, sine)


def turn_back_kernel(dq_ref, dkv_ref, cosine_ref, sine_ref, out_ref, sum_ref):
    cosine, sine = cosine_ref[...], sine_ref[...]
    wide = dq_ref.shape[1]

    def turned(value):
        return value * cosine - pltpu.roll(value, HD // 2, 1) * sine

    def store(at, value):
        low = value.astype(BF16)
        out_ref[:, at : at + HD] = low
        sum_ref[:, at : at + HD] = jnp.sum(low.astype(F32), axis=0, keepdims=True)

    for i in range(wide // HD):
        at = i * HD
        store(at, turned(dq_ref[:, at : at + HD]))
        here, there = slice(2 * at, 2 * at + HD), slice(2 * at + HD, 2 * at + 2 * HD)
        store(wide + at, turned(dkv_ref[:, here].astype(F32)))
        store(2 * wide + at, dkv_ref[:, there].astype(F32))


def turn_back(query_grads, kv_grads, cosine, sine):
    rows, wide = query_grads.shape
    return pl.pallas_call(
        turn_back_kernel,
        out_shape=[
            jax.ShapeDtypeStruct((rows, 3 * wide), BF16),
            jax.ShapeDtypeStruct((1, 3 * wide), F32),
        ],
        compiler_params=pltpu.CompilerParams(vmem_limit_bytes=40 << 20),
        cost_estimate=QUICK,
    )(query_grads, kv_grads, cosine, sine)


def attend_kernel(place_ref, q_ref, kv_ref, out_ref, log_ref, peak, total, mix, *, groups, score_scale):
    me, length = place_ref[0], place_ref[1]
    rows = q_ref.shape[0]
    query = q_ref[...]
    peak[...] = jnp.full_like(peak, NEGATIVE)
    total[...] = jnp.zeros_like(total)
    mix[...] = jnp.zeros_like(mix)

    def block(j, last):
        here = slice(j * rows, (j + 1) * rows)
        key, value = kv_ref[here, :HD], kv_ref[here, HD:]
        scores = dot_tt(query, key) * score_scale
        column = lax.broadcasted_iota(jnp.int32, (rows, rows), 1)
        good = column < length - j * rows
        if last:
            good &= column <= lax.broadcasted_iota(jnp.int32, (rows, rows), 0)
        scores = jnp.where(good, scores, NEGATIVE)
        new_peak = jnp.maximum(peak[...], jnp.max(scores, axis=1, keepdims=True))
        keep = jnp.exp(peak[...] - new_peak)
        lifted = jnp.exp(scores - new_peak)
        peak[...] = new_peak
        total[...] = total[...] * keep + jnp.sum(lifted, axis=1, keepdims=True)
        mix[...] = mix[...] * keep + dot(lifted.astype(BF16), value)

    for j in range(groups):
        alive = j * rows < length
        pl.when((j < me) & alive)(functools.partial(block, j, False))
        pl.when((j == me) & alive)(functools.partial(block, j, True))
    out_ref[...] = (mix[...] / total[...]).astype(BF16)
    log_ref[0] = peak[...] + jnp.log(total[...])


def attend(place, query, kv, heads, score_scale):
    rows = query.shape[0]
    groups = kv.shape[0] // rows
    spec = pltpu.PrefetchScalarGridSpec(
        num_scalar_prefetch=1,
        grid=(heads,),
        in_specs=[
            pl.BlockSpec((rows, HD), lambda h, p: (0, h)),
            pl.BlockSpec((groups * rows, 2 * HD), lambda h, p: (0, h)),
        ],
        out_specs=[
            pl.BlockSpec((rows, HD), lambda h, p: (0, h)),
            pl.BlockSpec((1, rows, 1), lambda h, p: (h, 0, 0)),
        ],
        scratch_shapes=[
            pltpu.VMEM((rows, 1), F32),
            pltpu.VMEM((rows, 1), F32),
            pltpu.VMEM((rows, HD), F32),
        ],
    )
    work = heads * rows * rows * groups
    return pl.pallas_call(
        functools.partial(attend_kernel, groups=groups, score_scale=score_scale),
        grid_spec=spec,
        out_shape=[
            jax.ShapeDtypeStruct((rows, heads * HD), BF16),
            jax.ShapeDtypeStruct((heads, rows, 1), F32),
        ],
        compiler_params=pltpu.CompilerParams(vmem_limit_bytes=40 << 20),
        cost_estimate=QUICK,
    )(place, query, kv)


def attend_back_kernel(
    place_ref, q_ref, g_ref, o_ref, log_ref, kv_ref, dq_ref, dkv_ref, total, *, groups, score_scale
):
    me, length = place_ref[0], place_ref[1]
    rows = q_ref.shape[0]
    query, grad = q_ref[...], g_ref[...]
    log_sum = log_ref[0]
    centre = jnp.sum(grad.astype(F32) * o_ref[...].astype(F32), axis=1, keepdims=True)
    total[...] = jnp.zeros_like(total)

    def block(j, last):
        here = slice(j * rows, (j + 1) * rows)
        key, value = kv_ref[here, :HD], kv_ref[here, HD:]
        scores = dot_tt(query, key) * score_scale
        column = lax.broadcasted_iota(jnp.int32, (rows, rows), 1)
        good = column < length - j * rows
        if last:
            good &= column <= lax.broadcasted_iota(jnp.int32, (rows, rows), 0)
        weights = jnp.exp(jnp.where(good, scores, NEGATIVE) - log_sum)
        weight_grad = dot_tt(grad, value)
        score_grad = (weights * (weight_grad - centre)).astype(BF16)
        total[...] += dot(score_grad, key)
        dkv_ref[here, :HD] = (dot_nt(score_grad, query) * score_scale).astype(BF16)
        dkv_ref[here, HD:] = dot_nt(weights.astype(BF16), grad).astype(BF16)

    def nothing(j):
        dkv_ref[j * rows : (j + 1) * rows, :] = jnp.zeros((rows, 2 * HD), BF16)

    for j in range(groups):
        alive = j * rows < length
        pl.when((j < me) & alive)(functools.partial(block, j, False))
        pl.when((j == me) & alive)(functools.partial(block, j, True))
        pl.when((j > me) | jnp.logical_not(alive))(functools.partial(nothing, j))
    dq_ref[...] = total[...] * score_scale


def attend_back(place, query, grad, out, log_sums, kv, heads, score_scale):
    rows = query.shape[0]
    groups = kv.shape[0] // rows
    head = pl.BlockSpec((rows, HD), lambda h, p: (0, h))
    pair = pl.BlockSpec((groups * rows, 2 * HD), lambda h, p: (0, h))
    spec = pltpu.PrefetchScalarGridSpec(
        num_scalar_prefetch=1,
        grid=(heads,),
        in_specs=[head, head, head, pl.BlockSpec((1, rows, 1), lambda h, p: (h, 0, 0)), pair],
        out_specs=[head, pair],
        scratch_shapes=[pltpu.VMEM((rows, HD), F32)],
    )
    work = heads * rows * rows * groups
    return pl.pallas_call(
        functools.partial(attend_back_kernel, groups=groups, score_scale=score_scale),
        grid_spec=spec,
        out_shape=[
            jax.ShapeDtypeStruct((rows, heads * HD), F32),
            jax.ShapeDtypeStruct((groups * rows, 2 * heads * HD), BF16),
        ],
        compiler_params=pltpu.CompilerParams(vmem_limit_bytes=48 << 20),
        cost_estimate=QUICK,
    )(place, query, grad, out, log_sums, kv)


def side_by_side_kernel(place_ref, *refs, groups):
    pieces, stack, outs = refs[:groups], refs[-1], refs[groups:-1]
    units = pieces[0].shape[1]
    for s in range(groups):
        stack[s] = pieces[s][...]
    for j in range(groups):
        found = stack[place_ref[0] ^ j]
        for i, out in enumerate(outs):
            out[:, j * units : (j + 1) * units] = found[i].astype(F32).T


def side_by_side(place, pieces):
    count, units, rows = pieces[0].shape
    groups = len(pieces)
    return pl.pallas_call(
        functools.partial(side_by_side_kernel, groups=groups),
        grid_spec=pltpu.PrefetchScalarGridSpec(
            num_scalar_prefetch=1,
            in_specs=[pl.BlockSpec(memory_space=pltpu.VMEM)] * groups,
            out_specs=[pl.BlockSpec(memory_space=pltpu.VMEM)] * count,
            scratch_shapes=[pltpu.VMEM((groups, count, units, rows), BF16)],
        ),
        out_shape=[jax.ShapeDtypeStruct((rows, groups * units), F32)] * count,
        compiler_params=pltpu.CompilerParams(vmem_limit_bytes=40 << 20),
    )(place, *pieces)


def mixture_kernel(
    mix_ref, hidden_grad_ref, kept_ref, spot_ref, router_ref, weight_ref,
    lin_grad_ref, hidden_ref, small_ref, part_ref,
    total, probs_ref, logits_ref, gate_grad_ref, *, experts, local,
):
    step = pl.program_id(1)
    width = hidden_ref.shape[1]
    mix = mix_ref[...]
    lane = lax.broadcasted_iota(jnp.int32, kept_ref.shape, 1)

    @pl.when(step == 0)
    def _():
        logits = dot_tt(mix, router_ref[...])
        logits_ref[...] = logits
        masked = jnp.where(lane < experts, logits, NEGATIVE)
        lifted = jnp.exp(masked - jnp.max(masked, axis=1, keepdims=True))
        probs_ref[...] = lifted / jnp.sum(lifted, axis=1, keepdims=True)
        gate_grad_ref[...] = jnp.zeros_like(gate_grad_ref)
        total[...] = jnp.zeros_like(total)

    spot = spot_ref[pl.ds(step, 1), :]
    kept = kept_ref[...].astype(F32)
    gate = jnp.sum(probs_ref[...] * kept * spot, axis=1, keepdims=True)
    switch = jax.nn.sigmoid(jnp.sum(logits_ref[...] * spot, axis=1, keepdims=True))
    routed = step < local
    scale = jnp.where(routed, gate, switch)
    weight = weight_ref[...]
    lin = dot_tt(mix, weight)
    gate_lin, up_lin = lin[:, :width], lin[:, width:]
    logistic = jax.nn.sigmoid(gate_lin)
    silu = gate_lin * logistic
    hidden = silu * up_lin
    hidden_grad = hidden_grad_ref[...]
    row_sum = jnp.sum(hidden * hidden_grad, axis=1, keepdims=True)
    factor = jnp.where(routed, jnp.sum(kept * spot, axis=1, keepdims=True), switch * (1.0 - switch))
    gate_grad_ref[...] += row_sum * factor * spot
    hidden_ref[...] = (scale * hidden).astype(BF16)
    scaled = scale * hidden_grad
    lin_grad_ref[:, :width] = (
        scaled * up_lin * logistic * (1.0 + gate_lin * (1.0 - logistic))
    ).astype(BF16)
    lin_grad_ref[:, width:] = (scaled * silu).astype(BF16)
    total[...] += dot(lin_grad_ref[...], weight)

    @pl.when(step == local)
    def _():
        grads = gate_grad_ref[...]
        probs = probs_ref[...]
        routed_grads = jnp.where(lane < experts, grads, 0.0)
        inner = jnp.sum(probs * routed_grads, axis=1, keepdims=True)
        small = jnp.where(lane < experts, probs * (grads - inner), grads).astype(BF16)
        small_ref[...] = small
        part_ref[...] = (total[...] + dot(small, router_ref[...])).astype(BF16)


def mixture(mix, hidden_grad, kept, spot, router, weight, rows, experts, local):
    tokens, depth = mix.shape
    steps = local + 1
    pair = weight.shape[0] // steps
    width = pair // 2
    whole = lambda shape: pl.BlockSpec(shape, lambda i, j: (0, 0))
    by_row = lambda size: pl.BlockSpec((rows, size), lambda i, j: (i, 0))
    by_both = lambda size: pl.BlockSpec((rows, size), lambda i, j: (i, j))
    return pl.pallas_call(
        functools.partial(mixture_kernel, experts=experts, local=local),
        grid=(tokens // rows, steps),
        in_specs=[
            by_row(depth),
            by_both(width),
            by_row(LANES),
            whole(spot.shape),
            whole((LANES, depth)),
            pl.BlockSpec((pair, depth), lambda i, j: (j, 0)),
        ],
        out_specs=[by_both(pair), by_both(width), by_row(LANES), by_row(depth)],
        out_shape=[
            jax.ShapeDtypeStruct((tokens, steps * pair), BF16),
            jax.ShapeDtypeStruct((tokens, steps * width), BF16),
            jax.ShapeDtypeStruct((tokens, LANES), BF16),
            jax.ShapeDtypeStruct((tokens, depth), BF16),
        ],
        scratch_shapes=[
            pltpu.VMEM((rows, depth), F32),
            pltpu.VMEM((rows, LANES), F32),
            pltpu.VMEM((rows, LANES), F32),
            pltpu.VMEM((rows, LANES), F32),
        ],
        compiler_params=pltpu.CompilerParams(vmem_limit_bytes=56 << 20),
        cost_estimate=pl.CostEstimate(
            flops=5 * tokens * depth * steps * pair, bytes_accessed=80 << 20, transcendentals=0
        ),
    )(mix, hidden_grad, kept, spot, router, weight)


def shards(
    layer_input,
    attention_gain,
    query_weight,
    key_weight,
    value_weight,
    query_bias,
    key_bias,
    value_bias,
    output_weight,
    mixture_gain,
    router_weight,
    expert_gate,
    expert_up,
    expert_down,
    shared_gate,
    shared_up,
    shared_down,
    shared_switch,
    slot_lengths,
    routes,
    cotangent,
):
    rows, depth = layer_input.shape[1:]
    groups = lax.axis_size("expert")
    tensors = lax.axis_size("tensor")
    slots = lax.axis_size("dp")
    slot_at = lax.axis_index("dp")
    block_at = lax.axis_index("expert")
    tensor_at = lax.axis_index("tensor")
    experts = router_weight.shape[1]
    local, _, expert_units = expert_gate.shape
    shared_units = shared_gate.shape[1] // groups
    capacity = rows * TOP // experts
    score_scale = HD ** (-0.5)
    heads_here = query_weight.shape[1] // HD
    wide = heads_here * HD
    piece = rows // tensors
    width = up_to(max(expert_units, shared_units), LANES)
    pair = 2 * width
    steps = local + 1
    length = slot_lengths[0]
    positions = block_at * rows + jnp.arange(rows, dtype=jnp.int32)
    live_rows = positions < length
    place = jnp.stack([block_at.astype(jnp.int32), length])

    links = Links()
    order = reversed_order(groups)
    behind = [(tensor_at - k) % tensors for k in range(tensors)]
    ahead = [(tensor_at + k) % tensors for k in range(tensors)]

    def rows_of(value, index):
        return rows_at(value, index * piece, piece)

    qkv_full = lax.all_gather(
        jnp.concatenate([query_weight, key_weight, value_weight], axis=1),
        ("dp", "expert"), axis=0, tiled=True,
    )
    inputs = layer_input[0].astype(F32)
    gain_one = attention_gain.astype(F32)
    inverse_one = lax.rsqrt(jnp.mean(inputs * inputs, axis=1, keepdims=True) + EPS)
    normed = (inputs * inverse_one * gain_one).astype(BF16)
    bias = jnp.concatenate([query_bias, key_bias, value_bias])[None, :]
    cosine_table, sine_table = rotary_tables(positions, HD)
    queries, kv_own = project(normed, qkv_full, bias, cosine_table, sine_table)
    kv = lax.all_gather(kv_own, "expert", axis=0, tiled=True)
    output_here = lax.all_gather(
        after(output_weight, kv), ("dp", "expert"), axis=0, tiled=True
    )
    heads_low, log_sums = attend(place, queries, kv, heads_here, score_scale)

    (
        route_block, upstream_source, gate_source, up_source, down_source, shared_source, small_source,
    ) = after(
        (
            routes[0], cotangent[0], expert_gate, expert_up, expert_down,
            (shared_gate, shared_up, shared_down), (router_weight, shared_switch),
        ),
        kv_own,
    )

    shared_own = jnp.stack([w.T for w in shared_source])
    own_rows = shared_own.shape[2]

    def units_of(block):
        return lax.dynamic_slice_in_dim(shared_own, block * shared_units, shared_units, axis=1)

    shared_pieces = links.swaps([after(units_of(block_at ^ s), kv) for s in range(1, groups)], "expert")

    expert_ids = jnp.arange(experts, dtype=jnp.int32)
    chosen = jnp.any(route_block[:, :, None] == expert_ids[None, None, :], axis=1) & live_rows[:, None]
    row_ids = jnp.arange(rows, dtype=jnp.int32)
    earlier = (row_ids[None, :] < row_ids[:, None]).astype(BF16)
    before = dot(earlier, chosen.astype(BF16))
    kept = chosen & (before < capacity)
    kept = jnp.pad(kept.astype(BF16), ((0, 0), (0, LANES - experts)))

    upstream_low = jnp.where(live_rows[:, None], upstream_source, jnp.zeros((), BF16))
    upstream_all = links.spread(upstream_low, "expert", low=2)
    kept_all = links.spread(kept, "expert", low=2)

    def pad_units(weight):
        return jnp.pad(weight, ((0, width - weight.shape[0]), (0, 0)))

    gates_t, ups_t, downs_t = (w.transpose(0, 2, 1) for w in (gate_source, up_source, down_source))
    weight_parts = []
    for j in range(local):
        weight_parts += [pad_units(gates_t[j]), pad_units(ups_t[j])]
    lin_weight = jnp.concatenate(weight_parts + [jnp.zeros((pair, depth), BF16)], axis=0)
    down_weight = jnp.concatenate(
        [pad_units(downs_t[j]) for j in range(local)] + [jnp.zeros((width, depth), BF16)], axis=0
    )
    small_weight = jnp.pad(
        jnp.concatenate([small_source[0].T, small_source[1][None, :]], axis=0),
        ((0, LANES - experts - 1), (0, 0)),
    )
    spot_at = jnp.concatenate(
        [block_at * local + jnp.arange(local, dtype=jnp.int32), jnp.full((1,), experts, jnp.int32)]
    )
    spot = (spot_at[:, None] == jnp.arange(LANES, dtype=jnp.int32)[None, :]).astype(F32)
    spot = jnp.pad(spot, ((0, up_to(steps, 8) - steps), (0, 0)))

    shared_pieces = [units_of(block_at)] + shared_pieces
    attended_part = dot_tt(after(heads_low, tuple(shared_pieces)), output_here).astype(BF16)
    shared_half = in_order(shared_pieces, [block_at ^ s for s in range(groups)], 2)
    halves = [shared_half] + links.shifts([shared_half] * (slots - 1), "dp")
    attended = lax.psum_scatter(attended_part, "tensor", scatter_dimension=0, tiled=True).astype(F32)
    inputs_own = rows_of(inputs, tensor_at)
    live_own = rows_of(live_rows, tensor_at)[:, None]
    residual = inputs_own + after(attended, (tuple(halves), upstream_all, kept_all))
    gain_two = mixture_gain.astype(F32)
    inverse_two = lax.rsqrt(jnp.mean(residual * residual, axis=1, keepdims=True) + EPS)
    mix_own = (residual * inverse_two * gain_two).astype(BF16)

    mix_all = lax.all_gather(mix_own, ("expert", "tensor"), axis=0, tiled=True)

    def all_blocks(half):
        found = jnp.concatenate([half, links.swap(half, "expert", 1)], axis=0)
        return in_order(
            [found[i * rows : (i + 1) * rows] for i in range(groups)], [block_at ^ s for s in order], 0
        )

    upstream_all, kept_all = (all_blocks(v) for v in after((upstream_all, kept_all), mix_own))

    halves = list(after(tuple(halves), mix_own))
    for k, found in enumerate(halves):
        column = (slot_at - k) % slots * (depth // slots)
        down_weight = lax.dynamic_update_slice(down_weight, found[2], (local * width, column))
        for i in (0, 1):
            lin_weight = lax.dynamic_update_slice(
                lin_weight, found[i], (local * pair + i * width, column)
            )
    hidden_grads = dot_tt(upstream_all, down_weight)

    output_full = lax.all_gather(
        after(output_weight, (mix_all, hidden_grads)), ("dp", "expert", "tensor"), axis=0, tiled=True
    )
    lin_grads, hiddens, smalls, mix_part = mixture(
        after(mix_all, hidden_grads), hidden_grads, kept_all, spot, small_weight, lin_weight,
        rows, experts, local,
    )
    mix_sum = lax.psum_scatter(after(mix_part, output_full), ("expert", "tensor"), scatter_dimension=0, tiled=True)

    expert_rows = local * width
    down_grad = dot_nt(hiddens[:, :expert_rows], upstream_all).astype(BF16)

    def over_slots(part):
        return links.shifts([part] * (slots - 1), "dp")

    def total(own, arrived):
        return sum((a.astype(F32) for a in arrived), own.astype(F32))

    everyone = ("expert", "dp", "tensor")
    down_parts = jnp.concatenate(
        [down_grad[j * width : j * width + expert_units] for j in range(local)], axis=0
    )
    down_arrived = over_slots(down_parts)

    shared_lin_grad = dot_nt(lin_grads[:, local * pair :], mix_all).astype(BF16)
    shared_down_grad = dot_nt(hiddens[:, expert_rows:], after(upstream_all, down_parts)).astype(BF16)
    shared_part = jnp.concatenate(
        [
            shared_lin_grad[:shared_units],
            shared_lin_grad[width : width + shared_units],
            shared_down_grad[:shared_units],
        ],
        axis=0,
    )
    half = depth // slots

    def half_of(value, index):
        return lax.dynamic_slice_in_dim(value, index * half, half, axis=1)

    lin_parts = []
    for j in range(local):
        found = dot_nt(after(lin_grads[:, j * pair : (j + 1) * pair], shared_part), mix_all).astype(BF16)
        lin_parts.append(
            jnp.concatenate([found[:expert_units], found[width : width + expert_units]], axis=0)
        )
    lin_part = jnp.concatenate(lin_parts, axis=0)
    shared_halves = [half_of(shared_part, (slot_at + k) % slots) for k in range(1, slots)]
    ring = [[(i, (i + k) % slots) for i in range(slots)] for k in range(1, slots)]
    arrived = links.send("x", shared_halves + [lin_part] * (slots - 1), "dp", ring * 2)
    shared_arrived, lin_arrived = arrived[: slots - 1], arrived[slots - 1 :]
    small_grad = dot_nt(after(smalls, down_parts), mix_all)[: experts + 1]
    small_total = sum_over_all(small_grad.reshape(-1), everyone).reshape(experts + 1, depth)

    output_part = dot(after(hiddens, down_parts), down_weight).astype(BF16)
    output_part = output_part.reshape(groups, rows, depth)

    output_full = output_full.reshape(slots * groups, tensors, depth // (slots * groups), wide)
    output_full = output_full.transpose(0, 2, 1, 3).reshape(depth, tensors * wide)
    mix_sum, output_part, lin_own, shared_own_part, output_full = together(
        after(mix_sum, (tuple(down_arrived), small_grad)), output_part, lin_part, shared_part, output_full
    )
    mix_grad = mix_sum.astype(F32)
    down_total = total(down_parts, after(tuple(down_arrived), mix_sum))
    down_total = down_total.reshape(local, expert_units, depth)
    scaled_two = mix_grad * gain_two
    mixture_gain_grad = jnp.sum(mix_grad * residual * inverse_two, axis=0)
    upstream_own = rows_of(upstream_low, tensor_at).astype(F32)
    residual_grad = (
        upstream_own
        + inverse_two * scaled_two
        - residual * inverse_two**3 * jnp.mean(scaled_two * residual, axis=1, keepdims=True)
    )
    attended_grad = residual_grad.astype(BF16)
    attended_all = lax.all_gather(attended_grad, "tensor", axis=0, tiled=True)
    heads_grad_rows = dot(attended_grad, output_full).astype(BF16)

    def heads_of(index):
        return lax.dynamic_slice_in_dim(heads_grad_rows, index * wide, wide, axis=1)

    grads_in = [heads_of(tensor_at)] + links.shifts(
        [heads_of(ahead[k]) for k in range(1, tensors)], "tensor"
    )

    heads_grad = in_order(grads_in, behind, 0)
    query_grads, kv_grads = attend_back(
        place, queries, heads_grad, heads_low, log_sums, kv, heads_here, score_scale
    )
    kv_sum = lax.psum_scatter(kv_grads, "expert", scatter_dimension=0, tiled=True)
    pre_grad, bias_grad = turn_back(
        query_grads, kv_sum, cosine_table, sine_table)
    normed_part = dot_tt(pre_grad, qkv_full).astype(BF16)
    normed_sum = lax.psum_scatter(normed_part, "tensor", scatter_dimension=0, tiled=True)
    normed_grad = after(normed_sum, tuple(arrived)).astype(F32)
    inverse_own = rows_of(inverse_one, tensor_at)
    scaled_one = normed_grad * gain_one
    attention_gain_grad = jnp.sum(normed_grad * inputs_own * inverse_own, axis=0)
    input_grad = (
        residual_grad
        + inverse_own * scaled_one
        - inputs_own * inverse_own**3 * jnp.mean(scaled_one * inputs_own, axis=1, keepdims=True)
    )
    input_low = input_grad.astype(BF16)
    input_all = lax.all_gather(input_low, "tensor", axis=0, tiled=True)

    shared_sum = total(half_of(shared_own_part, slot_at), after(tuple(shared_arrived), input_low))
    shared_sum = shared_sum.astype(BF16).reshape(3, shared_units, depth // slots)
    lin_total = total(lin_own, after(tuple(lin_arrived), input_low))
    lin_total = lin_total.reshape(local, 2, expert_units, depth)

    input_grad = input_all.astype(F32)
    own = depth // (slots * groups)

    def columns_for(value, part):
        return jnp.concatenate(
            [
                lax.dynamic_slice_in_dim(
                    value, (((slot_at + k) % slots) * groups + (block_at ^ s)) * own, own, axis=1
                )
                for s in part
                for k in range(slots)
            ],
            axis=1,
        )

    weight_grads = []
    for part in (order[: groups // 2], order[groups // 2 :]):
        weight_grads.append(
            jnp.concatenate(
                [
                    dot_nt(columns_for(normed, part), after(pre_grad, normed_part)).astype(BF16),
                    dot_nt(columns_for(attended_all, part), heads_low).astype(BF16),
                ],
                axis=1,
            )
        )

    output_part = links.scatter(output_part, "expert", kv_sum)
    mine = [rows_of(output_part, tensor_at)] + links.shifts(
        [rows_of(output_part, ahead[k]) for k in range(1, tensors)], "tensor"
    )
    mixed = sum(s.astype(F32) for s in after(tuple(mine), input_low))
    output_own = jnp.where(live_own, residual + mixed, 0.0).astype(BF16)
    layer_output = lax.all_gather(after(output_own, input_all), "tensor", axis=0, tiled=True)

    weight_grad = links.collect(*weight_grads, "expert")
    weight_grads = [weight_grad[k * own : (k + 1) * own] for k in range(slots)]
    weight_grad = sum(
        p.astype(F32) for p in [weight_grads[0]] + links.shifts(weight_grads[1:], "dp")
    )

    def owned_by(block):
        return lax.dynamic_slice_in_dim(shared_sum, block * own_rows, own_rows, axis=2)

    shared_back = [owned_by(block_at)] + [
        links.swap(owned_by(block_at ^ s), "expert", s) for s in range(1, groups)
    ]
    shared_grads = side_by_side(place, shared_back)

    bias_place = lax.dynamic_update_slice_in_dim(
        jnp.zeros((tensors * 3 * wide,), F32), bias_grad[0], tensor_at * 3 * wide, axis=0
    )
    last_sums = sum_over_all(
        jnp.concatenate([attention_gain_grad, mixture_gain_grad, bias_place]), everyone
    )
    bias_total = lax.dynamic_slice_in_dim(
        last_sums, 2 * depth + tensor_at * 3 * wide, 3 * wide, axis=0
    )
    return (
        layer_output[None],
        input_grad[None],
        last_sums[:depth],
        weight_grad[:, :wide],
        weight_grad[:, wide : 2 * wide],
        weight_grad[:, 2 * wide : 3 * wide],
        bias_total[:wide],
        bias_total[wide : 2 * wide],
        bias_total[2 * wide :],
        weight_grad[:, 3 * wide :],
        last_sums[depth : 2 * depth],
        small_total[:experts].T,
        lin_total[:, 0].transpose(0, 2, 1),
        lin_total[:, 1].transpose(0, 2, 1),
        down_total.transpose(0, 2, 1),
        shared_grads[0],
        shared_grads[1],
        shared_grads[2],
        small_total[experts],
    )


def solution(mesh):
    dense = P(("dp", "expert"), "tensor")
    routed = P("expert", None, "tensor")
    rows = P("dp", "expert", None)
    in_specs = (
        rows, P(), dense, dense, dense, P("tensor"), P("tensor"), P("tensor"), dense, P(), P(),
        routed, routed, routed, dense, dense, dense, P(), P("dp"), rows, rows,
    )
    out_specs = (
        rows, rows, P(), dense, dense, dense, P("tensor"), P("tensor"), P("tensor"), dense, P(), P(),
        routed, routed, routed, dense, dense, dense, P(),
    )
    return jax.shard_map(shards, mesh=mesh, in_specs=in_specs, out_specs=out_specs, check_vma=False)
```

time: 1150 us -> 872 us (0.76)
  local copies, waits for them, and re-layouts: 234 us -> 129 us
  starting transfers between devices: 118 us -> 50 us
  waiting for transfers between devices: 439 us -> 374 us
  matrix products: 123 us -> 99.3 us
    ppermute x89 -> x35, waiting for transfers between devices: 439 us -> 198 us  [the longest x25 108 us: send(): arrived = tuple((lax.ppermute(v, axis, p) for v, p in zip(values, perms)))]
    all_gather x1 -> x6, waiting for transfers between devices: 0.02 us -> 74.7 us  [the longest x1 34.6 us: shards(): kv = lax.all_gather(kv_own, 'expert', axis=0, tiled=True)]
    ppermute x89 -> x35, starting transfers between devices: 117 us -> 48 us  [the longest x25 35.9 us: send(): arrived = tuple((lax.ppermute(v, axis, p) for v, p in zip(values, perms)))]
    reduce_scatter x2 -> x4, waiting for transfers between devices: 0.01 us -> 53.2 us  [the longest x1 47.4 us: shards(): lax.psum_scatter(kv_grads, 'expert', scatter_dimension=0, tiled=True)]
    unnamed x305 -> x172, local copies, waits for them, and re-layouts: 91.9 us -> 40.2 us
    all_gather x1, waiting for transfers between devices: 0.01 us -> 45.5 us  [shards(): lax.all_gather(jnp.concatenate([query_weight, key_weight, value_weight],...]
    dynamic_update_slice x26 -> x14, local copies, waits for them, and re-layouts: 46.6 us -> 12.2 us  [in_order(): whole = lax.dynamic_update_slice_in_dim(whole, piece, place * size, axis)]
    another operation x8 -> x1, other arithmetic: 27.3 us -> 1.82 us  [shards(): shared_own = jnp.stack([w.T for w in shared_source])]
  transfers between devices with their start and end apart: 95 -> 47, of which waited for: 30 -> 24; matrix products, arithmetic and copies ran while one was open for 39% -> 34% of each run, Pallas kernels for 9% -> 10%
where the time goes in v2:
time: 872 us; the launch traced here: 867 us
  waiting for transfers between devices  374 us (43%)
  local copies, waits for them, and re-layouts  129 us (15%)
  other arithmetic  105 us (12%)
  matrix products  99.3 us (11%)
  Pallas kernels  94 us (11%)
  starting transfers between devices  50 us (6%)
  between operations  16.7 us (2%)
    ppermute x25, waiting for transfers between devices, send(): arrived = tuple((lax.ppermute(v, axis, p) for v, p in zip(values, perms)))  108 us
    ppermute x10, waiting for transfers between devices, sum_over_all(): lax.ppermute(value, axis, [(i, i ^ bit) for i in range(size)])  90.3 us
    pallas_call x1, Pallas kernels, mixture(): pl.pallas_call(functools.partial(mixture_kernel, experts=experts, local=l...  69.1 us
    dot_general x10, matrix products, dot_nt(): lax.dot_general(a, b, (((0,), (0,)), ((), ())), preferred_element_type=F32)  54.3 us
    reduce_scatter x1, waiting for transfers between devices, shards(): lax.psum_scatter(kv_grads, 'expert', scatter_dimension=0, tiled=True)  47.4 us
    all_gather x1, waiting for transfers between devices, shards(): lax.all_gather(jnp.concatenate([query_weight, key_weight, value_weight],...  45.5 us
    unnamed x172, local copies, waits for them, and re-layouts  40.2 us
    ppermute x25, starting transfers between devices, send(): arrived = tuple((lax.ppermute(v, axis, p) for v, p in zip(values, perms)))  35.9 us
  transfers between devices with their start and end apart: 47, of which 24 were waited for; matrix products, arithmetic and copies ran while one was open for 34% of the time, Pallas kernels for 10%

profile of v2, /device:TPU:0, one launch (start us, length us, event | category | flops | bytes accessed | tf_op | source)
XLA Modules:
  0.0 867.0 jit_solution(15122360624881595562)
XLA Ops:
  13.3 45.5 %all-gather.9.cloned.1.call-done.wq_ref.wk_ref.wv_ref = bf16[2048,1536]{1,0:T(8,128)(2,1)} async-done(((bf16[256,1536]{1,0:T(8,128)(2,1)}), bf16[2048,1536]{1,0:T(8,128)(2,1)}) %all-gather.9.cloned.1.call-update) | async-done | bytes 6291472 | tf_op jit(solution)/shard_map/all_gather | solution.py:544
  66.9 34.6 %all-gather.11.cloned.1.call-done.kv_ref = bf16[2048,1024]{1,0:T(8,128)(2,1)} async-done(((bf16[512,1024]{1,0:T(8,128)(2,1)}), bf16[2048,1024]{1,0:T(8,128)(2,1)}) %all-gather.11.cloned.1.call-update) | async-done | bytes 4194320 | tf_op jit(solution)/shard_map/all_gather | solution.py:555
  113.5 7.4 shard_map.349
  130.3 14.8 %collective-permute-done.2 = bf16[3,352,256]{2,1,0:T(8,128)(2,1)S(1)} collective-permute-done((bf16[3,352,256]{2,1,0:T(8,128)(2,1)S(1)}, bf16[3,352,256]{2,1,0:T(8,128)(2,1)S(1)}, u32[]{:S(2)}, u32[]{:S(2)}) %collective-permute-start.2) | collective-permute-done | bytes 540704 | tf_op jit(solution)/shard_map/over_y/ppermute | solution.py:49
  165.1 36.8 %collective-permute-done.4 = bf16[512,2048]{1,0:T(8,128)(2,1)} collective-permute-done((bf16[512,2048]{1,0:T(8,128)(2,1)}, bf16[512,2048]{1,0:T(8,128)(2,1)}, u32[]{:S(2)}, u32[]{:S(2)}) %collective-permute-start.4) | collective-permute-done | bytes 2097184 | tf_op jit(solution)/shard_map/over_y/ppermute | solution.py:49
  223.5 7.7 fusion.5
  246.4 13.4 %fusion.84.hidden_grad_ref = f32[2048,1152]{1,0:T(8,128)} fusion(bf16[2048,2048]{1,0:T(8,128)(2,1)S(1)} %slice_dynamic-update-slice_fusion, bf16[1152,2048]{1,0:T(8,128)(2,1)S(1)} %get-tuple-element.198), kind=kOutput, calls=%fused_computation.222 | convolution fusion | flops 9663676416 | bytes 22544384 | tf_op jit(solution)/shard_map/dot_general | solution.py:153
  259.8 29.2 %all-gather.15.cloned.1.call-done.mix_ref = bf16[2048,2048]{1,0:T(8,128)(2,1)} async-done(((bf16[128,2048]{1,0:T(8,128)(2,1)}), bf16[2048,2048]{1,0:T(8,128)(2,1)}) %all-gather.15.cloned.1.call-update) | async-done | bytes 8388624 | tf_op jit(solution)/shard_map/all_gather | solution.py:624
  293.3 69.1 %shard_map.350 = (bf16[2048,2304]{1,0:T(8,128)(2,1)}, bf16[2048,1152]{1,0:T(8,128)(2,1)}, bf16[2048,128]{1,0:T(8,128)(2,1)}, bf16[2048,2048]{1,0:T(8,128)(2,1)}) custom-call(bf16[2048,2048]{1,0:T(8,128)(2,1)} %all-gather.15.cloned.1.call-done.mix_ref, f32[2048,1152]{1,0:T(8,128)} %fusion.84.hidden_grad_ref, bf16[2048,128]{1,0:T(8,128)(2,1)} %copy-done.41, ...), custom_call_target="tpu_custom_call" | custom-call | flops 48318382080 | bytes 83886080 | tf_op jit(solution)/shard_map/pallas_call | solution.py:459
  362.4 12.2 %convolution_convert_fusion.6 = bf16[768,2048]{1,0:T(8,128)(2,1)} fusion(bf16[2048,2048]{1,0:T(8,128)(2,1)} %copy-done.27, bf16[2048,1152]{1,0:T(8,128)(2,1)} %get-tuple-element.126), kind=kOutput, calls=%fused_computation.34 | convolution fusion | flops 6444023808 | bytes 14680064 | tf_op jit(solution)/shard_map/dot_general | solution.py:157
  380.0 9.5 %fusion.11 = bf16[384,2048]{1,0:T(8,128)(2,1)S(1)} fusion(bf16[2048,2048]{1,0:T(8,128)(2,1)} %copy-done.27, bf16[2048,1152]{1,0:T(8,128)(2,1)} %get-tuple-element.126), kind=kOutput, calls=%fused_computation.50 | convolution fusion | flops 3221225472 | bytes 11534336 | tf_op jit(solution)/shard_map/dot_general | solution.py:157
  390.5 7.3 convolution_convert_fusion.5
  402.6 8.4 convolution_convert_fusion.3
  411.4 7.0 convolution_convert_fusion.4
  420.6 12.9 %pad_maximum_fusion = bf16[1408,2048]{1,0:T(8,128)(2,1)} fusion(bf16[352,2048]{1,0:T(8,128)(2,1)S(1)} %get-tuple-element.182, bf16[352,2048]{1,0:T(8,128)(2,1)S(1)} %get-tuple-element.181, bf16[352,2048]{1,0:T(8,128)(2,1)S(1)} %get-tuple-element.180, bf16[352,2048]{1,0:T(8,128)(2,1)S(1)} %get-tuple-element.179), kind=kLoop, calls=%fused_computation.13 | loop fusion | flops 23068672 | bytes 11534336 | tf_op jit(solution)/shard_map/concatenate | solution.py:689
  433.6 12.9 %convolution_convert_fusion = bf16[2048,2048]{1,0:T(8,128)(2,1)} fusion(bf16[2048,1152]{1,0:T(8,128)(2,1)S(1)} %bitcast.159, bf16[1152,2048]{1,0:T(8,128)(2,1)S(1)} %bitcast.144), kind=kOutput, calls=%fused_computation.10 | convolution fusion | flops 9667870720 | bytes 17825792 | tf_op jit(solution)/shard_map/dot_general | solution.py:161
  446.5 15.0 %copy.75 = bf16[8,4,256,512]{2,0,3,1:T(8,128)(2,1)} copy(bf16[8,4,256,512]{3,2,1,0:T(8,128)(2,1)} %bitcast.141) | data formatting | bytes 16777216 | tf_op jit(solution)/shard_map/reshape | solution.py:700
  461.5 10.4 %copy.86 = bf16[256,8,8,256]{3,1,2,0:T(8,128)(2,1)} copy(bf16[256,8,8,256]{3,2,1,0:T(8,128)(2,1)} %bitcast.133) | data formatting | bytes 16777216
  483.0 6.4 convolution_convert_fusion.9
  502.8 7.7 collective-permute-done.11
  514.1 8.5 shard_map.351
  543.9 47.4 %reduce-scatter.9.cloned.1.call-done.dkv_ref = bf16[512,1024]{1,0:T(8,128)(2,1)} async-done(((bf16[2048,1024]{1,0:T(8,128)(2,1)}), bf16[512,1024]{1,0:T(8,128)(2,1)}) %reduce-scatter.9.cloned.1.call-update) | async-done | bytes 1048592 | tf_op jit(solution)/shard_map/reduce_scatter | solution.py:731
  593.3 7.4 convolution_convert_fusion.7
  618.9 43.6 %collective-permute-done.28 = f32[18432]{0:T(1024)S(1)} collective-permute-done((f32[18432]{0:T(1024)S(1)}, f32[18432]{0:T(1024)S(1)}, u32[]{:S(2)}, u32[]{:S(2)}) %collective-permute-start.28) | collective-permute-done | bytes 73760 | tf_op jit(solution)/shard_map/ppermute | solution.py:117
  667.0 6.9 collective-permute-start.30
  703.5 25.9 %collective-permute-done.17 = bf16[1056,1024]{1,0:T(8,128)(2,1)} collective-permute-done((bf16[1056,1024]{1,0:T(8,128)(2,1)}, bf16[1056,1024]{1,0:T(8,128)(2,1)}, u32[]{:S(2)}, u32[]{:S(2)}) %collective-permute-start.17) | collective-permute-done | bytes 2162720 | tf_op jit(solution)/shard_map/over_x/ppermute | solution.py:49
  744.6 9.4 %collective-permute-start.25 = (bf16[512,2048]{1,0:T(8,128)(2,1)}, bf16[512,2048]{1,0:T(8,128)(2,1)S(1)}, u32[]{:S(2)}, u32[]{:S(2)}) collective-permute-start(bf16[512,2048]{1,0:T(8,128)(2,1)} %slice.243), channel_id=1, source_target_pairs={{0,8},{4,12},{8,0},{12,4},{1,9},{5,13},{9,1},{13,5},{2,10},{6,14},... | collective-permute-start | bytes 6291464 | tf_op jit(solution)/shard_map/over_y/ppermute | solution.py:49
  754.0 11.4 %convert_add_fusion = f32[1408,2048]{1,0:T(8,128)} fusion(bf16[1408,2048]{1,0:T(8,128)(2,1)} %collective-permute-done.18, bf16[1408,2048]{1,0:T(8,128)(2,1)} %pad_maximum_fusion), kind=kLoop, calls=%fused_computation.2 | loop fusion | flops 8650752 | bytes 23068672 | tf_op jit(solution)/shard_map/add | solution.py:660
  770.0 31.3 %collective-permute-done.20 = f32[10240]{0:T(1024)S(1)} collective-permute-done((f32[10240]{0:T(1024)S(1)}, f32[10240]{0:T(1024)S(1)}, u32[]{:S(2)}, u32[]{:S(2)}) %collective-permute-start.20) | collective-permute-done | bytes 40992 | tf_op jit(solution)/shard_map/ppermute | solution.py:117
  815.3 11.3 %slice_bitcast_fusion = (f32[2,2048,352]{1,2,0:T(8,128)}, f32[2,2048,352]{1,2,0:T(8,128)}) fusion(f32[2,2,352,2048]{3,2,1,0:T(8,128)} %bitcast.131), kind=kLoop, calls=%fused_computation.11 | loop fusion | bytes 23068672 | tf_op jit(solution)/shard_map/transpose | solution.py:825
  828.0 7.9 collective-permute-done.26
  845.7 10.9 %all-gather.21.cloned.1.call-done = bf16[512,2048]{1,0:T(8,128)(2,1)} async-done(((bf16[128,2048]{1,0:T(8,128)(2,1)}), bf16[512,2048]{1,0:T(8,128)(2,1)}) %all-gather.21.cloned.1.call-update) | async-done | bytes 2097168 | tf_op jit(solution)/shard_map/all_gather | solution.py:786
  (399 shorter events, 260.4 us)
Async XLA Ops:
  7.2 51.6 %all-gather.9.cloned.1.call-start = ((), (), s32[]{:S(2)}) async-start(), calls=%async_computation.4 | async-start | bytes 7077888 | tf_op jit(solution)/shard_map/all_gather | solution.py:544
  9.5 92.1 %all-gather.11.cloned.1.call-start = ((), (), s32[]{:S(2)}) async-start(), calls=%async_computation.5 | async-start | bytes 5242880 | tf_op jit(solution)/shard_map/all_gather | solution.py:555
  66.9 79.0 %all-gather.13.cloned.1.call-start = ((), (), s32[]{:S(2)}) async-start(), calls=%async_computation.6 | async-start | bytes 2359296 | tf_op jit(solution)/shard_map/all_gather | solution.py:556
  101.5 105.5 %reduce-scatter.5.cloned.1.call-start = ((), (), s32[]{:S(2)}) async-start(), calls=%async_computation.7 | async-start | bytes 2621440 | tf_op jit(solution)/shard_map/reduce_scatter | solution.py:616
  111.2 18.3 %collective-permute-start.1 = (bf16[3,352,256]{2,1,0:T(8,128)(2,1)S(1)}, bf16[3,352,256]{2,1,0:T(8,128)(2,1)S(1)}, u32[]{:S(2)}, u32[]{:S(2)}) collective-permute-start(bf16[3,352,256]{2,1,0:T(8,128)(2,1)S(1)} %get-tuple-element.99), channel_id=1, source_target_pairs={{0,8},{4,12},{8,0},{12,4},{1,9},{5,13},{9,1},{13,5},{2,10},{6,14},... | collective-permute-start | bytes 1622024 | tf_op jit(solution)/shard_map/over_y/ppermute | solution.py:49
  111.5 33.6 %collective-permute-start.2 = (bf16[3,352,256]{2,1,0:T(8,128)(2,1)S(1)}, bf16[3,352,256]{2,1,0:T(8,128)(2,1)S(1)}, u32[]{:S(2)}, u32[]{:S(2)}) collective-permute-start(bf16[3,352,256]{2,1,0:T(8,128)(2,1)S(1)} %get-tuple-element.100), channel_id=1, source_target_pairs={{0,12},{4,8},{8,4},{12,0},{1,13},{5,9},{9,5},{13,1},{2,14},{6,10},... | collective-permute-start | bytes 1622024 | tf_op jit(solution)/shard_map/over_y/ppermute | solution.py:49
  150.3 138.7 %all-gather.15.cloned.1.call-start = ((), (), s32[]{:S(2)}) async-start(), calls=%async_computation.8 | async-start | bytes 8912896 | tf_op jit(solution)/shard_map/all_gather | solution.py:624
  154.0 48.0 %collective-permute-start.4 = (bf16[512,2048]{1,0:T(8,128)(2,1)}, bf16[512,2048]{1,0:T(8,128)(2,1)}, u32[]{:S(2)}, u32[]{:S(2)}) collective-permute-start(bf16[512,2048]{1,0:T(8,128)(2,1)} %broadcast_select_fusion), channel_id=1, source_target_pairs={{0,8},{4,12},{8,0},{12,4},{1,9},{5,13},{9,1},{13,5},{2,10},{6,14},... | collective-permute-start | bytes 6291464 | tf_op jit(solution)/shard_map/over_y/ppermute | solution.py:49
  160.1 49.2 %collective-permute-start.3 = (bf16[3,352,1024]{2,1,0:T(8,128)(2,1)}, bf16[3,352,1024]{2,1,0:T(8,128)(2,1)}, u32[]{:S(2)}, u32[]{:S(2)}) collective-permute-start(bf16[3,352,1024]{2,1,0:T(8,128)(2,1)} %constant_dynamic-update-slice_fusion.3), channel_id=1, source_target_pairs={{0,16},{16,0},{1,17},{17,1},{2,18},{18,2},{3,19},{19,3},{4,20},{20... | collective-permute-start | bytes 6488072 | tf_op jit(solution)/shard_map/over_x/ppermute | solution.py:49
  212.8 161.8 %all-gather.17.cloned.1.call-start = ((), (), s32[]{:S(2)}) async-start(), calls=%async_computation.9 | async-start | bytes 8650752 | tf_op jit(solution)/shard_map/all_gather | solution.py:644
  221.0 18.4 %collective-permute-start.6 = (bf16[1024,2048]{1,0:T(8,128)(2,1)S(1)}, bf16[1024,2048]{1,0:T(8,128)(2,1)}, u32[]{:S(2)}, u32[]{:S(2)}) collective-permute-start(bf16[1024,2048]{1,0:T(8,128)(2,1)S(1)} %copy-done.22), channel_id=1, source_target_pairs={{0,4},{4,0},{8,12},{12,8},{1,5},{5,1},{9,13},{13,9},{2,6},{6,2},{1... | collective-permute-start | bytes 12582920 | tf_op jit(solution)/shard_map/over_core/ppermute | solution.py:49
  289.0 188.6 %reduce-scatter.7.cloned.1.call-start = ((), (), s32[]{:S(2)}) async-start(), calls=%async_computation.10 | async-start | bytes 8912896 | tf_op jit(solution)/shard_map/reduce_scatter | solution.py:651
  374.6 165.0 %all-gather.23.cloned.1.call-start = ((), (), s32[]{:S(2)}) async-start(), calls=%async_computation.15 | async-start | bytes 2621440 | tf_op jit(solution)/shard_map/all_gather | solution.py:717
  378.5 93.4 %collective-permute-start.8 = (bf16[704,2048]{1,0:T(8,128)(2,1)}, bf16[704,2048]{1,0:T(8,128)(2,1)}, u32[]{:S(2)}, u32[]{:S(2)}) collective-permute-start(bf16[704,2048]{1,0:T(8,128)(2,1)} %pad_maximum_fusion.4), channel_id=1, source_target_pairs={{0,16},{16,0},{1,17},{17,1},{2,18},{18,2},{3,19},{19,3},{4,20},{20... | collective-permute-start | bytes 8650760 | tf_op jit(solution)/shard_map/over_x/ppermute | solution.py:49
  482.7 108.6 %reduce-scatter.9.cloned.1.call-start = ((), (), s32[]{:S(2)}) async-start(), calls=%async_computation.11 | async-start | bytes 5242880 | tf_op jit(solution)/shard_map/reduce_scatter | solution.py:731
  492.7 17.8 %collective-permute-start.11 = (bf16[128,512]{1,0:T(8,128)(2,1)}, bf16[128,512]{1,0:T(8,128)(2,1)S(1)}, u32[]{:S(2)}, u32[]{:S(2)}) collective-permute-start(bf16[128,512]{1,0:T(8,128)(2,1)} %get-tuple-element.231), channel_id=1, source_target_pairs={{0,2},{1,3},{2,0},{3,1},{4,6},{5,7},{6,4},{7,5},{8,10},{9,11},{10,... | collective-permute-start | bytes 393224 | tf_op jit(solution)/shard_map/over_z/ppermute | solution.py:49
  523.6 208.4 %reduce-scatter.11.cloned.1.call-start = ((), (), s32[]{:S(2)}) async-start(), calls=%async_computation.12 | async-start | bytes 2621440 | tf_op jit(solution)/shard_map/reduce_scatter | solution.py:735
  528.4 72.7 %collective-permute-start.9 = (bf16[2,512,2048]{2,1,0:T(8,128)(2,1)}, bf16[2,512,2048]{2,1,0:T(8,128)(2,1)}, u32[]{:S(2)}, u32[]{:S(2)}) collective-permute-start(bf16[2,512,2048]{2,1,0:T(8,128)(2,1)} %dynamic-slice_bitcast_fusion), channel_id=1, source_target_pairs={{0,4},{4,0},{8,12},{12,8},{1,5},{5,1},{9,13},{13,9},{2,6},{6,2},{1... | collective-permute-start | bytes 12582920 | tf_op jit(solution)/shard_map/over_core/ppermute | solution.py:49
  536.1 195.8 %collective-permute-start.18 = (bf16[1408,2048]{1,0:T(8,128)(2,1)}, bf16[1408,2048]{1,0:T(8,128)(2,1)}, u32[]{:S(2)}, u32[]{:S(2)}) collective-permute-start(bf16[1408,2048]{1,0:T(8,128)(2,1)} %pad_maximum_fusion), channel_id=1, source_target_pairs={{0,16},{16,0},{1,17},{17,1},{2,18},{18,2},{3,19},{19,3},{4,20},{20... | collective-permute-start | bytes 17301512 | tf_op jit(solution)/shard_map/over_x/ppermute | solution.py:49
  600.8 208.7 %all-gather.19.cloned.1.call-start = ((), (), s32[]{:S(2)}) async-start(), calls=%async_computation.13 | async-start | bytes 2621440 | tf_op jit(solution)/shard_map/all_gather | solution.py:746
  611.3 126.0 %collective-permute-start.24 = (bf16[1024,2048]{1,0:T(8,128)(2,1)}, bf16[1024,2048]{1,0:T(8,128)(2,1)}, u32[]{:S(2)}, u32[]{:S(2)}) collective-permute-start(bf16[1024,2048]{1,0:T(8,128)(2,1)} %pad_maximum_fusion.3), channel_id=1, source_target_pairs={{0,4},{4,0},{8,12},{12,8},{1,5},{5,1},{9,13},{13,9},{2,6},{6,2},{1... | collective-permute-start | bytes 12582920 | tf_op jit(solution)/shard_map/over_core/ppermute | solution.py:49
  612.8 83.8 %collective-permute-start.13 = (bf16[1,512,2048]{2,1,0:T(8,128)(2,1)}, bf16[1,512,2048]{2,1,0:T(8,128)(2,1)}, u32[]{:S(2)}, u32[]{:S(2)}) collective-permute-start(bf16[1,512,2048]{2,1,0:T(8,128)(2,1)} %constant_dynamic-slice_fusion.21), channel_id=1, source_target_pairs={{0,8},{4,12},{8,0},{12,4},{1,9},{5,13},{9,1},{13,5},{2,10},{6,14},... | collective-permute-start | bytes 6291464 | tf_op jit(solution)/shard_map/over_y/ppermute | solution.py:49
  618.6 44.0 %collective-permute-start.28 = (f32[18432]{0:T(1024)S(1)}, f32[18432]{0:T(1024)S(1)}, u32[]{:S(2)}, u32[]{:S(2)}) collective-permute-start(f32[18432]{0:T(1024)S(1)} %add.495), channel_id=1, source_target_pairs={{0,8},{4,12},{8,0},{12,4},{1,9},{5,13},{9,1},{13,5},{2,10},{6,14},... | collective-permute-start | bytes 221192 | tf_op jit(solution)/shard_map/ppermute | solution.py:117
  682.9 46.6 %collective-permute-start.17 = (bf16[1056,1024]{1,0:T(8,128)(2,1)}, bf16[1056,1024]{1,0:T(8,128)(2,1)}, u32[]{:S(2)}, u32[]{:S(2)}) collective-permute-start(bf16[1056,1024]{1,0:T(8,128)(2,1)} %constant_dynamic-slice_fusion.20), channel_id=1, source_target_pairs={{0,16},{16,0},{1,17},{17,1},{2,18},{18,2},{3,19},{19,3},{4,20},{20... | collective-permute-start | bytes 6488072 | tf_op jit(solution)/shard_map/over_x/ppermute | solution.py:49
  700.3 69.6 %collective-permute-start.14 = (bf16[128,2048]{1,0:T(8,128)(2,1)}, bf16[128,2048]{1,0:T(8,128)(2,1)}, u32[]{:S(2)}, u32[]{:S(2)}) collective-permute-start(bf16[128,2048]{1,0:T(8,128)(2,1)} %get-tuple-element.138), channel_id=1, source_target_pairs={{0,1},{1,2},{2,3},{3,0},{4,5},{5,6},{6,7},{7,4},{8,9},{9,10},{10,1... | collective-permute-start | bytes 1572872 | tf_op jit(solution)/shard_map/over_z/ppermute | solution.py:49
  702.4 67.6 %collective-permute-start.15 = (bf16[128,2048]{1,0:T(8,128)(2,1)}, bf16[128,2048]{1,0:T(8,128)(2,1)}, u32[]{:S(2)}, u32[]{:S(2)}) collective-permute-start(bf16[128,2048]{1,0:T(8,128)(2,1)} %get-tuple-element.139), channel_id=1, source_target_pairs={{0,2},{1,3},{2,0},{3,1},{4,6},{5,7},{6,4},{7,5},{8,10},{9,11},{10,... | collective-permute-start | bytes 1572872 | tf_op jit(solution)/shard_map/over_z/ppermute | solution.py:49
  729.4 40.6 %collective-permute-start.16 = (bf16[128,2048]{1,0:T(8,128)(2,1)}, bf16[128,2048]{1,0:T(8,128)(2,1)}, u32[]{:S(2)}, u32[]{:S(2)}) collective-permute-start(bf16[128,2048]{1,0:T(8,128)(2,1)} %get-tuple-element.140), channel_id=1, source_target_pairs={{0,3},{1,0},{2,1},{3,2},{4,7},{5,4},{6,5},{7,6},{8,11},{9,8},{10,9... | collective-permute-start | bytes 1572872 | tf_op jit(solution)/shard_map/over_z/ppermute | solution.py:49
  736.9 119.7 %all-gather.21.cloned.1.call-start = ((), (), s32[]{:S(2)}) async-start(), calls=%async_computation.14 | async-start | bytes 2621440 | tf_op jit(solution)/shard_map/all_gather | solution.py:786
  737.2 28.2 %collective-permute-start.19 = (f32[10240]{0:T(1024)S(1)}, f32[10240]{0:T(1024)S(1)}, u32[]{:S(2)}, u32[]{:S(2)}) collective-permute-start(f32[10240]{0:T(1024)S(1)} %pad_maximum_fusion.10), channel_id=1, source_target_pairs={{0,4},{4,0},{8,12},{12,8},{1,5},{5,1},{9,13},{13,9},{2,6},{6,2},{1... | collective-permute-start | bytes 122888 | tf_op jit(solution)/shard_map/ppermute | solution.py:117
  744.6 65.0 %collective-permute-start.25 = (bf16[512,2048]{1,0:T(8,128)(2,1)}, bf16[512,2048]{1,0:T(8,128)(2,1)S(1)}, u32[]{:S(2)}, u32[]{:S(2)}) collective-permute-start(bf16[512,2048]{1,0:T(8,128)(2,1)} %slice.243), channel_id=1, source_target_pairs={{0,8},{4,12},{8,0},{12,4},{1,9},{5,13},{9,1},{13,5},{2,10},{6,14},... | collective-permute-start | bytes 6291464 | tf_op jit(solution)/shard_map/over_y/ppermute | solution.py:49
  765.4 35.9 %collective-permute-start.20 = (f32[10240]{0:T(1024)S(1)}, f32[10240]{0:T(1024)S(1)}, u32[]{:S(2)}, u32[]{:S(2)}) collective-permute-start(f32[10240]{0:T(1024)S(1)} %fusion.74), channel_id=1, source_target_pairs={{0,8},{4,12},{8,0},{12,4},{1,9},{5,13},{9,1},{13,5},{2,10},{6,14},... | collective-permute-start | bytes 122888 | tf_op jit(solution)/shard_map/ppermute | solution.py:117
  812.1 23.8 %collective-permute-start.26 = (bf16[256,2048]{1,0:T(8,128)(2,1)S(1)}, bf16[256,2048]{1,0:T(8,128)(2,1)}, u32[]{:S(2)}, u32[]{:S(2)}) collective-permute-start(bf16[256,2048]{1,0:T(8,128)(2,1)S(1)} %slice.245), channel_id=1, source_target_pairs={{0,16},{16,0},{1,17},{17,1},{2,18},{18,2},{3,19},{19,3},{4,20},{20... | collective-permute-start | bytes 3145736 | tf_op jit(solution)/shard_map/over_x/ppermute | solution.py:49
  (98 other events, 1221.1 us)
Sparse Core Ops, SparseCore 0:
  10.5 48.2 all-gather.8
  67.0 34.4 all-gather.10
  103.4 36.2 all-gather.12
  150.4 43.8 reduce-scatter.4
  212.9 76.0 all-gather.14
  292.3 75.6 all-gather.16
  374.7 102.8 reduce-scatter.6
  482.8 56.7 all-gather.22
  542.9 48.3 reduce-scatter.8
  600.9 43.8 reduce-scatter.10
  737.0 52.0 all-gather.18
  809.7 46.8 all-gather.20

commit v3 on v2

--- a/solution.py
+++ b/solution.py
@@ -82,20 +82,17 @@
         arrived = self.swap(far, axis, bit)
         return (near.astype(F32) + arrived.astype(F32)).astype(near.dtype)
 
-    def scatter(self, value, axis, wait):
+    def scatter(self, value, axis, bit, upto):
         at = lax.axis_index(axis)
-        bit = 1
-        while value.shape[0] > 1:
+        while bit < upto:
             value = value.reshape(value.shape[0] // 2, 2, *value.shape[1:])
             own = lax.rem(at // bit, 2)
             near, far = (
                 lax.dynamic_index_in_dim(value, i, axis=1, keepdims=False) for i in (own, 1 - own)
             )
             value = self.meet(near, far, axis, bit)
-            if bit == 1:
-                value = after(value, wait)
             bit *= 2
-        return value[0]
+        return value
 
     def collect(self, near, far, axis, low=1):
         bit = low
@@ -133,6 +130,11 @@
 
 def together(*values):
     return lax.optimization_barrier(values)
+
+
+def halves_of(value):
+    half = value.shape[0] // 2
+    return value[:half], value[half:]
 
 
 def rows_at(value, start, size):
@@ -240,36 +242,34 @@
     )(query_grads, kv_grads, cosine, sine)
 
 
-def attend_kernel(place_ref, q_ref, kv_ref, out_ref, log_ref, peak, total, mix, *, groups, score_scale):
+def seen_scores(query, key, length, score_scale):
+    rows, columns = query.shape[0], key.shape[0]
+    scores = dot_tt(query, key) * score_scale
+    column = lax.broadcasted_iota(jnp.int32, (1, columns), 1)
+    scores = scores + jnp.where(column < length, 0.0, NEGATIVE)
+    far = lax.broadcasted_iota(jnp.int32, (rows, rows), 1) <= lax.broadcasted_iota(jnp.int32, (rows, rows), 0)
+    near = jnp.where(far, scores[:, columns - rows :], NEGATIVE)
+    return near if columns == rows else jnp.concatenate([scores[:, : columns - rows], near], axis=1)
+
+
+def attend_kernel(place_ref, q_ref, kv_ref, out_ref, log_ref, *, groups, score_scale):
     me, length = place_ref[0], place_ref[1]
     rows = q_ref.shape[0]
-    query = q_ref[...]
-    peak[...] = jnp.full_like(peak, NEGATIVE)
-    total[...] = jnp.zeros_like(total)
-    mix[...] = jnp.zeros_like(mix)
-
-    def block(j, last):
-        here = slice(j * rows, (j + 1) * rows)
-        key, value = kv_ref[here, :HD], kv_ref[here, HD:]
-        scores = dot_tt(query, key) * score_scale
-        column = lax.broadcasted_iota(jnp.int32, (rows, rows), 1)
-        good = column < length - j * rows
-        if last:
-            good &= column <= lax.broadcasted_iota(jnp.int32, (rows, rows), 0)
-        scores = jnp.where(good, scores, NEGATIVE)
-        new_peak = jnp.maximum(peak[...], jnp.max(scores, axis=1, keepdims=True))
-        keep = jnp.exp(peak[...] - new_peak)
-        lifted = jnp.exp(scores - new_peak)
-        peak[...] = new_peak
-        total[...] = total[...] * keep + jnp.sum(lifted, axis=1, keepdims=True)
-        mix[...] = mix[...] * keep + dot(lifted.astype(BF16), value)
+    part = rows // 2
+
+    def block(j):
+        for first in range(0, rows, part):
+            here, seen = slice(first, first + part), slice(0, j * rows + first + part)
+            scores = seen_scores(q_ref[here, :], kv_ref[seen, :HD], length, score_scale)
+            peak = jnp.max(scores, axis=1, keepdims=True)
+            lifted = jnp.exp(scores - peak)
+            total = jnp.sum(lifted, axis=1, keepdims=True)
+            mix = dot(lifted.astype(BF16), kv_ref[seen, HD:])
+            out_ref[here, :] = (mix / total).astype(BF16)
+            log_ref[0, here, :] = peak + jnp.log(total)
 
     for j in range(groups):
-        alive = j * rows < length
-        pl.when((j < me) & alive)(functools.partial(block, j, False))
-        pl.when((j == me) & alive)(functools.partial(block, j, True))
-    out_ref[...] = (mix[...] / total[...]).astype(BF16)
-    log_ref[0] = peak[...] + jnp.log(total[...])
+        pl.when(me == j)(functools.partial(block, j))
 
 
 def attend(place, query, kv, heads, score_scale):
@@ -286,11 +286,6 @@
             pl.BlockSpec((rows, HD), lambda h, p: (0, h)),
             pl.BlockSpec((1, rows, 1), lambda h, p: (h, 0, 0)),
         ],
-        scratch_shapes=[
-            pltpu.VMEM((rows, 1), F32),
-            pltpu.VMEM((rows, 1), F32),
-            pltpu.VMEM((rows, HD), F32),
-        ],
     )
     work = heads * rows * rows * groups
     return pl.pallas_call(
@@ -306,39 +301,39 @@
 
 
 def attend_back_kernel(
-    place_ref, q_ref, g_ref, o_ref, log_ref, kv_ref, dq_ref, dkv_ref, total, *, groups, score_scale
+    place_ref, q_ref, g_ref, o_ref, log_ref, kv_ref, dq_ref, dkv_ref, sums, *, groups, score_scale
 ):
     me, length = place_ref[0], place_ref[1]
     rows = q_ref.shape[0]
-    query, grad = q_ref[...], g_ref[...]
-    log_sum = log_ref[0]
-    centre = jnp.sum(grad.astype(F32) * o_ref[...].astype(F32), axis=1, keepdims=True)
-    total[...] = jnp.zeros_like(total)
-
-    def block(j, last):
-        here = slice(j * rows, (j + 1) * rows)
-        key, value = kv_ref[here, :HD], kv_ref[here, HD:]
-        scores = dot_tt(query, key) * score_scale
-        column = lax.broadcasted_iota(jnp.int32, (rows, rows), 1)
-        good = column < length - j * rows
-        if last:
-            good &= column <= lax.broadcasted_iota(jnp.int32, (rows, rows), 0)
-        weights = jnp.exp(jnp.where(good, scores, NEGATIVE) - log_sum)
-        weight_grad = dot_tt(grad, value)
-        score_grad = (weights * (weight_grad - centre)).astype(BF16)
-        total[...] += dot(score_grad, key)
-        dkv_ref[here, :HD] = (dot_nt(score_grad, query) * score_scale).astype(BF16)
-        dkv_ref[here, HD:] = dot_nt(weights.astype(BF16), grad).astype(BF16)
-
-    def nothing(j):
-        dkv_ref[j * rows : (j + 1) * rows, :] = jnp.zeros((rows, 2 * HD), BF16)
+    part = rows // 2
+
+    def block(j):
+        for first in reversed(range(0, rows, part)):
+            here, seen = slice(first, first + part), slice(0, j * rows + first + part)
+            query, grad, key = q_ref[here, :], g_ref[here, :], kv_ref[seen, :HD]
+            centre = jnp.sum(
+                grad.astype(F32) * o_ref[here, :].astype(F32), axis=1, keepdims=True
+            )
+            scores = seen_scores(query, key, length, score_scale)
+            weights = jnp.exp(scores - log_ref[0, here, :])
+            weight_grad = dot_tt(grad, kv_ref[seen, HD:])
+            score_grad = (weights * (weight_grad - centre)).astype(BF16)
+            dq_ref[here, :] = dot(score_grad, key) * score_scale
+            key_grad = dot_nt(score_grad, query) * score_scale
+            value_grad = dot_nt(weights.astype(BF16), grad)
+            if first + part == rows:
+                sums[seen, :HD] = key_grad
+                sums[seen, HD:] = value_grad
+            else:
+                sums[seen, :HD] += key_grad
+                sums[seen, HD:] += value_grad
+        dkv_ref[: (j + 1) * rows, :] = sums[: (j + 1) * rows, :].astype(BF16)
+        if j + 1 < groups:
+            rest = (groups - 1 - j) * rows
+            dkv_ref[(j + 1) * rows :, :] = jnp.zeros((rest, 2 * HD), BF16)
 
     for j in range(groups):
-        alive = j * rows < length
-        pl.when((j < me) & alive)(functools.partial(block, j, False))
-        pl.when((j == me) & alive)(functools.partial(block, j, True))
-        pl.when((j > me) | jnp.logical_not(alive))(functools.partial(nothing, j))
-    dq_ref[...] = total[...] * score_scale
+        pl.when(me == j)(functools.partial(block, j))
 
 
 def attend_back(place, query, grad, out, log_sums, kv, heads, score_scale):
@@ -351,7 +346,7 @@
         grid=(heads,),
         in_specs=[head, head, head, pl.BlockSpec((1, rows, 1), lambda h, p: (h, 0, 0)), pair],
         out_specs=[head, pair],
-        scratch_shapes=[pltpu.VMEM((rows, HD), F32)],
+        scratch_shapes=[pltpu.VMEM((groups * rows, 2 * HD), F32)],
     )
     work = heads * rows * rows * groups
     return pl.pallas_call(
@@ -395,94 +390,76 @@
 
 def mixture_kernel(
     mix_ref, hidden_grad_ref, kept_ref, spot_ref, router_ref, weight_ref,
-    lin_grad_ref, hidden_ref, small_ref, part_ref,
-    total, probs_ref, logits_ref, gate_grad_ref, *, experts, local,
+    lin_grad_ref, hidden_ref, small_ref, part_ref, *, experts, local,
 ):
-    step = pl.program_id(1)
-    width = hidden_ref.shape[1]
+    pair = weight_ref.shape[0] // (local + 1)
+    width = pair // 2
     mix = mix_ref[...]
     lane = lax.broadcasted_iota(jnp.int32, kept_ref.shape, 1)
-
-    @pl.when(step == 0)
-    def _():
-        logits = dot_tt(mix, router_ref[...])
-        logits_ref[...] = logits
-        masked = jnp.where(lane < experts, logits, NEGATIVE)
-        lifted = jnp.exp(masked - jnp.max(masked, axis=1, keepdims=True))
-        probs_ref[...] = lifted / jnp.sum(lifted, axis=1, keepdims=True)
-        gate_grad_ref[...] = jnp.zeros_like(gate_grad_ref)
-        total[...] = jnp.zeros_like(total)
-
-    spot = spot_ref[pl.ds(step, 1), :]
+    logits = dot_tt(mix, router_ref[...])
+    masked = jnp.where(lane < experts, logits, NEGATIVE)
+    lifted = jnp.exp(masked - jnp.max(masked, axis=1, keepdims=True))
+    probs = lifted / jnp.sum(lifted, axis=1, keepdims=True)
     kept = kept_ref[...].astype(F32)
-    gate = jnp.sum(probs_ref[...] * kept * spot, axis=1, keepdims=True)
-    switch = jax.nn.sigmoid(jnp.sum(logits_ref[...] * spot, axis=1, keepdims=True))
-    routed = step < local
-    scale = jnp.where(routed, gate, switch)
-    weight = weight_ref[...]
-    lin = dot_tt(mix, weight)
-    gate_lin, up_lin = lin[:, :width], lin[:, width:]
-    logistic = jax.nn.sigmoid(gate_lin)
-    silu = gate_lin * logistic
-    hidden = silu * up_lin
-    hidden_grad = hidden_grad_ref[...]
-    row_sum = jnp.sum(hidden * hidden_grad, axis=1, keepdims=True)
-    factor = jnp.where(routed, jnp.sum(kept * spot, axis=1, keepdims=True), switch * (1.0 - switch))
-    gate_grad_ref[...] += row_sum * factor * spot
-    hidden_ref[...] = (scale * hidden).astype(BF16)
-    scaled = scale * hidden_grad
-    lin_grad_ref[:, :width] = (
-        scaled * up_lin * logistic * (1.0 + gate_lin * (1.0 - logistic))
+    grads = jnp.zeros(kept_ref.shape, F32)
+    for step in range(local + 1):
+        spot = spot_ref[step : step + 1, :]
+        if step < local:
+            factor = jnp.sum(kept * spot, axis=1, keepdims=True)
+            scale = jnp.sum(probs * kept * spot, axis=1, keepdims=True)
+        else:
+            scale = jax.nn.sigmoid(jnp.sum(logits * spot, axis=1, keepdims=True))
+            factor = scale * (1.0 - scale)
+        at = step * pair
+        lin = dot_tt(mix, weight_ref[at : at + pair, :])
+        gate_lin, up_lin = lin[:, :width], lin[:, width:]
+        logistic = jax.nn.sigmoid(gate_lin)
+        silu = gate_lin * logistic
+        hidden = silu * up_lin
+        hidden_grad = hidden_grad_ref[:, step * width : (step + 1) * width]
+        row_sum = jnp.sum(hidden * hidden_grad, axis=1, keepdims=True)
+        grads += row_sum * factor * spot
+        hidden_ref[:, step * width : (step + 1) * width] = (scale * hidden).astype(BF16)
+        scaled = scale * hidden_grad
+        lin_grad_ref[:, at : at + width] = (
+            scaled * up_lin * (logistic + silu * (1.0 - logistic))
+        ).astype(BF16)
+        lin_grad_ref[:, at + width : at + pair] = (scaled * silu).astype(BF16)
+    routed_grads = jnp.where(lane < experts, grads, 0.0)
+    inner = jnp.sum(probs * routed_grads, axis=1, keepdims=True)
+    small = jnp.where(lane < experts, probs * (grads - inner), grads).astype(BF16)
+    small_ref[...] = small
+    part_ref[...] = (
+        dot(lin_grad_ref[...], weight_ref[...]) + dot(small, router_ref[...])
     ).astype(BF16)
-    lin_grad_ref[:, width:] = (scaled * silu).astype(BF16)
-    total[...] += dot(lin_grad_ref[...], weight)
-
-    @pl.when(step == local)
-    def _():
-        grads = gate_grad_ref[...]
-        probs = probs_ref[...]
-        routed_grads = jnp.where(lane < experts, grads, 0.0)
-        inner = jnp.sum(probs * routed_grads, axis=1, keepdims=True)
-        small = jnp.where(lane < experts, probs * (grads - inner), grads).astype(BF16)
-        small_ref[...] = small
-        part_ref[...] = (total[...] + dot(small, router_ref[...])).astype(BF16)
 
 
 def mixture(mix, hidden_grad, kept, spot, router, weight, rows, experts, local):
     tokens, depth = mix.shape
-    steps = local + 1
-    pair = weight.shape[0] // steps
-    width = pair // 2
-    whole = lambda shape: pl.BlockSpec(shape, lambda i, j: (0, 0))
-    by_row = lambda size: pl.BlockSpec((rows, size), lambda i, j: (i, 0))
-    by_both = lambda size: pl.BlockSpec((rows, size), lambda i, j: (i, j))
+    units = weight.shape[0]
+    once = lambda shape: pl.BlockSpec(shape, lambda i: (0, 0), pipeline_mode=pl.Buffered(1))
+    by_row = lambda size: pl.BlockSpec((rows, size), lambda i: (i, 0))
     return pl.pallas_call(
         functools.partial(mixture_kernel, experts=experts, local=local),
-        grid=(tokens // rows, steps),
+        grid=(tokens // rows,),
         in_specs=[
             by_row(depth),
-            by_both(width),
+            by_row(units // 2),
             by_row(LANES),
-            whole(spot.shape),
-            whole((LANES, depth)),
-            pl.BlockSpec((pair, depth), lambda i, j: (j, 0)),
-        ],
-        out_specs=[by_both(pair), by_both(width), by_row(LANES), by_row(depth)],
+            once(spot.shape),
+            once((LANES, depth)),
+            once((units, depth)),
+        ],
+        out_specs=[by_row(units), by_row(units // 2), by_row(LANES), by_row(depth)],
         out_shape=[
-            jax.ShapeDtypeStruct((tokens, steps * pair), BF16),
-            jax.ShapeDtypeStruct((tokens, steps * width), BF16),
+            jax.ShapeDtypeStruct((tokens, units), BF16),
+            jax.ShapeDtypeStruct((tokens, units // 2), BF16),
             jax.ShapeDtypeStruct((tokens, LANES), BF16),
             jax.ShapeDtypeStruct((tokens, depth), BF16),
         ],
-        scratch_shapes=[
-            pltpu.VMEM((rows, depth), F32),
-            pltpu.VMEM((rows, LANES), F32),
-            pltpu.VMEM((rows, LANES), F32),
-            pltpu.VMEM((rows, LANES), F32),
-        ],
-        compiler_params=pltpu.CompilerParams(vmem_limit_bytes=56 << 20),
+        compiler_params=pltpu.CompilerParams(vmem_limit_bytes=60 << 20),
         cost_estimate=pl.CostEstimate(
-            flops=5 * tokens * depth * steps * pair, bytes_accessed=80 << 20, transcendentals=0
+            flops=5 * tokens * depth * units, bytes_accessed=80 << 20, transcendentals=0
         ),
     )(mix, hidden_grad, kept, spot, router, weight)
 
@@ -556,7 +533,6 @@
     output_here = lax.all_gather(
         after(output_weight, kv), ("dp", "expert"), axis=0, tiled=True
     )
-    heads_low, log_sums = attend(place, queries, kv, heads_here, score_scale)
 
     (
         route_block, upstream_source, gate_source, up_source, down_source, shared_source, small_source,
@@ -575,6 +551,8 @@
         return lax.dynamic_slice_in_dim(shared_own, block * shared_units, shared_units, axis=1)
 
     shared_pieces = links.swaps([after(units_of(block_at ^ s), kv) for s in range(1, groups)], "expert")
+
+    heads_low, log_sums = attend(place, queries, kv, heads_here, score_scale)
 
     expert_ids = jnp.arange(experts, dtype=jnp.int32)
     chosen = jnp.any(route_block[:, :, None] == expert_ids[None, None, :], axis=1) & live_rows[:, None]
@@ -641,14 +619,11 @@
             )
     hidden_grads = dot_tt(upstream_all, down_weight)
 
-    output_full = lax.all_gather(
-        after(output_weight, (mix_all, hidden_grads)), ("dp", "expert", "tensor"), axis=0, tiled=True
-    )
     lin_grads, hiddens, smalls, mix_part = mixture(
         after(mix_all, hidden_grads), hidden_grads, kept_all, spot, small_weight, lin_weight,
         rows, experts, local,
     )
-    mix_sum = lax.psum_scatter(after(mix_part, output_full), ("expert", "tensor"), scatter_dimension=0, tiled=True)
+    mix_sum = lax.psum_scatter(mix_part, ("expert", "tensor"), scatter_dimension=0, tiled=True)
 
     expert_rows = local * width
     down_grad = dot_nt(hiddens[:, :expert_rows], upstream_all).astype(BF16)
@@ -682,25 +657,24 @@
 
     lin_parts = []
     for j in range(local):
-        found = dot_nt(after(lin_grads[:, j * pair : (j + 1) * pair], shared_part), mix_all).astype(BF16)
+        earlier_ones = (shared_part, tuple(down_arrived)) if j == local - 1 else (shared_part,)
+        found = dot_nt(after(lin_grads[:, j * pair : (j + 1) * pair], earlier_ones), mix_all)
+        found = found.astype(BF16)
         lin_parts.append(
             jnp.concatenate([found[:expert_units], found[width : width + expert_units]], axis=0)
         )
-    lin_part = jnp.concatenate(lin_parts, axis=0)
-    shared_halves = [half_of(shared_part, (slot_at + k) % slots) for k in range(1, slots)]
-    ring = [[(i, (i + k) % slots) for i in range(slots)] for k in range(1, slots)]
-    arrived = links.send("x", shared_halves + [lin_part] * (slots - 1), "dp", ring * 2)
-    shared_arrived, lin_arrived = arrived[: slots - 1], arrived[slots - 1 :]
+    shared_arrived = links.shifts(
+        [half_of(shared_part, (slot_at + k) % slots) for k in range(1, slots)], "dp"
+    )
+    lin_arrived = [over_slots(part) for part in lin_parts]
     small_grad = dot_nt(after(smalls, down_parts), mix_all)[: experts + 1]
-    small_total = sum_over_all(small_grad.reshape(-1), everyone).reshape(experts + 1, depth)
 
     output_part = dot(after(hiddens, down_parts), down_weight).astype(BF16)
     output_part = output_part.reshape(groups, rows, depth)
 
-    output_full = output_full.reshape(slots * groups, tensors, depth // (slots * groups), wide)
-    output_full = output_full.transpose(0, 2, 1, 3).reshape(depth, tensors * wide)
-    mix_sum, output_part, lin_own, shared_own_part, output_full = together(
-        after(mix_sum, (tuple(down_arrived), small_grad)), output_part, lin_part, shared_part, output_full
+    output_part = links.scatter(output_part, "expert", 1, 2)
+    mix_sum, output_part, lin_parts, shared_own_part = together(
+        after(mix_sum, small_grad), output_part, tuple(lin_parts), shared_part
     )
     mix_grad = mix_sum.astype(F32)
     down_total = total(down_parts, after(tuple(down_arrived), mix_sum))
@@ -715,25 +689,22 @@
     )
     attended_grad = residual_grad.astype(BF16)
     attended_all = lax.all_gather(attended_grad, "tensor", axis=0, tiled=True)
-    heads_grad_rows = dot(attended_grad, output_full).astype(BF16)
-
-    def heads_of(index):
-        return lax.dynamic_slice_in_dim(heads_grad_rows, index * wide, wide, axis=1)
-
-    grads_in = [heads_of(tensor_at)] + links.shifts(
-        [heads_of(ahead[k]) for k in range(1, tensors)], "tensor"
-    )
-
-    heads_grad = in_order(grads_in, behind, 0)
+    output_part = links.scatter(output_part, "expert", 2, groups)[0]
+    attended_all, output_part = together(after(attended_all, tuple(shared_arrived)), output_part)
+    heads_grad = dot(attended_all, output_here).astype(BF16)
+
+    mine = [rows_of(output_part, tensor_at)] + links.shifts(
+        [rows_of(output_part, ahead[k]) for k in range(1, tensors)], "tensor"
+    )
     query_grads, kv_grads = attend_back(
         place, queries, heads_grad, heads_low, log_sums, kv, heads_here, score_scale
     )
     kv_sum = lax.psum_scatter(kv_grads, "expert", scatter_dimension=0, tiled=True)
     pre_grad, bias_grad = turn_back(
-        query_grads, kv_sum, cosine_table, sine_table)
+        query_grads, after(kv_sum, tuple(mine)), cosine_table, sine_table)
     normed_part = dot_tt(pre_grad, qkv_full).astype(BF16)
     normed_sum = lax.psum_scatter(normed_part, "tensor", scatter_dimension=0, tiled=True)
-    normed_grad = after(normed_sum, tuple(arrived)).astype(F32)
+    normed_grad = normed_sum.astype(F32)
     inverse_own = rows_of(inverse_one, tensor_at)
     scaled_one = normed_grad * gain_one
     attention_gain_grad = jnp.sum(normed_grad * inputs_own * inverse_own, axis=0)
@@ -745,10 +716,14 @@
     input_low = input_grad.astype(BF16)
     input_all = lax.all_gather(input_low, "tensor", axis=0, tiled=True)
 
-    shared_sum = total(half_of(shared_own_part, slot_at), after(tuple(shared_arrived), input_low))
+    shared_sum = total(half_of(shared_own_part, slot_at), after(tuple(shared_arrived), pre_grad))
     shared_sum = shared_sum.astype(BF16).reshape(3, shared_units, depth // slots)
-    lin_total = total(lin_own, after(tuple(lin_arrived), input_low))
-    lin_total = lin_total.reshape(local, 2, expert_units, depth)
+    lin_total = jnp.stack(
+        [
+            total(part, after(tuple(found), input_low)).reshape(2, expert_units, depth)
+            for part, found in zip(lin_parts, lin_arrived)
+        ]
+    )
 
     input_grad = input_all.astype(F32)
     own = depth // (slots * groups)
@@ -770,26 +745,18 @@
         weight_grads.append(
             jnp.concatenate(
                 [
-                    dot_nt(columns_for(normed, part), after(pre_grad, normed_part)).astype(BF16),
+                    dot_nt(
+                        columns_for(normed, part), after(pre_grad, (normed_part, tuple(lin_arrived[0])))
+                    ).astype(BF16),
                     dot_nt(columns_for(attended_all, part), heads_low).astype(BF16),
                 ],
                 axis=1,
             )
         )
 
-    output_part = links.scatter(output_part, "expert", kv_sum)
-    mine = [rows_of(output_part, tensor_at)] + links.shifts(
-        [rows_of(output_part, ahead[k]) for k in range(1, tensors)], "tensor"
-    )
-    mixed = sum(s.astype(F32) for s in after(tuple(mine), input_low))
+    mixed = sum(s.astype(F32) for s in mine)
     output_own = jnp.where(live_own, residual + mixed, 0.0).astype(BF16)
     layer_output = lax.all_gather(after(output_own, input_all), "tensor", axis=0, tiled=True)
-
-    weight_grad = links.collect(*weight_grads, "expert")
-    weight_grads = [weight_grad[k * own : (k + 1) * own] for k in range(slots)]
-    weight_grad = sum(
-        p.astype(F32) for p in [weight_grads[0]] + links.shifts(weight_grads[1:], "dp")
-    )
 
     def owned_by(block):
         return lax.dynamic_slice_in_dim(shared_sum, block * own_rows, own_rows, axis=2)
@@ -803,10 +770,21 @@
         jnp.zeros((tensors * 3 * wide,), F32), bias_grad[0], tensor_at * 3 * wide, axis=0
     )
     last_sums = sum_over_all(
-        jnp.concatenate([attention_gain_grad, mixture_gain_grad, bias_place]), everyone
-    )
+        jnp.concatenate(
+            [attention_gain_grad, mixture_gain_grad, small_grad.reshape(-1), bias_place]
+        ),
+        everyone,
+    )
+    weight_grad = links.meet(weight_grads[0], after(weight_grads[1], input_low), "expert", 1)
+    weight_grad = links.collect(*halves_of(weight_grad), "expert", low=2)
+    weight_grads = [weight_grad[k * own : (k + 1) * own] for k in range(slots)]
+    weight_grad = sum(
+        p.astype(F32) for p in [weight_grads[0]] + links.shifts(weight_grads[1:], "dp")
+    )
+
+    small_total = last_sums[2 * depth : (3 + experts) * depth].reshape(experts + 1, depth)
     bias_total = lax.dynamic_slice_in_dim(
-        last_sums, 2 * depth + tensor_at * 3 * wide, 3 * wide, axis=0
+        last_sums, (3 + experts) * depth + tensor_at * 3 * wide, 3 * wide, axis=0
     )
     return (
         layer_output[None],

time: 872 us -> 814 us (0.933)
  local copies, waits for them, and re-layouts: 129 us -> 89 us
  starting transfers between devices: 50 us -> 27.6 us
  waiting for transfers between devices: 374 us -> 396 us
  Pallas kernels: 94 us -> 77.2 us
    ppermute x25 -> x23, waiting for transfers between devices: 108 us -> 238 us  [send(): arrived = tuple((lax.ppermute(v, axis, p) for v, p in zip(values, perms)))]
    ppermute x10 -> x5, waiting for transfers between devices: 90.3 us -> 9.33 us  [sum_over_all(): lax.ppermute(value, axis, [(i, i ^ bit) for i in range(size)])]
    reduce_scatter x1, waiting for transfers between devices: 47.4 us -> 9.73 us  [shards(): lax.psum_scatter(kv_grads, 'expert', scatter_dimension=0, tiled=True)]
    ppermute x25 -> x23, starting transfers between devices: 35.9 us -> 19.3 us  [send(): arrived = tuple((lax.ppermute(v, axis, p) for v, p in zip(values, perms)))]
    reshape x1 -> x0, local copies, waits for them, and re-layouts: 15 us -> none  [shards(): output_full.reshape(slots * groups, tensors, depth // (slots * groups), w...]
    pallas_call x1, Pallas kernels: 69.1 us -> 56 us  [mixture(): pl.pallas_call(functools.partial(mixture_kernel, experts=experts, local=l...]
    unnamed x172 -> x141, local copies, waits for them, and re-layouts: 40.2 us -> 28.4 us
    reduce_scatter x1, waiting for transfers between devices: 5.77 us -> 17 us  [shards(): lax.psum_scatter(mix_part, ('expert', 'tensor'), scatter_dimension=0, til...]
  transfers between devices with their start and end apart: 47 -> 39, of which waited for: 24 -> 24; matrix products, arithmetic and copies ran while one was open for 34% -> 27% of each run, Pallas kernels for 10% -> 1%
where the time goes in v3:
time: 814 us; the launch traced here: 801 us
  waiting for transfers between devices  396 us (49%)
  other arithmetic  98.2 us (12%)
  matrix products  97.6 us (12%)
  local copies, waits for them, and re-layouts  89 us (11%)
  Pallas kernels  77.2 us (9%)
  starting transfers between devices  27.6 us (3%)
  between operations  15.9 us (2%)
    ppermute x23, waiting for transfers between devices, send(): arrived = tuple((lax.ppermute(v, axis, p) for v, p in zip(values, perms)))  238 us
    pallas_call x1, Pallas kernels, mixture(): pl.pallas_call(functools.partial(mixture_kernel, experts=experts, local=l...  56 us
    dot_general x10, matrix products, dot_nt(): lax.dot_general(a, b, (((0,), (0,)), ((), ())), preferred_element_type=F32)  54.6 us
    all_gather x1, waiting for transfers between devices, shards(): lax.all_gather(jnp.concatenate([query_weight, key_weight, value_weight],...  45.5 us
    all_gather x1, waiting for transfers between devices, shards(): kv = lax.all_gather(kv_own, 'expert', axis=0, tiled=True)  34.6 us
    unnamed x141, local copies, waits for them, and re-layouts  28.4 us
    dot_general x3, matrix products, dot_tt(): lax.dot_general(a, b, (((1,), (1,)), ((), ())), preferred_element_type=F32)  25.3 us
    all_gather x1, waiting for transfers between devices, shards(): mix_all = lax.all_gather(mix_own, ('expert', 'tensor'), axis=0, tiled=True)  22.5 us
  transfers between devices with their start and end apart: 39, of which 24 were waited for; matrix products, arithmetic and copies ran while one was open for 27% of the time, Pallas kernels for 1%

profile of v3, /device:TPU:0, one launch (start us, length us, event | category | flops | bytes accessed | tf_op | source)
XLA Modules:
  0.0 801.4 jit_solution(14162756442565786310)
XLA Ops:
  13.3 45.5 %all-gather.8.cloned.1.call-done.wq_ref.wk_ref.wv_ref = bf16[2048,1536]{1,0:T(8,128)(2,1)} async-done(((bf16[256,1536]{1,0:T(8,128)(2,1)}), bf16[2048,1536]{1,0:T(8,128)(2,1)}) %all-gather.8.cloned.1.call-update) | async-done | bytes 6291472 | tf_op jit(solution)/shard_map/all_gather | solution.py:521
  66.9 34.6 %all-gather.10.cloned.1.call-done.kv_ref = bf16[2048,1024]{1,0:T(8,128)(2,1)} async-done(((bf16[512,1024]{1,0:T(8,128)(2,1)}), bf16[2048,1024]{1,0:T(8,128)(2,1)}) %all-gather.10.cloned.1.call-update) | async-done | bytes 4194320 | tf_op jit(solution)/shard_map/all_gather | solution.py:532
  119.7 9.3 %collective-permute-done.2 = bf16[3,352,256]{2,1,0:T(8,128)(2,1)S(1)} collective-permute-done((bf16[3,352,256]{2,1,0:T(8,128)(2,1)S(1)}, bf16[3,352,256]{2,1,0:T(8,128)(2,1)S(1)}, u32[]{:S(2)}, u32[]{:S(2)}) %collective-permute-start.2) | collective-permute-done | bytes 540704 | tf_op jit(solution)/shard_map/over_y/ppermute | solution.py:49
  129.8 15.5 %collective-permute-done.1 = bf16[3,352,256]{2,1,0:T(8,128)(2,1)S(1)} collective-permute-done((bf16[3,352,256]{2,1,0:T(8,128)(2,1)S(1)}, bf16[3,352,256]{2,1,0:T(8,128)(2,1)S(1)}, u32[]{:S(2)}, u32[]{:S(2)}) %collective-permute-start.1) | collective-permute-done | bytes 540704 | tf_op jit(solution)/shard_map/over_y/ppermute | solution.py:49
  167.1 35.3 %collective-permute-done.4 = bf16[512,2048]{1,0:T(8,128)(2,1)} collective-permute-done((bf16[512,2048]{1,0:T(8,128)(2,1)}, bf16[512,2048]{1,0:T(8,128)(2,1)}, u32[]{:S(2)}, u32[]{:S(2)}) %collective-permute-start.4) | collective-permute-done | bytes 2097184 | tf_op jit(solution)/shard_map/over_y/ppermute | solution.py:49
  227.6 7.6 fusion.8
  253.4 13.3 %fusion.88.hidden_grad_ref = f32[2048,1152]{1,0:T(8,128)} fusion(bf16[2048,2048]{1,0:T(8,128)(2,1)S(1)} %slice_dynamic-update-slice_fusion, bf16[1152,2048]{1,0:T(8,128)(2,1)S(1)} %get-tuple-element.192), kind=kOutput, calls=%fused_computation.222 | convolution fusion | flops 9663676416 | bytes 22544384 | tf_op jit(solution)/shard_map/dot_general | solution.py:155
  266.7 22.5 %all-gather.14.cloned.1.call-done.mix_ref = bf16[2048,2048]{1,0:T(8,128)(2,1)} async-done(((bf16[128,2048]{1,0:T(8,128)(2,1)}), bf16[2048,2048]{1,0:T(8,128)(2,1)}) %all-gather.14.cloned.1.call-update) | async-done | bytes 8388624 | tf_op jit(solution)/shard_map/all_gather | solution.py:602
  289.2 56.0 %shard_map.350 = (bf16[2048,2304]{1,0:T(8,128)(2,1)}, bf16[2048,1152]{1,0:T(8,128)(2,1)}, bf16[2048,128]{1,0:T(8,128)(2,1)}, bf16[2048,2048]{1,0:T(8,128)(2,1)}) custom-call(bf16[2048,2048]{1,0:T(8,128)(2,1)} %all-gather.14.cloned.1.call-done.mix_ref, f32[2048,1152]{1,0:T(8,128)} %fusion.88.hidden_grad_ref, bf16[2048,128]{1,0:T(8,128)(2,1)} %copy-done.45, ...), custom_call_target="tpu_custom_call" | custom-call | flops 48318382080 | bytes 83886080 | tf_op jit(solution)/shard_map/pallas_call | solution.py:442
  345.2 10.1 %convolution_convert_fusion.6 = bf16[768,2048]{1,0:T(8,128)(2,1)S(1)} fusion(bf16[2048,2048]{1,0:T(8,128)(2,1)} %copy-done.30, bf16[2048,1152]{1,0:T(8,128)(2,1)} %get-tuple-element.119), kind=kOutput, calls=%fused_computation.38 | convolution fusion | flops 6444023808 | bytes 14680064 | tf_op jit(solution)/shard_map/dot_general | solution.py:159
  358.6 7.4 fusion.15
  367.7 11.0 %convolution_convert_fusion.5 = bf16[768,2048]{1,0:T(8,128)(2,1)S(1)} fusion(bf16[2048,2048]{1,0:T(8,128)(2,1)} %all-gather.14.cloned.1.call-done.mix_ref, bf16[2048,2304]{1,0:T(8,128)(2,1)} %get-tuple-element.120), kind=kOutput, calls=%fused_computation.37 | convolution fusion | flops 6444023808 | bytes 14680064 | tf_op jit(solution)/shard_map/dot_general | solution.py:159
  381.4 6.2 fusion.80
  387.7 13.7 %convolution_convert_fusion = bf16[2048,2048]{1,0:T(8,128)(2,1)S(1)} fusion(bf16[2048,1152]{1,0:T(8,128)(2,1)} %get-tuple-element.119, bf16[1152,2048]{1,0:T(8,128)(2,1)S(1)} %bitcast.129), kind=kOutput, calls=%fused_computation.11 | convolution fusion | flops 9667870720 | bytes 17825792 | tf_op jit(solution)/shard_map/dot_general | solution.py:163
  403.3 8.7 %convolution_convert_fusion.4 = bf16[768,2048]{1,0:T(8,128)(2,1)} fusion(bf16[2048,768]{1,0:T(8,128)(2,1)S(1)} %copy-done.34, bf16[2048,2048]{1,0:T(8,128)(2,1)S(1)} %bitcast.121), kind=kOutput, calls=%fused_computation.36 | convolution fusion | flops 6444023808 | bytes 14680064 | tf_op jit(solution)/shard_map/dot_general | solution.py:159
  417.1 14.1 %collective-permute-done.9 = bf16[704,2048]{1,0:T(8,128)(2,1)} collective-permute-done((bf16[704,2048]{1,0:T(8,128)(2,1)}, bf16[704,2048]{1,0:T(8,128)(2,1)}, u32[]{:S(2)}, u32[]{:S(2)}) %collective-permute-start.9) | collective-permute-done | bytes 2883616 | tf_op jit(solution)/shard_map/over_x/ppermute | solution.py:49
  431.2 7.1 convolution_convert_fusion.3
  444.5 17.0 %reduce-scatter.7.cloned.1.call-done = bf16[128,2048]{1,0:T(8,128)(2,1)} async-done(((bf16[2048,2048]{1,0:T(8,128)(2,1)}), bf16[128,2048]{1,0:T(8,128)(2,1)}) %reduce-scatter.7.cloned.1.call-update) | async-done | bytes 524304 | tf_op jit(solution)/shard_map/reduce_scatter | solution.py:626
  475.9 41.7 %collective-permute-done.11 = bf16[1,512,2048]{2,1,0:T(8,128)(2,1)} collective-permute-done((bf16[1,512,2048]{2,1,0:T(8,128)(2,1)}, bf16[1,512,2048]{2,1,0:T(8,128)(2,1)}, u32[]{:S(2)}, u32[]{:S(2)}) %collective-permute-start.11) | collective-permute-done | bytes 2097184 | tf_op jit(solution)/shard_map/over_y/ppermute | solution.py:49
  526.9 7.8 shard_map.351
  542.7 11.0 %collective-permute-done.12 = bf16[128,2048]{1,0:T(8,128)(2,1)S(1)} collective-permute-done((bf16[128,2048]{1,0:T(8,128)(2,1)S(1)}, bf16[128,2048]{1,0:T(8,128)(2,1)S(1)}, u32[]{:S(2)}, u32[]{:S(2)}) %collective-permute-start.12) | collective-permute-done | bytes 524320 | tf_op jit(solution)/shard_map/over_z/ppermute | solution.py:49
  553.7 22.9 %collective-permute-done.13 = bf16[128,2048]{1,0:T(8,128)(2,1)S(1)} collective-permute-done((bf16[128,2048]{1,0:T(8,128)(2,1)S(1)}, bf16[128,2048]{1,0:T(8,128)(2,1)S(1)}, u32[]{:S(2)}, u32[]{:S(2)}) %collective-permute-start.13) | collective-permute-done | bytes 524320 | tf_op jit(solution)/shard_map/over_z/ppermute | solution.py:49
  578.9 9.7 %reduce-scatter.9.cloned.1.call-done.dkv_ref = bf16[512,1024]{1,0:T(8,128)(2,1)} async-done(((bf16[2048,1024]{1,0:T(8,128)(2,1)}), bf16[512,1024]{1,0:T(8,128)(2,1)}) %reduce-scatter.9.cloned.1.call-update) | async-done | bytes 1048592 | tf_op jit(solution)/shard_map/reduce_scatter | solution.py:702
  593.1 7.6 convolution_convert_fusion.7
  606.2 59.2 %collective-permute-done.20 = bf16[704,2048]{1,0:T(8,128)(2,1)} collective-permute-done((bf16[704,2048]{1,0:T(8,128)(2,1)}, bf16[704,2048]{1,0:T(8,128)(2,1)}, u32[]{:S(2)}, u32[]{:S(2)}) %collective-permute-start.20) | collective-permute-done | bytes 2883616 | tf_op jit(solution)/shard_map/over_x/ppermute | solution.py:49
  691.8 9.1 %collective-permute-done.22.refs_2_ = bf16[3,352,256]{2,1,0:T(8,128)(2,1)S(1)} collective-permute-done((bf16[3,352,256]{2,1,0:T(8,128)(2,1)S(1)}, bf16[3,352,256]{2,1,0:T(8,128)(2,1)S(1)}, u32[]{:S(2)}, u32[]{:S(2)}) %collective-permute-start.22) | collective-permute-done | bytes 540704 | tf_op jit(solution)/shard_map/over_y/ppermute | solution.py:49
  706.6 8.9 %collective-permute-done.23.refs_3_ = bf16[3,352,256]{2,1,0:T(8,128)(2,1)S(1)} collective-permute-done((bf16[3,352,256]{2,1,0:T(8,128)(2,1)S(1)}, bf16[3,352,256]{2,1,0:T(8,128)(2,1)S(1)}, u32[]{:S(2)}, u32[]{:S(2)}) %collective-permute-start.23) | collective-permute-done | bytes 540704 | tf_op jit(solution)/shard_map/over_y/ppermute | solution.py:49
  716.0 5.5 convert_add_fusion.1
  725.8 8.9 %all-gather.18.cloned.1.call-done = bf16[512,2048]{1,0:T(8,128)(2,1)} async-done(((bf16[128,2048]{1,0:T(8,128)(2,1)}), bf16[512,2048]{1,0:T(8,128)(2,1)}) %all-gather.18.cloned.1.call-update) | async-done | bytes 2097168 | tf_op jit(solution)/shard_map/all_gather | solution.py:717
  747.9 7.4 collective-permute-done.18
  757.9 5.1 collective-permute-done.24
  776.9 9.8 %all-gather.20.cloned.1.call-done = bf16[512,2048]{1,0:T(8,128)(2,1)} async-done(((bf16[128,2048]{1,0:T(8,128)(2,1)}), bf16[512,2048]{1,0:T(8,128)(2,1)}) %all-gather.20.cloned.1.call-update) | async-done | bytes 2097168 | tf_op jit(solution)/shard_map/all_gather | solution.py:759
  (338 shorter events, 235.9 us)
Async XLA Ops:
  7.2 51.6 %all-gather.8.cloned.1.call-start = ((), (), s32[]{:S(2)}) async-start(), calls=%async_computation.4 | async-start | bytes 7077888 | tf_op jit(solution)/shard_map/all_gather | solution.py:521
  9.5 92.1 %all-gather.10.cloned.1.call-start = ((), (), s32[]{:S(2)}) async-start(), calls=%async_computation.5 | async-start | bytes 5242880 | tf_op jit(solution)/shard_map/all_gather | solution.py:532
  66.9 80.0 %all-gather.12.cloned.1.call-start = ((), (), s32[]{:S(2)}) async-start(), calls=%async_computation.6 | async-start | bytes 2359296 | tf_op jit(solution)/shard_map/all_gather | solution.py:533
  101.5 106.1 %reduce-scatter.5.cloned.1.call-start = ((), (), s32[]{:S(2)}) async-start(), calls=%async_computation.7 | async-start | bytes 2621440 | tf_op jit(solution)/shard_map/reduce_scatter | solution.py:594
  110.8 18.2 %collective-permute-start.2 = (bf16[3,352,256]{2,1,0:T(8,128)(2,1)S(1)}, bf16[3,352,256]{2,1,0:T(8,128)(2,1)S(1)}, u32[]{:S(2)}, u32[]{:S(2)}) collective-permute-start(bf16[3,352,256]{2,1,0:T(8,128)(2,1)S(1)} %get-tuple-element.96), channel_id=1, source_target_pairs={{0,12},{4,8},{8,4},{12,0},{1,13},{5,9},{9,5},{13,1},{2,14},{6,10},... | collective-permute-start | bytes 1622024 | tf_op jit(solution)/shard_map/over_y/ppermute | solution.py:49
  111.0 34.2 %collective-permute-start.1 = (bf16[3,352,256]{2,1,0:T(8,128)(2,1)S(1)}, bf16[3,352,256]{2,1,0:T(8,128)(2,1)S(1)}, u32[]{:S(2)}, u32[]{:S(2)}) collective-permute-start(bf16[3,352,256]{2,1,0:T(8,128)(2,1)S(1)} %get-tuple-element.95), channel_id=1, source_target_pairs={{0,8},{4,12},{8,0},{12,4},{1,9},{5,13},{9,1},{13,5},{2,10},{6,14},... | collective-permute-start | bytes 1622024 | tf_op jit(solution)/shard_map/over_y/ppermute | solution.py:49
  112.8 33.3 %collective-permute-start = (bf16[3,352,256]{2,1,0:T(8,128)(2,1)S(1)}, bf16[3,352,256]{2,1,0:T(8,128)(2,1)S(1)}, u32[]{:S(2)}, u32[]{:S(2)}) collective-permute-start(bf16[3,352,256]{2,1,0:T(8,128)(2,1)S(1)} %get-tuple-element.94), channel_id=1, source_target_pairs={{0,4},{4,0},{8,12},{12,8},{1,5},{5,1},{9,13},{13,9},{2,6},{6,2},{1... | collective-permute-start | bytes 1622024 | tf_op jit(solution)/shard_map/over_y/ppermute | solution.py:49
  151.3 137.9 %all-gather.14.cloned.1.call-start = ((), (), s32[]{:S(2)}) async-start(), calls=%async_computation.8 | async-start | bytes 8912896 | tf_op jit(solution)/shard_map/all_gather | solution.py:602
  154.5 47.9 %collective-permute-start.4 = (bf16[512,2048]{1,0:T(8,128)(2,1)}, bf16[512,2048]{1,0:T(8,128)(2,1)}, u32[]{:S(2)}, u32[]{:S(2)}) collective-permute-start(bf16[512,2048]{1,0:T(8,128)(2,1)} %broadcast_select_fusion), channel_id=1, source_target_pairs={{0,8},{4,12},{8,0},{12,4},{1,9},{5,13},{9,1},{13,5},{2,10},{6,14},... | collective-permute-start | bytes 6291464 | tf_op jit(solution)/shard_map/over_y/ppermute | solution.py:49
  160.6 49.0 %collective-permute-start.3 = (bf16[3,352,1024]{2,1,0:T(8,128)(2,1)}, bf16[3,352,1024]{2,1,0:T(8,128)(2,1)}, u32[]{:S(2)}, u32[]{:S(2)}) collective-permute-start(bf16[3,352,1024]{2,1,0:T(8,128)(2,1)} %constant_dynamic-update-slice_fusion), channel_id=1, source_target_pairs={{0,16},{16,0},{1,17},{17,1},{2,18},{18,2},{3,19},{19,3},{4,20},{20... | collective-permute-start | bytes 6488072 | tf_op jit(solution)/shard_map/over_x/ppermute | solution.py:49
  213.0 248.6 %reduce-scatter.7.cloned.1.call-start = ((), (), s32[]{:S(2)}) async-start(), calls=%async_computation.9 | async-start | bytes 8912896 | tf_op jit(solution)/shard_map/reduce_scatter | solution.py:626
  227.6 16.5 %collective-permute-start.6 = (bf16[1024,2048]{1,0:T(8,128)(2,1)S(1)}, bf16[1024,2048]{1,0:T(8,128)(2,1)}, u32[]{:S(2)}, u32[]{:S(2)}) collective-permute-start(bf16[1024,2048]{1,0:T(8,128)(2,1)S(1)} %copy-done.22), channel_id=1, source_target_pairs={{0,4},{4,0},{8,12},{12,8},{1,5},{5,1},{9,13},{13,9},{2,6},{6,2},{1... | collective-permute-start | bytes 12582920 | tf_op jit(solution)/shard_map/over_core/ppermute | solution.py:49
  358.6 164.7 %all-gather.16.cloned.1.call-start = ((), (), s32[]{:S(2)}) async-start(), calls=%async_computation.10 | async-start | bytes 2621440 | tf_op jit(solution)/shard_map/all_gather | solution.py:691
  366.2 65.0 %collective-permute-start.9 = (bf16[704,2048]{1,0:T(8,128)(2,1)}, bf16[704,2048]{1,0:T(8,128)(2,1)}, u32[]{:S(2)}, u32[]{:S(2)}) collective-permute-start(bf16[704,2048]{1,0:T(8,128)(2,1)} %pad_maximum_fusion.4), channel_id=1, source_target_pairs={{0,16},{16,0},{1,17},{17,1},{2,18},{18,2},{3,19},{19,3},{4,20},{20... | collective-permute-start | bytes 8650760 | tf_op jit(solution)/shard_map/over_x/ppermute | solution.py:49
  401.9 38.6 %collective-permute-start.8 = (bf16[2,512,2048]{2,1,0:T(8,128)(2,1)S(1)}, bf16[2,512,2048]{2,1,0:T(8,128)(2,1)S(1)}, u32[]{:S(2)}, u32[]{:S(2)}) collective-permute-start(bf16[2,512,2048]{2,1,0:T(8,128)(2,1)S(1)} %dynamic-slice_bitcast_fusion), channel_id=1, source_target_pairs={{0,4},{4,0},{8,12},{12,8},{1,5},{5,1},{9,13},{13,9},{2,6},{6,2},{1... | collective-permute-start | bytes 12582920 | tf_op jit(solution)/shard_map/over_core/ppermute | solution.py:49
  466.6 122.0 %reduce-scatter.9.cloned.1.call-start = ((), (), s32[]{:S(2)}) async-start(), calls=%async_computation.11 | async-start | bytes 5242880 | tf_op jit(solution)/shard_map/reduce_scatter | solution.py:702
  469.8 47.7 %collective-permute-start.11 = (bf16[1,512,2048]{2,1,0:T(8,128)(2,1)}, bf16[1,512,2048]{2,1,0:T(8,128)(2,1)}, u32[]{:S(2)}, u32[]{:S(2)}) collective-permute-start(bf16[1,512,2048]{2,1,0:T(8,128)(2,1)} %constant_dynamic-slice_fusion.24), channel_id=1, source_target_pairs={{0,8},{4,12},{8,0},{12,4},{1,9},{5,13},{9,1},{13,5},{2,10},{6,14},... | collective-permute-start | bytes 6291464 | tf_op jit(solution)/shard_map/over_y/ppermute | solution.py:49
  474.4 48.8 %collective-permute-start.10 = (bf16[1056,1024]{1,0:T(8,128)(2,1)}, bf16[1056,1024]{1,0:T(8,128)(2,1)}, u32[]{:S(2)}, u32[]{:S(2)}) collective-permute-start(bf16[1056,1024]{1,0:T(8,128)(2,1)} %constant_dynamic-slice_fusion.25), channel_id=1, source_target_pairs={{0,16},{16,0},{1,17},{17,1},{2,18},{18,2},{3,19},{19,3},{4,20},{20... | collective-permute-start | bytes 6488072 | tf_op jit(solution)/shard_map/over_x/ppermute | solution.py:49
  535.7 134.2 %reduce-scatter.11.cloned.1.call-start = ((), (), s32[]{:S(2)}) async-start(), calls=%async_computation.12 | async-start | bytes 2621440 | tf_op jit(solution)/shard_map/reduce_scatter | solution.py:706
  537.5 16.3 %collective-permute-start.12 = (bf16[128,2048]{1,0:T(8,128)(2,1)S(1)}, bf16[128,2048]{1,0:T(8,128)(2,1)S(1)}, u32[]{:S(2)}, u32[]{:S(2)}) collective-permute-start(bf16[128,2048]{1,0:T(8,128)(2,1)S(1)} %get-tuple-element.220), channel_id=1, source_target_pairs={{0,1},{1,2},{2,3},{3,0},{4,5},{5,6},{6,7},{7,4},{8,9},{9,10},{10,1... | collective-permute-start | bytes 1572872 | tf_op jit(solution)/shard_map/over_z/ppermute | solution.py:49
  539.0 37.6 %collective-permute-start.13 = (bf16[128,2048]{1,0:T(8,128)(2,1)S(1)}, bf16[128,2048]{1,0:T(8,128)(2,1)S(1)}, u32[]{:S(2)}, u32[]{:S(2)}) collective-permute-start(bf16[128,2048]{1,0:T(8,128)(2,1)S(1)} %get-tuple-element.222), channel_id=1, source_target_pairs={{0,2},{1,3},{2,0},{3,1},{4,6},{5,7},{6,4},{7,5},{8,10},{9,11},{10,... | collective-permute-start | bytes 1572872 | tf_op jit(solution)/shard_map/over_z/ppermute | solution.py:49
  540.4 36.2 %collective-permute-start.14 = (bf16[128,2048]{1,0:T(8,128)(2,1)S(1)}, bf16[128,2048]{1,0:T(8,128)(2,1)S(1)}, u32[]{:S(2)}, u32[]{:S(2)}) collective-permute-start(bf16[128,2048]{1,0:T(8,128)(2,1)S(1)} %get-tuple-element.221), channel_id=1, source_target_pairs={{0,3},{1,0},{2,1},{3,2},{4,7},{5,4},{6,5},{7,6},{8,11},{9,8},{10,9... | collective-permute-start | bytes 1572872 | tf_op jit(solution)/shard_map/over_z/ppermute | solution.py:49
  600.7 134.0 %all-gather.18.cloned.1.call-start = ((), (), s32[]{:S(2)}) async-start(), calls=%async_computation.13 | async-start | bytes 2621440 | tf_op jit(solution)/shard_map/all_gather | solution.py:717
  600.8 64.6 %collective-permute-start.20 = (bf16[704,2048]{1,0:T(8,128)(2,1)}, bf16[704,2048]{1,0:T(8,128)(2,1)}, u32[]{:S(2)}, u32[]{:S(2)}) collective-permute-start(bf16[704,2048]{1,0:T(8,128)(2,1)} %pad_maximum_fusion.5), channel_id=1, source_target_pairs={{0,16},{16,0},{1,17},{17,1},{2,18},{18,2},{3,19},{19,3},{4,20},{20... | collective-permute-start | bytes 8650760 | tf_op jit(solution)/shard_map/over_x/ppermute | solution.py:49
  674.7 27.4 %collective-permute-start.21 = (bf16[1024,2048]{1,0:T(8,128)(2,1)}, bf16[1024,2048]{1,0:T(8,128)(2,1)}, u32[]{:S(2)}, u32[]{:S(2)}) collective-permute-start(bf16[1024,2048]{1,0:T(8,128)(2,1)} %pad_maximum_fusion.3), channel_id=1, source_target_pairs={{0,4},{4,0},{8,12},{12,8},{1,5},{5,1},{9,13},{13,9},{2,6},{6,2},{1... | collective-permute-start | bytes 12582920 | tf_op jit(solution)/shard_map/over_core/ppermute | solution.py:49
  674.8 65.7 %collective-permute-start.25 = (bf16[704,2048]{1,0:T(8,128)(2,1)}, bf16[704,2048]{1,0:T(8,128)(2,1)}, u32[]{:S(2)}, u32[]{:S(2)}) collective-permute-start(bf16[704,2048]{1,0:T(8,128)(2,1)} %pad_maximum_fusion.6), channel_id=1, source_target_pairs={{0,16},{16,0},{1,17},{17,1},{2,18},{18,2},{3,19},{19,3},{4,20},{20... | collective-permute-start | bytes 8650760 | tf_op jit(solution)/shard_map/over_x/ppermute | solution.py:49
  683.7 102.9 %all-gather.20.cloned.1.call-start = ((), (), s32[]{:S(2)}) async-start(), calls=%async_computation.14 | async-start | bytes 2621440 | tf_op jit(solution)/shard_map/all_gather | solution.py:759
  687.0 34.5 %collective-permute-start.27 = (bf16[3,352,256]{2,1,0:T(8,128)(2,1)}, bf16[3,352,256]{2,1,0:T(8,128)(2,1)S(1)}, u32[]{:S(2)}, u32[]{:S(2)}) collective-permute-start(bf16[3,352,256]{2,1,0:T(8,128)(2,1)} %get-tuple-element.187), channel_id=1, source_target_pairs={{0,4},{4,0},{8,12},{12,8},{1,5},{5,1},{9,13},{13,9},{2,6},{6,2},{1... | collective-permute-start | bytes 1622024 | tf_op jit(solution)/shard_map/over_core/ppermute | solution.py:49
  700.9 24.4 %collective-permute-start.16 = (f32[28672]{0:T(1024)S(1)}, f32[28672]{0:T(1024)S(1)}, u32[]{:S(2)}, u32[]{:S(2)}) collective-permute-start(f32[28672]{0:T(1024)S(1)} %fusion.78), channel_id=1, source_target_pairs={{0,8},{4,12},{8,0},{12,4},{1,9},{5,13},{9,1},{13,5},{2,10},{6,14},... | collective-permute-start | bytes 344072 | tf_op jit(solution)/shard_map/ppermute | solution.py:114
  715.5 47.5 %collective-permute-start.24 = (bf16[512,2048]{1,0:T(8,128)(2,1)}, bf16[512,2048]{1,0:T(8,128)(2,1)}, u32[]{:S(2)}, u32[]{:S(2)}) collective-permute-start(bf16[512,2048]{1,0:T(8,128)(2,1)} %slice.248), channel_id=1, source_target_pairs={{0,8},{4,12},{8,0},{12,4},{1,9},{5,13},{9,1},{13,5},{2,10},{6,14},... | collective-permute-start | bytes 6291464 | tf_op jit(solution)/shard_map/over_y/ppermute | solution.py:49
  725.4 17.0 %collective-permute-start.17 = (f32[28672]{0:T(1024)S(1)}, f32[28672]{0:T(1024)S(1)}, u32[]{:S(2)}, u32[]{:S(2)}) collective-permute-start(f32[28672]{0:T(1024)S(1)} %add.408), channel_id=1, source_target_pairs={{0,16},{16,0},{1,17},{17,1},{2,18},{18,2},{3,19},{19,3},{4,20},{20... | collective-permute-start | bytes 344072 | tf_op jit(solution)/shard_map/ppermute | solution.py:114
  765.4 23.9 %collective-permute-start.26 = (bf16[256,2048]{1,0:T(8,128)(2,1)S(1)}, bf16[256,2048]{1,0:T(8,128)(2,1)}, u32[]{:S(2)}, u32[]{:S(2)}) collective-permute-start(bf16[256,2048]{1,0:T(8,128)(2,1)S(1)} %slice.250), channel_id=1, source_target_pairs={{0,16},{16,0},{1,17},{17,1},{2,18},{18,2},{3,19},{19,3},{4,20},{20... | collective-permute-start | bytes 3145736 | tf_op jit(solution)/shard_map/over_x/ppermute | solution.py:49
  (75 other events, 663.4 us)
Sparse Core Ops, SparseCore 0:
  10.5 48.2 all-gather.7
  67.0 34.4 all-gather.9
  103.4 36.4 all-gather.11
  151.4 43.8 reduce-scatter.4
  213.1 76.0 all-gather.13
  358.7 102.8 reduce-scatter.6
  466.7 45.6 all-gather.15
  535.9 52.7 reduce-scatter.8
  600.9 49.6 reduce-scatter.10
  683.9 50.8 all-gather.17
  736.9 49.6 all-gather.19

commit v4 on v3

--- a/solution.py
+++ b/solution.py
@@ -704,7 +704,15 @@
         query_grads, after(kv_sum, tuple(mine)), cosine_table, sine_table)
     normed_part = dot_tt(pre_grad, qkv_full).astype(BF16)
     normed_sum = lax.psum_scatter(normed_part, "tensor", scatter_dimension=0, tiled=True)
-    normed_grad = normed_sum.astype(F32)
+    shared_sum = total(half_of(shared_own_part, slot_at), after(tuple(shared_arrived), pre_grad))
+    shared_sum = shared_sum.astype(BF16).reshape(3, shared_units, depth // slots)
+    def owned_by(block):
+        return lax.dynamic_slice_in_dim(shared_sum, block * own_rows, own_rows, axis=2)
+
+    shared_back = [owned_by(block_at)] + [
+        links.swap(owned_by(block_at ^ s), "expert", s) for s in range(1, groups)
+    ]
+    normed_grad = after(normed_sum, tuple(shared_back[1:])).astype(F32)
     inverse_own = rows_of(inverse_one, tensor_at)
     scaled_one = normed_grad * gain_one
     attention_gain_grad = jnp.sum(normed_grad * inputs_own * inverse_own, axis=0)
@@ -713,11 +721,9 @@
         + inverse_own * scaled_one
         - inputs_own * inverse_own**3 * jnp.mean(scaled_one * inputs_own, axis=1, keepdims=True)
     )
-    input_low = input_grad.astype(BF16)
+    input_low, pre_later = together(input_grad.astype(BF16), pre_grad)
     input_all = lax.all_gather(input_low, "tensor", axis=0, tiled=True)
 
-    shared_sum = total(half_of(shared_own_part, slot_at), after(tuple(shared_arrived), pre_grad))
-    shared_sum = shared_sum.astype(BF16).reshape(3, shared_units, depth // slots)
     lin_total = jnp.stack(
         [
             total(part, after(tuple(found), input_low)).reshape(2, expert_units, depth)
@@ -746,7 +752,7 @@
             jnp.concatenate(
                 [
                     dot_nt(
-                        columns_for(normed, part), after(pre_grad, (normed_part, tuple(lin_arrived[0])))
+                        columns_for(normed, part), after(pre_later, tuple(lin_arrived[0]))
                     ).astype(BF16),
                     dot_nt(columns_for(attended_all, part), heads_low).astype(BF16),
                 ],
@@ -758,13 +764,8 @@
     output_own = jnp.where(live_own, residual + mixed, 0.0).astype(BF16)
     layer_output = lax.all_gather(after(output_own, input_all), "tensor", axis=0, tiled=True)
 
-    def owned_by(block):
-        return lax.dynamic_slice_in_dim(shared_sum, block * own_rows, own_rows, axis=2)
-
-    shared_back = [owned_by(block_at)] + [
-        links.swap(owned_by(block_at ^ s), "expert", s) for s in range(1, groups)
-    ]
     shared_grads = side_by_side(place, shared_back)
+
 
     bias_place = lax.dynamic_update_slice_in_dim(
         jnp.zeros((tensors * 3 * wide,), F32), bias_grad[0], tensor_at * 3 * wide, axis=0
@@ -775,7 +776,7 @@
         ),
         everyone,
     )
-    weight_grad = links.meet(weight_grads[0], after(weight_grads[1], input_low), "expert", 1)
+    weight_grad = links.meet(*weight_grads, "expert", 1)
     weight_grad = links.collect(*halves_of(weight_grad), "expert", low=2)
     weight_grads = [weight_grad[k * own : (k + 1) * own] for k in range(slots)]
     weight_grad = sum(

time: 814 us -> 804 us (0.988)
  waiting for transfers between devices: 396 us -> 386 us
    ppermute x23, waiting for transfers between devices: 238 us -> 197 us  [send(): arrived = tuple((lax.ppermute(v, axis, p) for v, p in zip(values, perms)))]
    reduce_scatter x1, waiting for transfers between devices: 0.01 us -> 15.9 us  [shards(): lax.psum_scatter(normed_part, 'tensor', scatter_dimension=0, tiled=True)]
    all_gather x1, waiting for transfers between devices: 8.92 us -> 24.1 us  [shards(): input_all = lax.all_gather(input_low, 'tensor', axis=0, tiled=True)]
    all_gather x1, waiting for transfers between devices: 9.8 us -> 0.01 us  [shards(): lax.all_gather(after(output_own, input_all), 'tensor', axis=0, tiled=True)]
    ppermute x5, waiting for transfers between devices: 9.33 us -> 18.9 us  [sum_over_all(): lax.ppermute(value, axis, [(i, i ^ bit) for i in range(size)])]
    unnamed x141 -> x147, local copies, waits for them, and re-layouts: 28.4 us -> 30.4 us
where the time goes in v4:
time: 804 us; the launch traced here: 795 us
  waiting for transfers between devices  386 us (48%)
  matrix products  100 us (12%)
  other arithmetic  97.1 us (12%)
  local copies, waits for them, and re-layouts  89.9 us (11%)
  Pallas kernels  78.2 us (10%)
  starting transfers between devices  27.5 us (3%)
  between operations  16 us (2%)
    ppermute x23, waiting for transfers between devices, send(): arrived = tuple((lax.ppermute(v, axis, p) for v, p in zip(values, perms)))  197 us
    dot_general x10, matrix products, dot_nt(): lax.dot_general(a, b, (((0,), (0,)), ((), ())), preferred_element_type=F32)  57.3 us
    pallas_call x1, Pallas kernels, mixture(): pl.pallas_call(functools.partial(mixture_kernel, experts=experts, local=l...  56 us
    all_gather x1, waiting for transfers between devices, shards(): lax.all_gather(jnp.concatenate([query_weight, key_weight, value_weight],...  45.5 us
    all_gather x1, waiting for transfers between devices, shards(): kv = lax.all_gather(kv_own, 'expert', axis=0, tiled=True)  34.6 us
    unnamed x147, local copies, waits for them, and re-layouts  30.4 us
    dot_general x3, matrix products, dot_tt(): lax.dot_general(a, b, (((1,), (1,)), ((), ())), preferred_element_type=F32)  25.3 us
    all_gather x1, waiting for transfers between devices, shards(): input_all = lax.all_gather(input_low, 'tensor', axis=0, tiled=True)  24.1 us
  transfers between devices with their start and end apart: 39, of which 24 were waited for; matrix products, arithmetic and copies ran while one was open for 27% of the time, Pallas kernels for 1%

profile of v4, /device:TPU:0, one launch (start us, length us, event | category | flops | bytes accessed | tf_op | source)
XLA Modules:
  0.0 794.8 jit_solution(10590408710087963363)
XLA Ops:
  13.3 45.5 %all-gather.8.cloned.1.call-done.wq_ref.wk_ref.wv_ref = bf16[2048,1536]{1,0:T(8,128)(2,1)} async-done(((bf16[256,1536]{1,0:T(8,128)(2,1)}), bf16[2048,1536]{1,0:T(8,128)(2,1)}) %all-gather.8.cloned.1.call-update) | async-done | bytes 6291472 | tf_op jit(solution)/shard_map/all_gather | solution.py:521
  66.9 34.6 %all-gather.10.cloned.1.call-done.kv_ref = bf16[2048,1024]{1,0:T(8,128)(2,1)} async-done(((bf16[512,1024]{1,0:T(8,128)(2,1)}), bf16[2048,1024]{1,0:T(8,128)(2,1)}) %all-gather.10.cloned.1.call-update) | async-done | bytes 4194320 | tf_op jit(solution)/shard_map/all_gather | solution.py:532
  119.7 9.3 %collective-permute-done.2 = bf16[3,352,256]{2,1,0:T(8,128)(2,1)S(1)} collective-permute-done((bf16[3,352,256]{2,1,0:T(8,128)(2,1)S(1)}, bf16[3,352,256]{2,1,0:T(8,128)(2,1)S(1)}, u32[]{:S(2)}, u32[]{:S(2)}) %collective-permute-start.2) | collective-permute-done | bytes 540704 | tf_op jit(solution)/shard_map/over_y/ppermute | solution.py:49
  129.8 15.5 %collective-permute-done.1 = bf16[3,352,256]{2,1,0:T(8,128)(2,1)S(1)} collective-permute-done((bf16[3,352,256]{2,1,0:T(8,128)(2,1)S(1)}, bf16[3,352,256]{2,1,0:T(8,128)(2,1)S(1)}, u32[]{:S(2)}, u32[]{:S(2)}) %collective-permute-start.1) | collective-permute-done | bytes 540704 | tf_op jit(solution)/shard_map/over_y/ppermute | solution.py:49
  167.1 35.3 %collective-permute-done.4 = bf16[512,2048]{1,0:T(8,128)(2,1)} collective-permute-done((bf16[512,2048]{1,0:T(8,128)(2,1)}, bf16[512,2048]{1,0:T(8,128)(2,1)}, u32[]{:S(2)}, u32[]{:S(2)}) %collective-permute-start.4) | collective-permute-done | bytes 2097184 | tf_op jit(solution)/shard_map/over_y/ppermute | solution.py:49
  227.6 7.6 fusion.8
  253.4 13.4 %fusion.88.hidden_grad_ref = f32[2048,1152]{1,0:T(8,128)} fusion(bf16[2048,2048]{1,0:T(8,128)(2,1)S(1)} %slice_dynamic-update-slice_fusion, bf16[1152,2048]{1,0:T(8,128)(2,1)S(1)} %get-tuple-element.196), kind=kOutput, calls=%fused_computation.222 | convolution fusion | flops 9663676416 | bytes 22544384 | tf_op jit(solution)/shard_map/dot_general | solution.py:155
  266.8 22.4 %all-gather.14.cloned.1.call-done.mix_ref = bf16[2048,2048]{1,0:T(8,128)(2,1)} async-done(((bf16[128,2048]{1,0:T(8,128)(2,1)}), bf16[2048,2048]{1,0:T(8,128)(2,1)}) %all-gather.14.cloned.1.call-update) | async-done | bytes 8388624 | tf_op jit(solution)/shard_map/all_gather | solution.py:602
  289.2 56.0 %shard_map.350 = (bf16[2048,2304]{1,0:T(8,128)(2,1)}, bf16[2048,1152]{1,0:T(8,128)(2,1)}, bf16[2048,128]{1,0:T(8,128)(2,1)}, bf16[2048,2048]{1,0:T(8,128)(2,1)}) custom-call(bf16[2048,2048]{1,0:T(8,128)(2,1)} %all-gather.14.cloned.1.call-done.mix_ref, f32[2048,1152]{1,0:T(8,128)} %fusion.88.hidden_grad_ref, bf16[2048,128]{1,0:T(8,128)(2,1)} %copy-done.46, ...), custom_call_target="tpu_custom_call" | custom-call | flops 48318382080 | bytes 83886080 | tf_op jit(solution)/shard_map/pallas_call | solution.py:442
  345.2 10.1 %convolution_convert_fusion.6 = bf16[768,2048]{1,0:T(8,128)(2,1)S(1)} fusion(bf16[2048,2048]{1,0:T(8,128)(2,1)} %copy-done.30, bf16[2048,1152]{1,0:T(8,128)(2,1)} %get-tuple-element.121), kind=kOutput, calls=%fused_computation.38 | convolution fusion | flops 6444023808 | bytes 14680064 | tf_op jit(solution)/shard_map/dot_general | solution.py:159
  358.6 7.4 fusion.15
  367.7 11.0 %convolution_convert_fusion.5 = bf16[768,2048]{1,0:T(8,128)(2,1)S(1)} fusion(bf16[2048,2048]{1,0:T(8,128)(2,1)} %all-gather.14.cloned.1.call-done.mix_ref, bf16[2048,2304]{1,0:T(8,128)(2,1)} %get-tuple-element.122), kind=kOutput, calls=%fused_computation.37 | convolution fusion | flops 6444023808 | bytes 14680064 | tf_op jit(solution)/shard_map/dot_general | solution.py:159
  381.4 6.2 fusion.80
  387.7 13.7 %convolution_convert_fusion = bf16[2048,2048]{1,0:T(8,128)(2,1)S(1)} fusion(bf16[2048,1152]{1,0:T(8,128)(2,1)} %get-tuple-element.121, bf16[1152,2048]{1,0:T(8,128)(2,1)S(1)} %bitcast.129), kind=kOutput, calls=%fused_computation.11 | convolution fusion | flops 9667870720 | bytes 17825792 | tf_op jit(solution)/shard_map/dot_general | solution.py:163
  403.3 8.7 %convolution_convert_fusion.4 = bf16[768,2048]{1,0:T(8,128)(2,1)} fusion(bf16[2048,768]{1,0:T(8,128)(2,1)S(1)} %copy-done.33, bf16[2048,2048]{1,0:T(8,128)(2,1)S(1)} %bitcast.121), kind=kOutput, calls=%fused_computation.36 | convolution fusion | flops 6444023808 | bytes 14680064 | tf_op jit(solution)/shard_map/dot_general | solution.py:159
  417.1 14.1 %collective-permute-done.9 = bf16[704,2048]{1,0:T(8,128)(2,1)} collective-permute-done((bf16[704,2048]{1,0:T(8,128)(2,1)}, bf16[704,2048]{1,0:T(8,128)(2,1)}, u32[]{:S(2)}, u32[]{:S(2)}) %collective-permute-start.9) | collective-permute-done | bytes 2883616 | tf_op jit(solution)/shard_map/over_x/ppermute | solution.py:49
  431.2 7.1 convolution_convert_fusion.3
  444.5 17.0 %reduce-scatter.7.cloned.1.call-done = bf16[128,2048]{1,0:T(8,128)(2,1)} async-done(((bf16[2048,2048]{1,0:T(8,128)(2,1)}), bf16[128,2048]{1,0:T(8,128)(2,1)}) %reduce-scatter.7.cloned.1.call-update) | async-done | bytes 524304 | tf_op jit(solution)/shard_map/reduce_scatter | solution.py:626
  475.9 41.7 %collective-permute-done.11 = bf16[1,512,2048]{2,1,0:T(8,128)(2,1)} collective-permute-done((bf16[1,512,2048]{2,1,0:T(8,128)(2,1)}, bf16[1,512,2048]{2,1,0:T(8,128)(2,1)}, u32[]{:S(2)}, u32[]{:S(2)}) %collective-permute-start.11) | collective-permute-done | bytes 2097184 | tf_op jit(solution)/shard_map/over_y/ppermute | solution.py:49
  526.9 7.8 shard_map.351
  542.7 11.1 %collective-permute-done.12 = bf16[128,2048]{1,0:T(8,128)(2,1)S(1)} collective-permute-done((bf16[128,2048]{1,0:T(8,128)(2,1)S(1)}, bf16[128,2048]{1,0:T(8,128)(2,1)S(1)}, u32[]{:S(2)}, u32[]{:S(2)}) %collective-permute-start.12) | collective-permute-done | bytes 524320 | tf_op jit(solution)/shard_map/over_z/ppermute | solution.py:49
  553.7 22.9 %collective-permute-done.13 = bf16[128,2048]{1,0:T(8,128)(2,1)S(1)} collective-permute-done((bf16[128,2048]{1,0:T(8,128)(2,1)S(1)}, bf16[128,2048]{1,0:T(8,128)(2,1)S(1)}, u32[]{:S(2)}, u32[]{:S(2)}) %collective-permute-start.13) | collective-permute-done | bytes 524320 | tf_op jit(solution)/shard_map/over_z/ppermute | solution.py:49
  578.9 9.7 %reduce-scatter.9.cloned.1.call-done.dkv_ref = bf16[512,1024]{1,0:T(8,128)(2,1)} async-done(((bf16[2048,1024]{1,0:T(8,128)(2,1)}), bf16[512,1024]{1,0:T(8,128)(2,1)}) %reduce-scatter.9.cloned.1.call-update) | async-done | bytes 1048592 | tf_op jit(solution)/shard_map/reduce_scatter | solution.py:702
  593.1 7.6 convolution_convert_fusion.7
  608.8 12.2 %collective-permute-done.16.refs_2_ = bf16[3,352,256]{2,1,0:T(8,128)(2,1)} collective-permute-done((bf16[3,352,256]{2,1,0:T(8,128)(2,1)}, bf16[3,352,256]{2,1,0:T(8,128)(2,1)}, u32[]{:S(2)}, u32[]{:S(2)}) %collective-permute-start.16) | collective-permute-done | bytes 540704 | tf_op jit(solution)/shard_map/over_y/ppermute | solution.py:49
  624.6 10.0 %collective-permute-done.17.refs_3_ = bf16[3,352,256]{2,1,0:T(8,128)(2,1)S(1)} collective-permute-done((bf16[3,352,256]{2,1,0:T(8,128)(2,1)S(1)}, bf16[3,352,256]{2,1,0:T(8,128)(2,1)S(1)}, u32[]{:S(2)}, u32[]{:S(2)}) %collective-permute-start.17) | collective-permute-done | bytes 540704 | tf_op jit(solution)/shard_map/over_y/ppermute | solution.py:49
  634.6 15.9 %reduce-scatter.11.cloned.1.call-done = bf16[128,2048]{1,0:T(8,128)(2,1)} async-done(((bf16[512,2048]{1,0:T(8,128)(2,1)}), bf16[128,2048]{1,0:T(8,128)(2,1)}) %reduce-scatter.11.cloned.1.call-update) | async-done | bytes 524304 | tf_op jit(solution)/shard_map/reduce_scatter | solution.py:706
  655.8 9.6 %collective-permute-done.23 = bf16[704,2048]{1,0:T(8,128)(2,1)} collective-permute-done((bf16[704,2048]{1,0:T(8,128)(2,1)}, bf16[704,2048]{1,0:T(8,128)(2,1)}, u32[]{:S(2)}, u32[]{:S(2)}) %collective-permute-start.23) | collective-permute-done | bytes 2883616 | tf_op jit(solution)/shard_map/over_x/ppermute | solution.py:49
  700.2 24.1 %all-gather.18.cloned.1.call-done = bf16[512,2048]{1,0:T(8,128)(2,1)} async-done(((bf16[128,2048]{1,0:T(8,128)(2,1)}), bf16[512,2048]{1,0:T(8,128)(2,1)}) %all-gather.18.cloned.1.call-update) | async-done | bytes 2097168 | tf_op jit(solution)/shard_map/all_gather | solution.py:725
  728.3 9.0 %collective-permute-done.26 = bf16[704,2048]{1,0:T(8,128)(2,1)} collective-permute-done((bf16[704,2048]{1,0:T(8,128)(2,1)}, bf16[704,2048]{1,0:T(8,128)(2,1)}, u32[]{:S(2)}, u32[]{:S(2)}) %collective-permute-start.26) | collective-permute-done | bytes 2883616 | tf_op jit(solution)/shard_map/over_x/ppermute | solution.py:49
  744.8 10.0 %collective-permute-done.21 = f32[28672]{0:T(1024)S(1)} collective-permute-done((f32[28672]{0:T(1024)S(1)}, f32[28672]{0:T(1024)S(1)}, u32[]{:S(2)}, u32[]{:S(2)}) %collective-permute-start.21) | collective-permute-done | bytes 114720 | tf_op jit(solution)/shard_map/ppermute | solution.py:114
  764.9 6.9 collective-permute-done.22
  (344 shorter events, 245.4 us)
Async XLA Ops:
  7.2 51.6 %all-gather.8.cloned.1.call-start = ((), (), s32[]{:S(2)}) async-start(), calls=%async_computation.4 | async-start | bytes 7077888 | tf_op jit(solution)/shard_map/all_gather | solution.py:521
  9.5 92.1 %all-gather.10.cloned.1.call-start = ((), (), s32[]{:S(2)}) async-start(), calls=%async_computation.5 | async-start | bytes 5242880 | tf_op jit(solution)/shard_map/all_gather | solution.py:532
  66.9 80.0 %all-gather.12.cloned.1.call-start = ((), (), s32[]{:S(2)}) async-start(), calls=%async_computation.6 | async-start | bytes 2359296 | tf_op jit(solution)/shard_map/all_gather | solution.py:533
  101.5 106.1 %reduce-scatter.5.cloned.1.call-start = ((), (), s32[]{:S(2)}) async-start(), calls=%async_computation.7 | async-start | bytes 2621440 | tf_op jit(solution)/shard_map/reduce_scatter | solution.py:594
  110.8 18.2 %collective-permute-start.2 = (bf16[3,352,256]{2,1,0:T(8,128)(2,1)S(1)}, bf16[3,352,256]{2,1,0:T(8,128)(2,1)S(1)}, u32[]{:S(2)}, u32[]{:S(2)}) collective-permute-start(bf16[3,352,256]{2,1,0:T(8,128)(2,1)S(1)} %get-tuple-element.98), channel_id=1, source_target_pairs={{0,12},{4,8},{8,4},{12,0},{1,13},{5,9},{9,5},{13,1},{2,14},{6,10},... | collective-permute-start | bytes 1622024 | tf_op jit(solution)/shard_map/over_y/ppermute | solution.py:49
  111.0 34.2 %collective-permute-start.1 = (bf16[3,352,256]{2,1,0:T(8,128)(2,1)S(1)}, bf16[3,352,256]{2,1,0:T(8,128)(2,1)S(1)}, u32[]{:S(2)}, u32[]{:S(2)}) collective-permute-start(bf16[3,352,256]{2,1,0:T(8,128)(2,1)S(1)} %get-tuple-element.97), channel_id=1, source_target_pairs={{0,8},{4,12},{8,0},{12,4},{1,9},{5,13},{9,1},{13,5},{2,10},{6,14},... | collective-permute-start | bytes 1622024 | tf_op jit(solution)/shard_map/over_y/ppermute | solution.py:49
  112.8 33.3 %collective-permute-start = (bf16[3,352,256]{2,1,0:T(8,128)(2,1)S(1)}, bf16[3,352,256]{2,1,0:T(8,128)(2,1)S(1)}, u32[]{:S(2)}, u32[]{:S(2)}) collective-permute-start(bf16[3,352,256]{2,1,0:T(8,128)(2,1)S(1)} %get-tuple-element.96), channel_id=1, source_target_pairs={{0,4},{4,0},{8,12},{12,8},{1,5},{5,1},{9,13},{13,9},{2,6},{6,2},{1... | collective-permute-start | bytes 1622024 | tf_op jit(solution)/shard_map/over_y/ppermute | solution.py:49
  151.3 137.9 %all-gather.14.cloned.1.call-start = ((), (), s32[]{:S(2)}) async-start(), calls=%async_computation.8 | async-start | bytes 8912896 | tf_op jit(solution)/shard_map/all_gather | solution.py:602
  154.5 47.9 %collective-permute-start.4 = (bf16[512,2048]{1,0:T(8,128)(2,1)}, bf16[512,2048]{1,0:T(8,128)(2,1)}, u32[]{:S(2)}, u32[]{:S(2)}) collective-permute-start(bf16[512,2048]{1,0:T(8,128)(2,1)} %broadcast_select_fusion), channel_id=1, source_target_pairs={{0,8},{4,12},{8,0},{12,4},{1,9},{5,13},{9,1},{13,5},{2,10},{6,14},... | collective-permute-start | bytes 6291464 | tf_op jit(solution)/shard_map/over_y/ppermute | solution.py:49
  160.6 49.0 %collective-permute-start.3 = (bf16[3,352,1024]{2,1,0:T(8,128)(2,1)}, bf16[3,352,1024]{2,1,0:T(8,128)(2,1)}, u32[]{:S(2)}, u32[]{:S(2)}) collective-permute-start(bf16[3,352,1024]{2,1,0:T(8,128)(2,1)} %constant_dynamic-update-slice_fusion), channel_id=1, source_target_pairs={{0,16},{16,0},{1,17},{17,1},{2,18},{18,2},{3,19},{19,3},{4,20},{20... | collective-permute-start | bytes 6488072 | tf_op jit(solution)/shard_map/over_x/ppermute | solution.py:49
  213.0 248.6 %reduce-scatter.7.cloned.1.call-start = ((), (), s32[]{:S(2)}) async-start(), calls=%async_computation.9 | async-start | bytes 8912896 | tf_op jit(solution)/shard_map/reduce_scatter | solution.py:626
  227.6 16.5 %collective-permute-start.6 = (bf16[1024,2048]{1,0:T(8,128)(2,1)S(1)}, bf16[1024,2048]{1,0:T(8,128)(2,1)}, u32[]{:S(2)}, u32[]{:S(2)}) collective-permute-start(bf16[1024,2048]{1,0:T(8,128)(2,1)S(1)} %copy-done.22), channel_id=1, source_target_pairs={{0,4},{4,0},{8,12},{12,8},{1,5},{5,1},{9,13},{13,9},{2,6},{6,2},{1... | collective-permute-start | bytes 12582920 | tf_op jit(solution)/shard_map/over_core/ppermute | solution.py:49
  358.6 164.7 %all-gather.16.cloned.1.call-start = ((), (), s32[]{:S(2)}) async-start(), calls=%async_computation.10 | async-start | bytes 2621440 | tf_op jit(solution)/shard_map/all_gather | solution.py:691
  366.2 65.0 %collective-permute-start.9 = (bf16[704,2048]{1,0:T(8,128)(2,1)}, bf16[704,2048]{1,0:T(8,128)(2,1)}, u32[]{:S(2)}, u32[]{:S(2)}) collective-permute-start(bf16[704,2048]{1,0:T(8,128)(2,1)} %pad_maximum_fusion.4), channel_id=1, source_target_pairs={{0,16},{16,0},{1,17},{17,1},{2,18},{18,2},{3,19},{19,3},{4,20},{20... | collective-permute-start | bytes 8650760 | tf_op jit(solution)/shard_map/over_x/ppermute | solution.py:49
  401.9 38.6 %collective-permute-start.8 = (bf16[2,512,2048]{2,1,0:T(8,128)(2,1)S(1)}, bf16[2,512,2048]{2,1,0:T(8,128)(2,1)S(1)}, u32[]{:S(2)}, u32[]{:S(2)}) collective-permute-start(bf16[2,512,2048]{2,1,0:T(8,128)(2,1)S(1)} %dynamic-slice_bitcast_fusion), channel_id=1, source_target_pairs={{0,4},{4,0},{8,12},{12,8},{1,5},{5,1},{9,13},{13,9},{2,6},{6,2},{1... | collective-permute-start | bytes 12582920 | tf_op jit(solution)/shard_map/over_core/ppermute | solution.py:49
  466.6 122.0 %reduce-scatter.9.cloned.1.call-start = ((), (), s32[]{:S(2)}) async-start(), calls=%async_computation.11 | async-start | bytes 5242880 | tf_op jit(solution)/shard_map/reduce_scatter | solution.py:702
  469.8 47.7 %collective-permute-start.11 = (bf16[1,512,2048]{2,1,0:T(8,128)(2,1)}, bf16[1,512,2048]{2,1,0:T(8,128)(2,1)}, u32[]{:S(2)}, u32[]{:S(2)}) collective-permute-start(bf16[1,512,2048]{2,1,0:T(8,128)(2,1)} %constant_dynamic-slice_fusion.24), channel_id=1, source_target_pairs={{0,8},{4,12},{8,0},{12,4},{1,9},{5,13},{9,1},{13,5},{2,10},{6,14},... | collective-permute-start | bytes 6291464 | tf_op jit(solution)/shard_map/over_y/ppermute | solution.py:49
  474.4 48.8 %collective-permute-start.10 = (bf16[1056,1024]{1,0:T(8,128)(2,1)}, bf16[1056,1024]{1,0:T(8,128)(2,1)}, u32[]{:S(2)}, u32[]{:S(2)}) collective-permute-start(bf16[1056,1024]{1,0:T(8,128)(2,1)} %constant_dynamic-slice_fusion.25), channel_id=1, source_target_pairs={{0,16},{16,0},{1,17},{17,1},{2,18},{18,2},{3,19},{19,3},{4,20},{20... | collective-permute-start | bytes 6488072 | tf_op jit(solution)/shard_map/over_x/ppermute | solution.py:49
  535.7 114.8 %reduce-scatter.11.cloned.1.call-start = ((), (), s32[]{:S(2)}) async-start(), calls=%async_computation.12 | async-start | bytes 2621440 | tf_op jit(solution)/shard_map/reduce_scatter | solution.py:706
  537.4 16.3 %collective-permute-start.12 = (bf16[128,2048]{1,0:T(8,128)(2,1)S(1)}, bf16[128,2048]{1,0:T(8,128)(2,1)S(1)}, u32[]{:S(2)}, u32[]{:S(2)}) collective-permute-start(bf16[128,2048]{1,0:T(8,128)(2,1)S(1)} %get-tuple-element.224), channel_id=1, source_target_pairs={{0,1},{1,2},{2,3},{3,0},{4,5},{5,6},{6,7},{7,4},{8,9},{9,10},{10,1... | collective-permute-start | bytes 1572872 | tf_op jit(solution)/shard_map/over_z/ppermute | solution.py:49
  539.0 37.6 %collective-permute-start.13 = (bf16[128,2048]{1,0:T(8,128)(2,1)S(1)}, bf16[128,2048]{1,0:T(8,128)(2,1)S(1)}, u32[]{:S(2)}, u32[]{:S(2)}) collective-permute-start(bf16[128,2048]{1,0:T(8,128)(2,1)S(1)} %get-tuple-element.226), channel_id=1, source_target_pairs={{0,2},{1,3},{2,0},{3,1},{4,6},{5,7},{6,4},{7,5},{8,10},{9,11},{10,... | collective-permute-start | bytes 1572872 | tf_op jit(solution)/shard_map/over_z/ppermute | solution.py:49
  540.4 36.2 %collective-permute-start.14 = (bf16[128,2048]{1,0:T(8,128)(2,1)S(1)}, bf16[128,2048]{1,0:T(8,128)(2,1)S(1)}, u32[]{:S(2)}, u32[]{:S(2)}) collective-permute-start(bf16[128,2048]{1,0:T(8,128)(2,1)S(1)} %get-tuple-element.225), channel_id=1, source_target_pairs={{0,3},{1,0},{2,1},{3,2},{4,7},{5,4},{6,5},{7,6},{8,11},{9,8},{10,9... | collective-permute-start | bytes 1572872 | tf_op jit(solution)/shard_map/over_z/ppermute | solution.py:49
  600.7 123.5 %all-gather.18.cloned.1.call-start = ((), (), s32[]{:S(2)}) async-start(), calls=%async_computation.13 | async-start | bytes 2621440 | tf_op jit(solution)/shard_map/all_gather | solution.py:725
  600.8 64.6 %collective-permute-start.23 = (bf16[704,2048]{1,0:T(8,128)(2,1)}, bf16[704,2048]{1,0:T(8,128)(2,1)}, u32[]{:S(2)}, u32[]{:S(2)}) collective-permute-start(bf16[704,2048]{1,0:T(8,128)(2,1)} %pad_maximum_fusion.5), channel_id=1, source_target_pairs={{0,16},{16,0},{1,17},{17,1},{2,18},{18,2},{3,19},{19,3},{4,20},{20... | collective-permute-start | bytes 8650760 | tf_op jit(solution)/shard_map/over_x/ppermute | solution.py:49
  608.8 15.8 %collective-permute-start.15 = (bf16[3,352,256]{2,1,0:T(8,128)(2,1)S(1)}, bf16[3,352,256]{2,1,0:T(8,128)(2,1)S(1)}, u32[]{:S(2)}, u32[]{:S(2)}) collective-permute-start(bf16[3,352,256]{2,1,0:T(8,128)(2,1)S(1)} %copy-done.45), channel_id=1, source_target_pairs={{0,4},{4,0},{8,12},{12,8},{1,5},{5,1},{9,13},{13,9},{2,6},{6,2},{1... | collective-permute-start | bytes 1622024 | tf_op jit(solution)/shard_map/over_core/ppermute | solution.py:49
  671.7 65.7 %collective-permute-start.26 = (bf16[704,2048]{1,0:T(8,128)(2,1)}, bf16[704,2048]{1,0:T(8,128)(2,1)}, u32[]{:S(2)}, u32[]{:S(2)}) collective-permute-start(bf16[704,2048]{1,0:T(8,128)(2,1)} %pad_maximum_fusion.6), channel_id=1, source_target_pairs={{0,16},{16,0},{1,17},{17,1},{2,18},{18,2},{3,19},{19,3},{4,20},{20... | collective-permute-start | bytes 8650760 | tf_op jit(solution)/shard_map/over_x/ppermute | solution.py:49
  673.2 104.7 %all-gather.20.cloned.1.call-start = ((), (), s32[]{:S(2)}) async-start(), calls=%async_computation.14 | async-start | bytes 2621440 | tf_op jit(solution)/shard_map/all_gather | solution.py:765
  680.6 18.9 %collective-permute-start.19 = (f32[28672]{0:T(1024)S(1)}, f32[28672]{0:T(1024)S(1)}, u32[]{:S(2)}, u32[]{:S(2)}) collective-permute-start(f32[28672]{0:T(1024)S(1)} %fusion.78), channel_id=1, source_target_pairs={{0,8},{4,12},{8,0},{12,4},{1,9},{5,13},{9,1},{13,5},{2,10},{6,14},... | collective-permute-start | bytes 344072 | tf_op jit(solution)/shard_map/ppermute | solution.py:114
  687.7 68.2 %collective-permute-start.25 = (bf16[512,2048]{1,0:T(8,128)(2,1)}, bf16[512,2048]{1,0:T(8,128)(2,1)}, u32[]{:S(2)}, u32[]{:S(2)}) collective-permute-start(bf16[512,2048]{1,0:T(8,128)(2,1)} %slice.248), channel_id=1, source_target_pairs={{0,8},{4,12},{8,0},{12,4},{1,9},{5,13},{9,1},{13,5},{2,10},{6,14},... | collective-permute-start | bytes 6291464 | tf_op jit(solution)/shard_map/over_y/ppermute | solution.py:49
  699.5 39.8 %collective-permute-start.20 = (f32[28672]{0:T(1024)S(1)}, f32[28672]{0:T(1024)S(1)}, u32[]{:S(2)}, u32[]{:S(2)}) collective-permute-start(f32[28672]{0:T(1024)S(1)} %add.410), channel_id=1, source_target_pairs={{0,16},{16,0},{1,17},{17,1},{2,18},{18,2},{3,19},{19,3},{4,20},{20... | collective-permute-start | bytes 344072 | tf_op jit(solution)/shard_map/ppermute | solution.py:114
  754.9 16.9 %collective-permute-start.22 = (f32[28672]{0:T(1024)S(1)}, f32[28672]{0:T(1024)S(1)}, u32[]{:S(2)}, u32[]{:S(2)}) collective-permute-start(f32[28672]{0:T(1024)S(1)} %add.412), channel_id=1, source_target_pairs={{0,2},{1,3},{2,0},{3,1},{4,6},{5,7},{6,4},{7,5},{8,10},{9,11},{10,... | collective-permute-start | bytes 344072 | tf_op jit(solution)/shard_map/ppermute | solution.py:114
  758.4 24.3 %collective-permute-start.27 = (bf16[256,2048]{1,0:T(8,128)(2,1)S(1)}, bf16[256,2048]{1,0:T(8,128)(2,1)}, u32[]{:S(2)}, u32[]{:S(2)}) collective-permute-start(bf16[256,2048]{1,0:T(8,128)(2,1)S(1)} %slice.250), channel_id=1, source_target_pairs={{0,16},{16,0},{1,17},{17,1},{2,18},{18,2},{3,19},{19,3},{4,20},{20... | collective-permute-start | bytes 3145736 | tf_op jit(solution)/shard_map/over_x/ppermute | solution.py:49
  (78 other events, 741.5 us)
Sparse Core Ops, SparseCore 0:
  10.5 48.2 all-gather.7
  67.0 34.4 all-gather.9
  103.4 36.4 all-gather.11
  151.4 43.8 reduce-scatter.4
  213.1 76.0 all-gather.13
  358.7 102.8 reduce-scatter.6
  466.7 45.6 all-gather.15
  535.8 52.7 reduce-scatter.8
  600.9 49.6 reduce-scatter.10
  673.3 50.8 all-gather.17
  726.4 49.4 all-gather.19

commit v5 on v4

--- a/solution.py
+++ b/solution.py
@@ -563,8 +563,12 @@
     kept = jnp.pad(kept.astype(BF16), ((0, 0), (0, LANES - experts)))
 
     upstream_low = jnp.where(live_rows[:, None], upstream_source, jnp.zeros((), BF16))
+    shared_half = in_order(
+        [units_of(block_at)] + shared_pieces, [block_at ^ s for s in range(groups)], 2
+    )
+    heads_ready, upstream_low, kept, shared_half = together(heads_low, upstream_low, kept, shared_half)
+    kept_all = links.spread(kept, "expert", low=2)
     upstream_all = links.spread(upstream_low, "expert", low=2)
-    kept_all = links.spread(kept, "expert", low=2)
 
     def pad_units(weight):
         return jnp.pad(weight, ((0, width - weight.shape[0]), (0, 0)))
@@ -587,9 +591,7 @@
     spot = (spot_at[:, None] == jnp.arange(LANES, dtype=jnp.int32)[None, :]).astype(F32)
     spot = jnp.pad(spot, ((0, up_to(steps, 8) - steps), (0, 0)))
 
-    shared_pieces = [units_of(block_at)] + shared_pieces
-    attended_part = dot_tt(after(heads_low, tuple(shared_pieces)), output_here).astype(BF16)
-    shared_half = in_order(shared_pieces, [block_at ^ s for s in range(groups)], 2)
+    attended_part = dot_tt(heads_ready, output_here).astype(BF16)
     halves = [shared_half] + links.shifts([shared_half] * (slots - 1), "dp")
     attended = lax.psum_scatter(attended_part, "tensor", scatter_dimension=0, tiled=True).astype(F32)
     inputs_own = rows_of(inputs, tensor_at)

time: 804 us -> 804 us (level)
  local copies, waits for them, and re-layouts: 89.9 us -> 98.4 us
    unnamed x147 -> x137, local copies, waits for them, and re-layouts: 30.4 us -> 33.2 us
where the time goes in v5:
time: 804 us; the launch traced here: 795 us
  waiting for transfers between devices  385 us (48%)
  matrix products  100 us (12%)
  local copies, waits for them, and re-layouts  98.4 us (12%)
  other arithmetic  89.8 us (11%)
  Pallas kernels  78.4 us (10%)
  starting transfers between devices  27.4 us (3%)
  between operations  15.9 us (2%)
    ppermute x23, waiting for transfers between devices, send(): arrived = tuple((lax.ppermute(v, axis, p) for v, p in zip(values, perms)))  196 us
    dot_general x10, matrix products, dot_nt(): lax.dot_general(a, b, (((0,), (0,)), ((), ())), preferred_element_type=F32)  57.1 us
    pallas_call x1, Pallas kernels, mixture(): pl.pallas_call(functools.partial(mixture_kernel, experts=experts, local=l...  56 us
    all_gather x1, waiting for transfers between devices, shards(): lax.all_gather(jnp.concatenate([query_weight, key_weight, value_weight],...  45.5 us
    all_gather x1, waiting for transfers between devices, shards(): kv = lax.all_gather(kv_own, 'expert', axis=0, tiled=True)  34.6 us
    unnamed x137, local copies, waits for them, and re-layouts  33.2 us
    dot_general x3, matrix products, dot_tt(): lax.dot_general(a, b, (((1,), (1,)), ((), ())), preferred_element_type=F32)  25.3 us
    all_gather x1, waiting for transfers between devices, shards(): input_all = lax.all_gather(input_low, 'tensor', axis=0, tiled=True)  24.5 us
  transfers between devices with their start and end apart: 39, of which 24 were waited for; matrix products, arithmetic and copies ran while one was open for 27% of the time, Pallas kernels for 1%

profile of v5, /device:TPU:0, one launch (start us, length us, event | category | flops | bytes accessed | tf_op | source)
XLA Modules:
  0.0 794.9 jit_solution(5124127850336471881)
XLA Ops:
  13.3 45.5 %all-gather.8.cloned.1.call-done.wq_ref.wk_ref.wv_ref = bf16[2048,1536]{1,0:T(8,128)(2,1)} async-done(((bf16[256,1536]{1,0:T(8,128)(2,1)}), bf16[2048,1536]{1,0:T(8,128)(2,1)}) %all-gather.8.cloned.1.call-update) | async-done | bytes 6291472 | tf_op jit(solution)/shard_map/all_gather | solution.py:521
  67.0 34.6 %all-gather.10.cloned.1.call-done.kv_ref = bf16[2048,1024]{1,0:T(8,128)(2,1)} async-done(((bf16[512,1024]{1,0:T(8,128)(2,1)}), bf16[2048,1024]{1,0:T(8,128)(2,1)}) %all-gather.10.cloned.1.call-update) | async-done | bytes 4194320 | tf_op jit(solution)/shard_map/all_gather | solution.py:532
  128.6 8.4 %collective-permute-done.1 = bf16[3,352,256]{2,1,0:T(8,128)(2,1)} collective-permute-done((bf16[3,352,256]{2,1,0:T(8,128)(2,1)}, bf16[3,352,256]{2,1,0:T(8,128)(2,1)}, u32[]{:S(2)}, u32[]{:S(2)}) %collective-permute-start.1) | collective-permute-done | bytes 540704 | tf_op jit(solution)/shard_map/over_y/ppermute | solution.py:49
  138.9 8.3 %collective-permute-done.2 = bf16[3,352,256]{2,1,0:T(8,128)(2,1)S(1)} collective-permute-done((bf16[3,352,256]{2,1,0:T(8,128)(2,1)}, bf16[3,352,256]{2,1,0:T(8,128)(2,1)S(1)}, u32[]{:S(2)}, u32[]{:S(2)}) %collective-permute-start.2) | collective-permute-done | bytes 540704 | tf_op jit(solution)/shard_map/over_y/ppermute | solution.py:49
  169.2 37.3 %collective-permute-done.5 = bf16[512,2048]{1,0:T(8,128)(2,1)} collective-permute-done((bf16[512,2048]{1,0:T(8,128)(2,1)}, bf16[512,2048]{1,0:T(8,128)(2,1)}, u32[]{:S(2)}, u32[]{:S(2)}) %collective-permute-start.5) | collective-permute-done | bytes 2097184 | tf_op jit(solution)/shard_map/over_y/ppermute | solution.py:49
  227.2 7.7 fusion.8
  254.3 13.3 %fusion.88.hidden_grad_ref = f32[2048,1152]{1,0:T(8,128)} fusion(bf16[2048,2048]{1,0:T(8,128)(2,1)S(1)} %slice_dynamic-update-slice_fusion, bf16[1152,2048]{1,0:T(8,128)(2,1)S(1)} %get-tuple-element.200), kind=kOutput, calls=%fused_computation.223 | convolution fusion | flops 9663676416 | bytes 22544384 | tf_op jit(solution)/shard_map/dot_general | solution.py:155
  267.6 21.8 %all-gather.14.cloned.1.call-done.mix_ref = bf16[2048,2048]{1,0:T(8,128)(2,1)} async-done(((bf16[128,2048]{1,0:T(8,128)(2,1)}), bf16[2048,2048]{1,0:T(8,128)(2,1)}) %all-gather.14.cloned.1.call-update) | async-done | bytes 8388624 | tf_op jit(solution)/shard_map/all_gather | solution.py:604
  289.4 56.0 %shard_map.350 = (bf16[2048,2304]{1,0:T(8,128)(2,1)}, bf16[2048,1152]{1,0:T(8,128)(2,1)}, bf16[2048,128]{1,0:T(8,128)(2,1)}, bf16[2048,2048]{1,0:T(8,128)(2,1)}) custom-call(bf16[2048,2048]{1,0:T(8,128)(2,1)} %all-gather.14.cloned.1.call-done.mix_ref, f32[2048,1152]{1,0:T(8,128)} %fusion.88.hidden_grad_ref, bf16[2048,128]{1,0:T(8,128)(2,1)} %copy-done.39, ...), custom_call_target="tpu_custom_call" | custom-call | flops 48318382080 | bytes 83886080 | tf_op jit(solution)/shard_map/pallas_call | solution.py:442
  345.4 10.1 %convolution_convert_fusion.6 = bf16[768,2048]{1,0:T(8,128)(2,1)S(1)} fusion(bf16[2048,2048]{1,0:T(8,128)(2,1)} %copy-done.25, bf16[2048,1152]{1,0:T(8,128)(2,1)} %get-tuple-element.127), kind=kOutput, calls=%fused_computation.37 | convolution fusion | flops 6444023808 | bytes 14680064 | tf_op jit(solution)/shard_map/dot_general | solution.py:159
  358.8 7.4 fusion.15
  367.9 11.0 %convolution_convert_fusion.5 = bf16[768,2048]{1,0:T(8,128)(2,1)S(1)} fusion(bf16[2048,2048]{1,0:T(8,128)(2,1)} %all-gather.14.cloned.1.call-done.mix_ref, bf16[2048,2304]{1,0:T(8,128)(2,1)} %get-tuple-element.128), kind=kOutput, calls=%fused_computation.36 | convolution fusion | flops 6444023808 | bytes 14680064 | tf_op jit(solution)/shard_map/dot_general | solution.py:159
  381.6 6.2 fusion.80
  387.8 13.7 %convolution_convert_fusion = bf16[2048,2048]{1,0:T(8,128)(2,1)S(1)} fusion(bf16[2048,1152]{1,0:T(8,128)(2,1)} %get-tuple-element.127, bf16[1152,2048]{1,0:T(8,128)(2,1)S(1)} %bitcast.129), kind=kOutput, calls=%fused_computation.11 | convolution fusion | flops 9667870720 | bytes 17825792 | tf_op jit(solution)/shard_map/dot_general | solution.py:163
  403.5 8.6 %convolution_convert_fusion.4 = bf16[768,2048]{1,0:T(8,128)(2,1)} fusion(bf16[2048,768]{1,0:T(8,128)(2,1)S(1)} %copy-done.28, bf16[2048,2048]{1,0:T(8,128)(2,1)S(1)} %bitcast.121), kind=kOutput, calls=%fused_computation.35 | convolution fusion | flops 6444023808 | bytes 14680064 | tf_op jit(solution)/shard_map/dot_general | solution.py:159
  417.3 14.1 %collective-permute-done.9 = bf16[704,2048]{1,0:T(8,128)(2,1)} collective-permute-done((bf16[704,2048]{1,0:T(8,128)(2,1)}, bf16[704,2048]{1,0:T(8,128)(2,1)}, u32[]{:S(2)}, u32[]{:S(2)}) %collective-permute-start.9) | collective-permute-done | bytes 2883616 | tf_op jit(solution)/shard_map/over_x/ppermute | solution.py:49
  431.4 7.1 convolution_convert_fusion.3
  444.7 17.1 %reduce-scatter.7.cloned.1.call-done = bf16[128,2048]{1,0:T(8,128)(2,1)} async-done(((bf16[2048,2048]{1,0:T(8,128)(2,1)}), bf16[128,2048]{1,0:T(8,128)(2,1)}) %reduce-scatter.7.cloned.1.call-update) | async-done | bytes 524304 | tf_op jit(solution)/shard_map/reduce_scatter | solution.py:628
  476.1 41.7 %collective-permute-done.11 = bf16[1,512,2048]{2,1,0:T(8,128)(2,1)} collective-permute-done((bf16[1,512,2048]{2,1,0:T(8,128)(2,1)}, bf16[1,512,2048]{2,1,0:T(8,128)(2,1)}, u32[]{:S(2)}, u32[]{:S(2)}) %collective-permute-start.11) | collective-permute-done | bytes 2097184 | tf_op jit(solution)/shard_map/over_y/ppermute | solution.py:49
  527.1 7.8 shard_map.351
  542.9 11.0 %collective-permute-done.12 = bf16[128,2048]{1,0:T(8,128)(2,1)S(1)} collective-permute-done((bf16[128,2048]{1,0:T(8,128)(2,1)S(1)}, bf16[128,2048]{1,0:T(8,128)(2,1)S(1)}, u32[]{:S(2)}, u32[]{:S(2)}) %collective-permute-start.12) | collective-permute-done | bytes 524320 | tf_op jit(solution)/shard_map/over_z/ppermute | solution.py:49
  554.0 22.9 %collective-permute-done.13 = bf16[128,2048]{1,0:T(8,128)(2,1)S(1)} collective-permute-done((bf16[128,2048]{1,0:T(8,128)(2,1)S(1)}, bf16[128,2048]{1,0:T(8,128)(2,1)S(1)}, u32[]{:S(2)}, u32[]{:S(2)}) %collective-permute-start.13) | collective-permute-done | bytes 524320 | tf_op jit(solution)/shard_map/over_z/ppermute | solution.py:49
  579.1 9.8 %reduce-scatter.9.cloned.1.call-done.dkv_ref = bf16[512,1024]{1,0:T(8,128)(2,1)} async-done(((bf16[2048,1024]{1,0:T(8,128)(2,1)}), bf16[512,1024]{1,0:T(8,128)(2,1)}) %reduce-scatter.9.cloned.1.call-update) | async-done | bytes 1048592 | tf_op jit(solution)/shard_map/reduce_scatter | solution.py:704
  593.4 7.6 convolution_convert_fusion.7
  609.1 12.2 %collective-permute-done.16.refs_2_ = bf16[3,352,256]{2,1,0:T(8,128)(2,1)} collective-permute-done((bf16[3,352,256]{2,1,0:T(8,128)(2,1)}, bf16[3,352,256]{2,1,0:T(8,128)(2,1)}, u32[]{:S(2)}, u32[]{:S(2)}) %collective-permute-start.16) | collective-permute-done | bytes 540704 | tf_op jit(solution)/shard_map/over_y/ppermute | solution.py:49
  624.9 10.0 %collective-permute-done.17.refs_3_ = bf16[3,352,256]{2,1,0:T(8,128)(2,1)S(1)} collective-permute-done((bf16[3,352,256]{2,1,0:T(8,128)(2,1)S(1)}, bf16[3,352,256]{2,1,0:T(8,128)(2,1)S(1)}, u32[]{:S(2)}, u32[]{:S(2)}) %collective-permute-start.17) | collective-permute-done | bytes 540704 | tf_op jit(solution)/shard_map/over_y/ppermute | solution.py:49
  634.9 15.9 %reduce-scatter.11.cloned.1.call-done = bf16[128,2048]{1,0:T(8,128)(2,1)} async-done(((bf16[512,2048]{1,0:T(8,128)(2,1)}), bf16[128,2048]{1,0:T(8,128)(2,1)}) %reduce-scatter.11.cloned.1.call-update) | async-done | bytes 524304 | tf_op jit(solution)/shard_map/reduce_scatter | solution.py:708
  656.0 9.7 %collective-permute-done.23 = bf16[704,2048]{1,0:T(8,128)(2,1)} collective-permute-done((bf16[704,2048]{1,0:T(8,128)(2,1)}, bf16[704,2048]{1,0:T(8,128)(2,1)}, u32[]{:S(2)}, u32[]{:S(2)}) %collective-permute-start.23) | collective-permute-done | bytes 2883616 | tf_op jit(solution)/shard_map/over_x/ppermute | solution.py:49
  700.0 24.5 %all-gather.18.cloned.1.call-done = bf16[512,2048]{1,0:T(8,128)(2,1)} async-done(((bf16[128,2048]{1,0:T(8,128)(2,1)}), bf16[512,2048]{1,0:T(8,128)(2,1)}) %all-gather.18.cloned.1.call-update) | async-done | bytes 2097168 | tf_op jit(solution)/shard_map/all_gather | solution.py:727
  728.6 9.1 %collective-permute-done.26 = bf16[704,2048]{1,0:T(8,128)(2,1)} collective-permute-done((bf16[704,2048]{1,0:T(8,128)(2,1)}, bf16[704,2048]{1,0:T(8,128)(2,1)}, u32[]{:S(2)}, u32[]{:S(2)}) %collective-permute-start.26) | collective-permute-done | bytes 2883616 | tf_op jit(solution)/shard_map/over_x/ppermute | solution.py:49
  744.8 10.3 %collective-permute-done.21 = f32[28672]{0:T(1024)S(1)} collective-permute-done((f32[28672]{0:T(1024)S(1)}, f32[28672]{0:T(1024)S(1)}, u32[]{:S(2)}, u32[]{:S(2)}) %collective-permute-start.21) | collective-permute-done | bytes 114720 | tf_op jit(solution)/shard_map/ppermute | solution.py:114
  765.0 7.1 collective-permute-done.22
  (334 shorter events, 251.2 us)
Async XLA Ops:
  7.2 51.6 %all-gather.8.cloned.1.call-start = ((), (), s32[]{:S(2)}) async-start(), calls=%async_computation.4 | async-start | bytes 7077888 | tf_op jit(solution)/shard_map/all_gather | solution.py:521
  9.5 92.1 %all-gather.10.cloned.1.call-start = ((), (), s32[]{:S(2)}) async-start(), calls=%async_computation.5 | async-start | bytes 5242880 | tf_op jit(solution)/shard_map/all_gather | solution.py:532
  66.9 81.1 %all-gather.12.cloned.1.call-start = ((), (), s32[]{:S(2)}) async-start(), calls=%async_computation.6 | async-start | bytes 2359296 | tf_op jit(solution)/shard_map/all_gather | solution.py:533
  101.6 108.2 %reduce-scatter.5.cloned.1.call-start = ((), (), s32[]{:S(2)}) async-start(), calls=%async_computation.7 | async-start | bytes 2621440 | tf_op jit(solution)/shard_map/reduce_scatter | solution.py:596
  115.9 21.0 %collective-permute-start.1 = (bf16[3,352,256]{2,1,0:T(8,128)(2,1)}, bf16[3,352,256]{2,1,0:T(8,128)(2,1)}, u32[]{:S(2)}, u32[]{:S(2)}) collective-permute-start(bf16[3,352,256]{2,1,0:T(8,128)(2,1)} %get-tuple-element.102), channel_id=1, source_target_pairs={{0,8},{4,12},{8,0},{12,4},{1,9},{5,13},{9,1},{13,5},{2,10},{6,14},... | collective-permute-start | bytes 1622024 | tf_op jit(solution)/shard_map/over_y/ppermute | solution.py:49
  116.4 30.8 %collective-permute-start.2 = (bf16[3,352,256]{2,1,0:T(8,128)(2,1)}, bf16[3,352,256]{2,1,0:T(8,128)(2,1)S(1)}, u32[]{:S(2)}, u32[]{:S(2)}) collective-permute-start(bf16[3,352,256]{2,1,0:T(8,128)(2,1)} %get-tuple-element.103), channel_id=1, source_target_pairs={{0,12},{4,8},{8,4},{12,0},{1,13},{5,9},{9,5},{13,1},{2,14},{6,10},... | collective-permute-start | bytes 1622024 | tf_op jit(solution)/shard_map/over_y/ppermute | solution.py:49
  152.4 137.0 %all-gather.14.cloned.1.call-start = ((), (), s32[]{:S(2)}) async-start(), calls=%async_computation.8 | async-start | bytes 8912896 | tf_op jit(solution)/shard_map/all_gather | solution.py:604
  159.0 47.6 %collective-permute-start.5 = (bf16[512,2048]{1,0:T(8,128)(2,1)}, bf16[512,2048]{1,0:T(8,128)(2,1)}, u32[]{:S(2)}, u32[]{:S(2)}) collective-permute-start(bf16[512,2048]{1,0:T(8,128)(2,1)} %broadcast_select_fusion), channel_id=1, source_target_pairs={{0,8},{4,12},{8,0},{12,4},{1,9},{5,13},{9,1},{13,5},{2,10},{6,14},... | collective-permute-start | bytes 6291464 | tf_op jit(solution)/shard_map/over_y/ppermute | solution.py:49
  159.3 51.6 %collective-permute-start.3 = (bf16[3,352,1024]{2,1,0:T(8,128)(2,1)}, bf16[3,352,1024]{2,1,0:T(8,128)(2,1)}, u32[]{:S(2)}, u32[]{:S(2)}) collective-permute-start(bf16[3,352,1024]{2,1,0:T(8,128)(2,1)} %constant_dynamic-update-slice_fusion.4), channel_id=1, source_target_pairs={{0,16},{16,0},{1,17},{17,1},{2,18},{18,2},{3,19},{19,3},{4,20},{20... | collective-permute-start | bytes 6488072 | tf_op jit(solution)/shard_map/over_x/ppermute | solution.py:49
  214.3 247.5 %reduce-scatter.7.cloned.1.call-start = ((), (), s32[]{:S(2)}) async-start(), calls=%async_computation.9 | async-start | bytes 8912896 | tf_op jit(solution)/shard_map/reduce_scatter | solution.py:628
  227.1 22.2 %collective-permute-start.6 = (bf16[1024,2048]{1,0:T(8,128)(2,1)}, bf16[1024,2048]{1,0:T(8,128)(2,1)S(1)}, u32[]{:S(2)}, u32[]{:S(2)}) collective-permute-start(bf16[1024,2048]{1,0:T(8,128)(2,1)} %constant_dynamic-update-slice_fusion), channel_id=1, source_target_pairs={{0,4},{4,0},{8,12},{12,8},{1,5},{5,1},{9,13},{13,9},{2,6},{6,2},{1... | collective-permute-start | bytes 12582920 | tf_op jit(solution)/shard_map/over_core/ppermute | solution.py:49
  358.8 164.7 %all-gather.16.cloned.1.call-start = ((), (), s32[]{:S(2)}) async-start(), calls=%async_computation.10 | async-start | bytes 2621440 | tf_op jit(solution)/shard_map/all_gather | solution.py:693
  366.4 65.0 %collective-permute-start.9 = (bf16[704,2048]{1,0:T(8,128)(2,1)}, bf16[704,2048]{1,0:T(8,128)(2,1)}, u32[]{:S(2)}, u32[]{:S(2)}) collective-permute-start(bf16[704,2048]{1,0:T(8,128)(2,1)} %pad_maximum_fusion.3), channel_id=1, source_target_pairs={{0,16},{16,0},{1,17},{17,1},{2,18},{18,2},{3,19},{19,3},{4,20},{20... | collective-permute-start | bytes 8650760 | tf_op jit(solution)/shard_map/over_x/ppermute | solution.py:49
  402.1 38.5 %collective-permute-start.8 = (bf16[2,512,2048]{2,1,0:T(8,128)(2,1)S(1)}, bf16[2,512,2048]{2,1,0:T(8,128)(2,1)S(1)}, u32[]{:S(2)}, u32[]{:S(2)}) collective-permute-start(bf16[2,512,2048]{2,1,0:T(8,128)(2,1)S(1)} %dynamic-slice_bitcast_fusion), channel_id=1, source_target_pairs={{0,4},{4,0},{8,12},{12,8},{1,5},{5,1},{9,13},{13,9},{2,6},{6,2},{1... | collective-permute-start | bytes 12582920 | tf_op jit(solution)/shard_map/over_core/ppermute | solution.py:49
  466.8 122.0 %reduce-scatter.9.cloned.1.call-start = ((), (), s32[]{:S(2)}) async-start(), calls=%async_computation.11 | async-start | bytes 5242880 | tf_op jit(solution)/shard_map/reduce_scatter | solution.py:704
  470.1 47.7 %collective-permute-start.11 = (bf16[1,512,2048]{2,1,0:T(8,128)(2,1)}, bf16[1,512,2048]{2,1,0:T(8,128)(2,1)}, u32[]{:S(2)}, u32[]{:S(2)}) collective-permute-start(bf16[1,512,2048]{2,1,0:T(8,128)(2,1)} %constant_dynamic-slice_fusion.24), channel_id=1, source_target_pairs={{0,8},{4,12},{8,0},{12,4},{1,9},{5,13},{9,1},{13,5},{2,10},{6,14},... | collective-permute-start | bytes 6291464 | tf_op jit(solution)/shard_map/over_y/ppermute | solution.py:49
  474.7 48.9 %collective-permute-start.10 = (bf16[1056,1024]{1,0:T(8,128)(2,1)}, bf16[1056,1024]{1,0:T(8,128)(2,1)}, u32[]{:S(2)}, u32[]{:S(2)}) collective-permute-start(bf16[1056,1024]{1,0:T(8,128)(2,1)} %constant_dynamic-slice_fusion.25), channel_id=1, source_target_pairs={{0,16},{16,0},{1,17},{17,1},{2,18},{18,2},{3,19},{19,3},{4,20},{20... | collective-permute-start | bytes 6488072 | tf_op jit(solution)/shard_map/over_x/ppermute | solution.py:49
  536.0 114.8 %reduce-scatter.11.cloned.1.call-start = ((), (), s32[]{:S(2)}) async-start(), calls=%async_computation.12 | async-start | bytes 2621440 | tf_op jit(solution)/shard_map/reduce_scatter | solution.py:708
  537.7 16.3 %collective-permute-start.12 = (bf16[128,2048]{1,0:T(8,128)(2,1)S(1)}, bf16[128,2048]{1,0:T(8,128)(2,1)S(1)}, u32[]{:S(2)}, u32[]{:S(2)}) collective-permute-start(bf16[128,2048]{1,0:T(8,128)(2,1)S(1)} %get-tuple-element.227), channel_id=1, source_target_pairs={{0,1},{1,2},{2,3},{3,0},{4,5},{5,6},{6,7},{7,4},{8,9},{9,10},{10,1... | collective-permute-start | bytes 1572872 | tf_op jit(solution)/shard_map/over_z/ppermute | solution.py:49
  539.3 37.6 %collective-permute-start.13 = (bf16[128,2048]{1,0:T(8,128)(2,1)S(1)}, bf16[128,2048]{1,0:T(8,128)(2,1)S(1)}, u32[]{:S(2)}, u32[]{:S(2)}) collective-permute-start(bf16[128,2048]{1,0:T(8,128)(2,1)S(1)} %get-tuple-element.229), channel_id=1, source_target_pairs={{0,2},{1,3},{2,0},{3,1},{4,6},{5,7},{6,4},{7,5},{8,10},{9,11},{10,... | collective-permute-start | bytes 1572872 | tf_op jit(solution)/shard_map/over_z/ppermute | solution.py:49
  540.7 36.2 %collective-permute-start.14 = (bf16[128,2048]{1,0:T(8,128)(2,1)S(1)}, bf16[128,2048]{1,0:T(8,128)(2,1)S(1)}, u32[]{:S(2)}, u32[]{:S(2)}) collective-permute-start(bf16[128,2048]{1,0:T(8,128)(2,1)S(1)} %get-tuple-element.228), channel_id=1, source_target_pairs={{0,3},{1,0},{2,1},{3,2},{4,7},{5,4},{6,5},{7,6},{8,11},{9,8},{10,9... | collective-permute-start | bytes 1572872 | tf_op jit(solution)/shard_map/over_z/ppermute | solution.py:49
  601.1 123.4 %all-gather.18.cloned.1.call-start = ((), (), s32[]{:S(2)}) async-start(), calls=%async_computation.13 | async-start | bytes 2621440 | tf_op jit(solution)/shard_map/all_gather | solution.py:727
  601.1 64.6 %collective-permute-start.23 = (bf16[704,2048]{1,0:T(8,128)(2,1)}, bf16[704,2048]{1,0:T(8,128)(2,1)}, u32[]{:S(2)}, u32[]{:S(2)}) collective-permute-start(bf16[704,2048]{1,0:T(8,128)(2,1)} %pad_maximum_fusion.4), channel_id=1, source_target_pairs={{0,16},{16,0},{1,17},{17,1},{2,18},{18,2},{3,19},{19,3},{4,20},{20... | collective-permute-start | bytes 8650760 | tf_op jit(solution)/shard_map/over_x/ppermute | solution.py:49
  609.0 15.9 %collective-permute-start.15 = (bf16[3,352,256]{2,1,0:T(8,128)(2,1)S(1)}, bf16[3,352,256]{2,1,0:T(8,128)(2,1)S(1)}, u32[]{:S(2)}, u32[]{:S(2)}) collective-permute-start(bf16[3,352,256]{2,1,0:T(8,128)(2,1)S(1)} %copy-done.38), channel_id=1, source_target_pairs={{0,4},{4,0},{8,12},{12,8},{1,5},{5,1},{9,13},{13,9},{2,6},{6,2},{1... | collective-permute-start | bytes 1622024 | tf_op jit(solution)/shard_map/over_core/ppermute | solution.py:49
  672.0 65.7 %collective-permute-start.26 = (bf16[704,2048]{1,0:T(8,128)(2,1)}, bf16[704,2048]{1,0:T(8,128)(2,1)}, u32[]{:S(2)}, u32[]{:S(2)}) collective-permute-start(bf16[704,2048]{1,0:T(8,128)(2,1)} %pad_maximum_fusion.5), channel_id=1, source_target_pairs={{0,16},{16,0},{1,17},{17,1},{2,18},{18,2},{3,19},{19,3},{4,20},{20... | collective-permute-start | bytes 8650760 | tf_op jit(solution)/shard_map/over_x/ppermute | solution.py:49
  673.6 104.6 %all-gather.20.cloned.1.call-start = ((), (), s32[]{:S(2)}) async-start(), calls=%async_computation.14 | async-start | bytes 2621440 | tf_op jit(solution)/shard_map/all_gather | solution.py:767
  680.9 18.5 %collective-permute-start.19 = (f32[28672]{0:T(1024)S(1)}, f32[28672]{0:T(1024)S(1)}, u32[]{:S(2)}, u32[]{:S(2)}) collective-permute-start(f32[28672]{0:T(1024)S(1)} %fusion.78), channel_id=1, source_target_pairs={{0,8},{4,12},{8,0},{12,4},{1,9},{5,13},{9,1},{13,5},{2,10},{6,14},... | collective-permute-start | bytes 344072 | tf_op jit(solution)/shard_map/ppermute | solution.py:114
  687.9 68.3 %collective-permute-start.25 = (bf16[512,2048]{1,0:T(8,128)(2,1)}, bf16[512,2048]{1,0:T(8,128)(2,1)}, u32[]{:S(2)}, u32[]{:S(2)}) collective-permute-start(bf16[512,2048]{1,0:T(8,128)(2,1)} %slice.248), channel_id=1, source_target_pairs={{0,8},{4,12},{8,0},{12,4},{1,9},{5,13},{9,1},{13,5},{2,10},{6,14},... | collective-permute-start | bytes 6291464 | tf_op jit(solution)/shard_map/over_y/ppermute | solution.py:49
  699.4 40.2 %collective-permute-start.20 = (f32[28672]{0:T(1024)S(1)}, f32[28672]{0:T(1024)S(1)}, u32[]{:S(2)}, u32[]{:S(2)}) collective-permute-start(f32[28672]{0:T(1024)S(1)} %add.410), channel_id=1, source_target_pairs={{0,16},{16,0},{1,17},{17,1},{2,18},{18,2},{3,19},{19,3},{4,20},{20... | collective-permute-start | bytes 344072 | tf_op jit(solution)/shard_map/ppermute | solution.py:114
  739.6 15.5 %collective-permute-start.21 = (f32[28672]{0:T(1024)S(1)}, f32[28672]{0:T(1024)S(1)}, u32[]{:S(2)}, u32[]{:S(2)}) collective-permute-start(f32[28672]{0:T(1024)S(1)} %add.411), channel_id=1, source_target_pairs={{0,1},{1,0},{2,3},{3,2},{4,5},{5,4},{6,7},{7,6},{8,9},{9,8},{10,11... | collective-permute-start | bytes 344072 | tf_op jit(solution)/shard_map/ppermute | solution.py:114
  755.1 16.9 %collective-permute-start.22 = (f32[28672]{0:T(1024)S(1)}, f32[28672]{0:T(1024)S(1)}, u32[]{:S(2)}, u32[]{:S(2)}) collective-permute-start(f32[28672]{0:T(1024)S(1)} %add.412), channel_id=1, source_target_pairs={{0,2},{1,3},{2,0},{3,1},{4,6},{5,7},{6,4},{7,5},{8,10},{9,11},{10,... | collective-permute-start | bytes 344072 | tf_op jit(solution)/shard_map/ppermute | solution.py:114
  758.5 24.4 %collective-permute-start.27 = (bf16[256,2048]{1,0:T(8,128)(2,1)S(1)}, bf16[256,2048]{1,0:T(8,128)(2,1)}, u32[]{:S(2)}, u32[]{:S(2)}) collective-permute-start(bf16[256,2048]{1,0:T(8,128)(2,1)S(1)} %slice.250), channel_id=1, source_target_pairs={{0,16},{16,0},{1,17},{17,1},{2,18},{18,2},{3,19},{19,3},{4,20},{20... | collective-permute-start | bytes 3145736 | tf_op jit(solution)/shard_map/over_x/ppermute | solution.py:49
  (72 other events, 722.2 us)
Sparse Core Ops, SparseCore 0:
  10.5 48.2 all-gather.7
  67.0 34.4 all-gather.9
  103.4 33.6 all-gather.11
  152.5 43.9 reduce-scatter.4
  214.4 74.8 all-gather.13
  358.9 102.8 reduce-scatter.6
  467.0 45.6 all-gather.15
  536.1 52.7 reduce-scatter.8
  601.2 49.5 reduce-scatter.10
  673.7 50.7 all-gather.17
  726.7 49.4 all-gather.19
